TPU v7x, 1024 devices: a whole 4x4x32 slice. The times are simulated.
1024 devices in a mesh: dp: 16 (over z_lo, core), expert: 64 (over z_hi, y, x).
Axes of the slice: x: 4, y: 4, z: 32 (z_hi: 4, z_lo: 8; z = z_hi * 8 + z_lo), core: 2. Of those that a mesh axis runs over, the one named last changes fastest.
Arguments:
- latent: bfloat16 [131072, 1024], P(('dp', 'expert')), may hold values from -6 to 6
- expert_ids: int32 [131072, 8], P(('dp', 'expert')), may hold values from 0 to 255, all different within a row
- gate_probs: float32 [131072, 8], P(('dp', 'expert')), may hold values from 0.05 to 1
- cotangent: bfloat16 [131072, 1024], P(('dp', 'expert')), may hold values from -6 to 6
- w_gate_up: bfloat16 [64, 1024, 1024], P('expert'), may hold values from -0.1875 to 0.1875
- w_down: bfloat16 [64, 1024, 512], P('expert'), may hold values from -0.25 to 0.25
Outputs:
- mixed: bfloat16 [131072, 1024], P(('dp', 'expert'))
- latent_gradient: bfloat16 [131072, 1024], P(('dp', 'expert'))
- gate_grad: float32 [131072, 8], P(('dp', 'expert'))
- gate_up_grad: bfloat16 [64, 1024, 1024], P('expert', 'dp')
- down_grad: bfloat16 [64, 1024, 512], P('expert', 'dp')
All inputs are finite; a program needn't handle non-finite values.
Results may differ from a plain program's by a relative error of at most 0.023.
Values may be sent and summed in bfloat16 or wider, within the bound.
No kernel may reach another device: no remote copies, remote signals or barrier semaphores. Data moves between devices by JAX's collectives and lax.ppermute only.
A program may use at most 32 MiB of HBM per device.

v0:
```python
import jax
import jax.numpy as jnp
from jax import lax
from jax.sharding import PartitionSpec as P

EXP_DEV = 4
CAP = 2


def expert_forward(incoming_rows, weight_in, output_weight):
    ffw_width = output_weight.shape[1]
    hidden = jnp.dot(incoming_rows, weight_in, preferred_element_type=jnp.float32)
    silu_product = (jax.nn.silu(hidden[:, :ffw_width]) * hidden[:, ffw_width:]).astype(jnp.bfloat16)
    outputs = lax.dot_general(
        silu_product, output_weight, (((1,), (1,)), ((), ())), preferred_element_type=jnp.float32
    ).astype(jnp.bfloat16)
    return (outputs, silu_product, hidden)


def expert_backward(slot_cotangent, hidden, weight_in, output_weight):
    ffw_width = output_weight.shape[1]
    gate_part = hidden[:, :ffw_width]
    up_part = hidden[:, ffw_width:]
    grad_act = jnp.dot(slot_cotangent, output_weight, preferred_element_type=jnp.float32)
    sigmoid_gate = jax.nn.sigmoid(gate_part)
    grad_gate = grad_act * up_part * sigmoid_gate * (1.0 + gate_part * (1.0 - sigmoid_gate))
    grad_up = grad_act * gate_part * sigmoid_gate
    hidden_gradient = jnp.concatenate([grad_gate, grad_up], axis=1).astype(jnp.bfloat16)
    grad_rows = lax.dot_general(
        hidden_gradient, weight_in, (((1,), (1,)), ((), ())), preferred_element_type=jnp.float32
    ).astype(jnp.bfloat16)
    return (grad_rows, hidden_gradient)


def local(latent, expert_ids, gate_probs, cotangent, w_gate_up, w_down):
    lat_width = latent.shape[1]
    columns = lax.axis_size("expert")
    slot_total = columns * CAP
    expert_total = columns * EXP_DEV
    weight_in = w_gate_up[0]
    output_weight = w_down[0]
    ffw_width = output_weight.shape[1]
    expert_axis = lax.broadcasted_iota(jnp.int32, (1, 1, expert_total), 2)
    one_hot = jnp.sum((expert_ids[:, :, None] == expert_axis).astype(jnp.int32), axis=1)
    earlier = jnp.cumsum(one_hot, axis=0) - one_hot
    position = jnp.take_along_axis(earlier, expert_ids, axis=1)
    kept_slots = (expert_ids % EXP_DEV == 0) & (position < CAP)
    target = jnp.where(kept_slots, expert_ids // EXP_DEV * CAP + position, -1)
    slot_numbers = lax.broadcasted_iota(jnp.int32, (slot_total, 1, 1), 0)
    chosen = target[None, :, :] == slot_numbers
    token_pick = jnp.any(chosen, axis=2).astype(jnp.bfloat16)
    gate_pick = jnp.sum(jnp.where(chosen, gate_probs[None, :, :], jnp.float32(0.0)), axis=2)
    sent_rows = jnp.dot(token_pick, latent, preferred_element_type=jnp.float32).astype(jnp.bfloat16)
    sent_cot = jnp.dot(
        gate_pick, cotangent.astype(jnp.float32), precision=lax.Precision.HIGHEST
    ).astype(jnp.bfloat16)
    sent_rows = sent_rows.reshape(columns, CAP, lat_width)
    sent_cot = sent_cot.reshape(columns, CAP, lat_width)
    received = lax.all_to_all(sent_rows, "expert", split_axis=0, concat_axis=0, tiled=True)
    sources, items, width = received.shape
    outputs, silu_product, hidden = expert_forward(
        received.reshape(-1, width), weight_in, output_weight
    )
    returned = lax.all_to_all(
        outputs.reshape(sources, items, width), "expert", split_axis=0, concat_axis=0, tiled=True
    )
    act_there = silu_product.reshape(sources, items, -1)
    hidden_there = hidden.reshape(sources, items, -1)
    cot_there = lax.all_to_all(sent_cot, "expert", split_axis=0, concat_axis=0, tiled=True)
    grad_rows, hidden_gradient = expert_backward(
        cot_there.reshape(-1, lat_width),
        hidden_there.reshape(slot_total, -1),
        weight_in,
        output_weight,
    )
    inputs_home = lax.all_to_all(
        grad_rows.reshape(columns, CAP, lat_width),
        "expert",
        split_axis=0,
        concat_axis=0,
        tiled=True,
    )
    rows_flat = received.reshape(slot_total, lat_width)
    cot_flat = cot_there.reshape(slot_total, lat_width)
    act_flat = act_there.reshape(slot_total, ffw_width)
    sliced = cot_flat
    down_sum = lax.psum_scatter(
        lax.dot_general(
            sliced, act_flat, (((0,), (0,)), ((), ())), preferred_element_type=jnp.float32
        ).astype(jnp.bfloat16),
        "dp",
        scatter_dimension=0,
        tiled=True,
    )
    sliced = rows_flat
    gate_up_sum = lax.psum_scatter(
        lax.dot_general(
            sliced, hidden_gradient, (((0,), (0,)), ((), ())), preferred_element_type=jnp.float32
        ).astype(jnp.bfloat16),
        "dp",
        scatter_dimension=0,
        tiled=True,
    )
    outputs_flat = returned.reshape(slot_total, lat_width)
    mixed = jnp.dot(
        gate_pick.T, outputs_flat.astype(jnp.float32), precision=lax.Precision.HIGHEST
    ).astype(jnp.bfloat16)
    latent_gradient = jnp.dot(
        token_pick.T, inputs_home.reshape(slot_total, lat_width), preferred_element_type=jnp.float32
    ).astype(jnp.bfloat16)
    inner = jnp.dot(cotangent, outputs_flat.T, preferred_element_type=jnp.float32)
    gate_grad = jnp.einsum(
        "rtk,tr->tk", chosen.astype(jnp.float32), inner, precision=lax.Precision.HIGHEST
    )
    gate_up_grad = gate_up_sum[None]
    down_grad = down_sum[None]
    return (mixed, latent_gradient, gate_grad, gate_up_grad, down_grad)


def solution(mesh):
    return jax.shard_map(
        local,
        mesh=mesh,
        in_specs=(
            P(("dp", "expert"), None),
            P(("dp", "expert"), None),
            P(("dp", "expert"), None),
            P(("dp", "expert"), None),
            P("expert", None, None),
            P("expert", None, None),
        ),
        out_specs=(
            P(("dp", "expert"), None),
            P(("dp", "expert"), None),
            P(("dp", "expert"), None),
            P("expert", "dp", None),
            P("expert", "dp", None),
        ),
        check_vma=False,
    )
```

profile of v0, /device:TPU:24, one launch (start us, length us, event | category | flops | bytes accessed | tf_op | source)
XLA Modules:
  0.0 385.5 jit_solution(5950720915793149189)
XLA Ops:
  7.2 0.9 copy.32
  9.6 8.6 %gather_fusion = s32[1024]{0:T(1024)S(1)} fusion(s32[128,256]{1,0:T(8,128)S(1)} %sub.12, s32[1024]{0:T(1024)S(1)} %reshape.57), kind=kCustom, calls=%fused_computation | custom fusion | bytes 16384 | tf_op jit(solution)/shard_map/jit(take_along_axis)/gather | solution.py:46
  19.6 34.2 %all-to-all-start = ((bf16[64,2,1024]{2,1,0:T(2,128)(2,1)}), bf16[64,2,1024]{2,1,0:T(2,128)(2,1)S(1)}, u32[]{:S(2)}, u32[]{:S(2)}) async-start(bf16[64,2,1024]{2,1,0:T(2,128)(2,1)} %reshape.49), calls=%async_computation | async-start | bytes 524288 | tf_op jit(solution)/shard_map/all_to_all | solution.py:59
  55.2 32.8 %all-to-all-done = bf16[64,2,1024]{2,1,0:T(2,128)(2,1)S(1)} async-done(((bf16[64,2,1024]{2,1,0:T(2,128)(2,1)}), bf16[64,2,1024]{2,1,0:T(2,128)(2,1)S(1)}, u32[]{:S(2)}, u32[]{:S(2)}) %all-to-all-start) | async-done | bytes 262176 | tf_op jit(solution)/shard_map/all_to_all | solution.py:59
  88.8 17.5 %all-to-all-start.2 = ((bf16[64,2,1024]{2,1,0:T(2,128)(2,1)}), bf16[64,2,1024]{2,1,0:T(2,128)(2,1)}, u32[]{:S(2)}, u32[]{:S(2)}) async-start(bf16[64,2,1024]{2,1,0:T(2,128)(2,1)} %reshape.53), calls=%async_computation.2 | async-start | bytes 524288 | tf_op jit(solution)/shard_map/all_to_all | solution.py:69
  106.3 1.1 reshape.50
  107.4 1.3 fusion.2
  108.7 30.6 %all-to-all-done.2 = bf16[64,2,1024]{2,1,0:T(2,128)(2,1)} async-done(((bf16[64,2,1024]{2,1,0:T(2,128)(2,1)}), bf16[64,2,1024]{2,1,0:T(2,128)(2,1)}, u32[]{:S(2)}, u32[]{:S(2)}) %all-to-all-start.2) | async-done | bytes 262176 | tf_op jit(solution)/shard_map/all_to_all | solution.py:69
  139.3 1.8 reshape.54
  141.1 2.2 multiply_convert_fusion.1
  144.0 1.4 convolution_convert_fusion.1
  147.1 10.3 %all-to-all-start.3 = ((bf16[64,2,1024]{2,1,0:T(2,128)(2,1)}), bf16[64,2,1024]{2,1,0:T(2,128)(2,1)}, u32[]{:S(2)}, u32[]{:S(2)}) async-start(bf16[64,2,1024]{2,1,0:T(2,128)(2,1)} %reshape.55), calls=%async_computation.3 | async-start | bytes 524288 | tf_op jit(solution)/shard_map/all_to_all | solution.py:76
  157.5 3.1 convolution_convert_fusion
  160.6 0.9 copy-done.10
  161.5 1.2 convolution_convert_fusion.5
  162.7 1.8 reshape.51
  164.5 28.8 %all-to-all-done.3 = bf16[64,2,1024]{2,1,0:T(2,128)(2,1)} async-done(((bf16[64,2,1024]{2,1,0:T(2,128)(2,1)}), bf16[64,2,1024]{2,1,0:T(2,128)(2,1)}, u32[]{:S(2)}, u32[]{:S(2)}) %all-to-all-start.3) | async-done | bytes 262176 | tf_op jit(solution)/shard_map/all_to_all | solution.py:76
  193.2 8.0 %all-to-all-start.1 = ((bf16[64,2,1024]{2,1,0:T(2,128)(2,1)}), bf16[64,2,1024]{2,1,0:T(2,128)(2,1)S(1)}, u32[]{:S(2)}, u32[]{:S(2)}) async-start(bf16[64,2,1024]{2,1,0:T(2,128)(2,1)} %reshape.51), calls=%async_computation.1 | async-start | bytes 524288 | tf_op jit(solution)/shard_map/all_to_all | solution.py:64
  201.3 1.0 reshape.56
  202.3 27.4 %all-to-all-done.1 = bf16[64,2,1024]{2,1,0:T(2,128)(2,1)S(1)} async-done(((bf16[64,2,1024]{2,1,0:T(2,128)(2,1)}), bf16[64,2,1024]{2,1,0:T(2,128)(2,1)S(1)}, u32[]{:S(2)}, u32[]{:S(2)}) %all-to-all-start.1) | async-done | bytes 262176 | tf_op jit(solution)/shard_map/all_to_all | solution.py:64
  230.8 1.0 convolution_convert_fusion.2
  231.8 1.1 convolution_convert_fusion.4
  232.9 20.3 %reduce-scatter.5.cloned.1.call-done = bf16[64,512]{1,0:T(8,128)(2,1)} async-done(((bf16[1024,512]{1,0:T(8,128)(2,1)}), bf16[64,512]{1,0:T(8,128)(2,1)}) %reduce-scatter.5.cloned.1.call-update) | async-done | bytes 65552 | tf_op jit(solution)/shard_map/reduce_scatter | solution.py:87
  253.2 125.4 %reduce-scatter.3.cloned.1.call-done = bf16[64,1024]{1,0:T(8,128)(2,1)} async-done(((bf16[1024,1024]{1,0:T(8,128)(2,1)}), bf16[64,1024]{1,0:T(8,128)(2,1)}) %reduce-scatter.3.cloned.1.call-update) | async-done | bytes 131088 | tf_op jit(solution)/shard_map/reduce_scatter | solution.py:96
  (51 shorter events, 8.4 us)
Async XLA Ops:
  7.2 100.3 %copy-start = (bf16[1,1024,1024]{2,1,0:T(8,128)(2,1)S(1)}, bf16[1,1024,1024]{2,1,0:T(8,128)(2,1)}, u32[]{:S(2)}) copy-start(bf16[1,1024,1024]{2,1,0:T(8,128)(2,1)} %param.10) | copy-start | bytes 6291460
  9.6 8.8 %copy-start.12 = (s32[128,8]{0,1:T(8,128)S(1)}, s32[128,8]{0,1:T(8,128)}, u32[]{:S(2)}) copy-start(s32[128,8]{0,1:T(8,128)} %param.7) | copy-start | bytes 12292
  9.6 9.0 %copy-start.11 = (bf16[128,1024]{1,0:T(8,128)(2,1)S(1)}, bf16[128,1024]{1,0:T(8,128)(2,1)}, u32[]{:S(2)}) copy-start(bf16[128,1024]{1,0:T(8,128)(2,1)} %param.6) | copy-start | bytes 786436
  9.6 44.2 %copy-start.13 = (f32[128,8]{0,1:T(8,128)S(1)}, f32[128,8]{0,1:T(8,128)}, u32[]{:S(2)}) copy-start(f32[128,8]{0,1:T(8,128)} %param.8) | copy-start | bytes 12292
  9.6 44.4 %copy-start.3 = (bf16[128,1024]{1,0:T(8,128)(2,1)S(1)}, bf16[128,1024]{1,0:T(8,128)(2,1)}, u32[]{:S(2)}) copy-start(bf16[128,1024]{1,0:T(8,128)(2,1)} %param.9) | copy-start | bytes 786436
  19.6 68.4 %all-to-all-start = ((bf16[64,2,1024]{2,1,0:T(2,128)(2,1)}), bf16[64,2,1024]{2,1,0:T(2,128)(2,1)S(1)}, u32[]{:S(2)}, u32[]{:S(2)}) async-start(bf16[64,2,1024]{2,1,0:T(2,128)(2,1)} %reshape.49), calls=%async_computation | async-start | bytes 524288 | tf_op jit(solution)/shard_map/all_to_all | solution.py:59
  88.1 0.7 copy-start.5
  88.8 50.6 %all-to-all-start.2 = ((bf16[64,2,1024]{2,1,0:T(2,128)(2,1)}), bf16[64,2,1024]{2,1,0:T(2,128)(2,1)}, u32[]{:S(2)}, u32[]{:S(2)}) async-start(bf16[64,2,1024]{2,1,0:T(2,128)(2,1)} %reshape.53), calls=%async_computation.2 | async-start | bytes 524288 | tf_op jit(solution)/shard_map/all_to_all | solution.py:69
  106.2 34.9 %copy-start.1 = (bf16[1,1024,512]{2,1,0:T(8,128)(2,1)S(1)}, bf16[1,1024,512]{2,1,0:T(8,128)(2,1)}, u32[]{:S(2)}) copy-start(bf16[1,1024,512]{2,1,0:T(8,128)(2,1)} %param.11) | copy-start | bytes 3145732
  106.3 147.0 %reduce-scatter.5.cloned.1.call-start = ((), (), s32[]{:S(2)}) async-start(), calls=%async_computation.7 | async-start | bytes 1114112 | tf_op jit(solution)/shard_map/reduce_scatter | solution.py:87
  141.1 2.9 copy-start.6
  143.3 0.6 copy-start.9
  143.3 2.1 copy-start.7
  143.3 2.1 copy-start.8
  147.1 46.2 %all-to-all-start.3 = ((bf16[64,2,1024]{2,1,0:T(2,128)(2,1)}), bf16[64,2,1024]{2,1,0:T(2,128)(2,1)}, u32[]{:S(2)}, u32[]{:S(2)}) async-start(bf16[64,2,1024]{2,1,0:T(2,128)(2,1)} %reshape.55), calls=%async_computation.3 | async-start | bytes 524288 | tf_op jit(solution)/shard_map/all_to_all | solution.py:76
  157.4 3.2 copy-start.2
  157.4 221.2 %reduce-scatter.3.cloned.1.call-start = ((), (), s32[]{:S(2)}) async-start(), calls=%async_computation.6 | async-start | bytes 2228224 | tf_op jit(solution)/shard_map/reduce_scatter | solution.py:96
  160.6 0.9 copy-start.10
  162.7 67.2 %copy-start.4 = (bf16[128,1024]{1,0:T(8,128)(2,1)S(1)}, bf16[128,1024]{1,0:T(8,128)(2,1)}, u32[]{:S(2)}) copy-start(bf16[128,1024]{1,0:T(8,128)(2,1)} %param.9) | copy-start | bytes 786436
  193.2 36.5 %all-to-all-start.1 = ((bf16[64,2,1024]{2,1,0:T(2,128)(2,1)}), bf16[64,2,1024]{2,1,0:T(2,128)(2,1)S(1)}, u32[]{:S(2)}, u32[]{:S(2)}) async-start(bf16[64,2,1024]{2,1,0:T(2,128)(2,1)} %reshape.51), calls=%async_computation.1 | async-start | bytes 524288 | tf_op jit(solution)/shard_map/all_to_all | solution.py:64
Sparse Core Ops, SparseCore 0:
  145.5 107.6 reduce-scatter.4
  257.6 121.0 reduce-scatter.2
where the time goes:
time: 387 us; the launch traced here: 385 us
  waiting for transfers between devices  265 us (68%)
  starting transfers between devices  70.1 us (18%)
  local copies, waits for them, and re-layouts  20.4 us (5%)
  between operations  14.3 us (4%)
  matrix products  12.9 us (3%)
    reduce_scatter x1, waiting for transfers between devices, local(): lax.psum_scatter(lax.dot_general(sliced, hidden_gradient, (((0,), (0,)),...  125 us
    all_to_all x1, starting transfers between devices, local(): lax.all_to_all(sent_rows, 'expert', split_axis=0, concat_axis=0, tiled=True)  34.2 us
    all_to_all x1, waiting for transfers between devices, local(): lax.all_to_all(sent_rows, 'expert', split_axis=0, concat_axis=0, tiled=True)  32.8 us
    all_to_all x1, waiting for transfers between devices, local(): lax.all_to_all(sent_cot, 'expert', split_axis=0, concat_axis=0, tiled=True)  30.6 us
    all_to_all x1, waiting for transfers between devices, local(): lax.all_to_all(grad_rows.reshape(columns, CAP, lat_width), 'expert', spli...  28.8 us
    all_to_all x1, waiting for transfers between devices, local(): lax.all_to_all(outputs.reshape(sources, items, width), 'expert', split_ax...  27.4 us
    reduce_scatter x1, waiting for transfers between devices, local(): lax.psum_scatter(lax.dot_general(sliced, act_flat, (((0,), (0,)), ((), ()...  20.3 us
    all_to_all x1, starting transfers between devices, local(): lax.all_to_all(sent_cot, 'expert', split_axis=0, concat_axis=0, tiled=True)  17.5 us
  transfers between devices with their start and end apart: 6, of which 6 were waited for; matrix products, arithmetic and copies ran while one was open for 4% of the time, Pallas kernels for 0%

commit v1 on v0

v1 whole, which is shorter than its diff:
```python
import jax
import jax.numpy as jnp
from jax import lax
from jax.sharding import PartitionSpec as P

EXP_DEV = 4
CAP = 2
F32 = jnp.float32
BF16 = jnp.bfloat16


def mm(a, b, ca, cb):
    return lax.dot_general(a, b, (((ca,), (cb,)), ((), ())), preferred_element_type=F32)


def halves(value):
    high = value.astype(BF16)
    return high, (value - high.astype(F32)).astype(BF16)


def route(expert_ids, gate_probs, columns):
    tokens = expert_ids.shape[0]
    rows = columns * 2 * CAP
    ids = expert_ids.T
    probs = gate_probs.T
    row = lax.broadcasted_iota(jnp.int32, (rows, tokens), 0)
    expert = row // (2 * CAP) * EXP_DEV
    named = jnp.zeros((rows, tokens), F32)
    gate = jnp.zeros((rows, tokens), F32)
    for slot in range(ids.shape[0]):
        hit = ids[slot][None, :] == expert
        named = named + jnp.where(hit, 1.0, 0.0)
        gate = gate + jnp.where(hit, probs[slot][None, :], 0.0)
    before = lax.broadcasted_iota(jnp.int32, (tokens, tokens), 0)
    after = lax.broadcasted_iota(jnp.int32, (tokens, tokens), 1)
    earlier = mm(named.astype(BF16), (before < after).astype(BF16), 1, 0)
    place = (row % CAP).astype(F32)
    pick = (named > 0.5) & (earlier == place)
    return pick, jnp.where(pick, gate, 0.0), row % (2 * CAP) < CAP


def local(latent, expert_ids, gate_probs, cotangent, w_gate_up, w_down):
    tokens, lat = latent.shape
    top = expert_ids.shape[1]
    columns = lax.axis_size("expert")
    replicas = lax.axis_size("dp")
    weight_in = w_gate_up[0]
    weight_out = w_down[0]
    ffw = weight_out.shape[1]
    slots = columns * CAP

    pick, gate, first = route(expert_ids, gate_probs, columns)
    token_part = jnp.where(pick & first, 1.0, 0.0).astype(BF16)
    gate_part = jnp.where(first, 0.0, gate)
    gate_high, gate_low = halves(gate_part)
    sent = mm(
        jnp.concatenate([token_part, gate_high, gate_low], axis=1),
        jnp.concatenate([latent, cotangent, cotangent], axis=0), 1, 0,
    ).astype(BF16)
    there = lax.all_to_all(
        sent.reshape(columns, 2 * CAP, lat), "expert", split_axis=0, concat_axis=0, tiled=True
    )
    rows = there[:, :CAP].reshape(slots, lat)
    cot = there[:, CAP:].reshape(slots, lat)

    hidden = mm(rows, weight_in, 1, 0)
    g = hidden[:, :ffw]
    u = hidden[:, ffw:]
    s = jax.nn.sigmoid(g)
    act = (g * s * u).astype(BF16)
    out = mm(act, weight_out, 1, 1).astype(BF16)
    grad_act = mm(cot, weight_out, 1, 0)
    grad_hidden = jnp.concatenate(
        [grad_act * u * s * (1.0 + g * (1.0 - s)), grad_act * g * s], axis=1
    ).astype(BF16)
    grad_rows = mm(grad_hidden, weight_in, 1, 1).astype(BF16)
    back = lax.all_to_all(
        jnp.concatenate(
            [out.reshape(columns, CAP, lat), grad_rows.reshape(columns, CAP, lat)], axis=1
        ),
        "expert", split_axis=0, concat_axis=0, tiled=True,
    )

    terms = jnp.concatenate([mm(rows, grad_hidden, 0, 0), mm(cot, act, 0, 0)], axis=1)
    width = 3 * ffw
    share = lat // replicas
    terms = terms.astype(BF16).reshape(replicas // 2, 2, share, width)
    core = lax.axis_index("dp") % 2
    mine = jnp.where(core == 0, terms[:, 0], terms[:, 1])
    other = jnp.where(core == 0, terms[:, 1], terms[:, 0])
    swapped = lax.ppermute(other, "dp", [(i, i ^ 1) for i in range(replicas)])
    pair = (mine.astype(F32) + swapped.astype(F32)).astype(BF16).reshape(lat // 2, width)
    summed = lax.psum_scatter(
        pair, "dp", scatter_dimension=0, tiled=True,
        axis_index_groups=[list(range(c, replicas, 2)) for c in range(2)],
    )

    home = back.reshape(2 * slots, lat)
    out_high, out_low = halves(jnp.where(pick & first, gate, 0.0))
    mixed = (mm(out_high, home, 0, 0) + mm(out_low, home, 0, 0)).astype(BF16)
    latent_gradient = mm(jnp.where(pick & ~first, 1.0, 0.0).astype(BF16), home, 0, 0).astype(BF16)
    inner = mm(home, cotangent, 1, 1)
    inner = jnp.where(pick & first, inner, 0.0)
    row = lax.broadcasted_iota(jnp.int32, inner.shape, 0)
    expert = row // (2 * CAP) * EXP_DEV
    ids = expert_ids.T
    gate_grad = jnp.stack(
        [jnp.sum(jnp.where(ids[k][None, :] == expert, inner, 0.0), axis=0) for k in range(top)], axis=1
    )
    return (mixed, latent_gradient, gate_grad, summed[None, :, : 2 * ffw], summed[None, :, 2 * ffw :])


def solution(mesh):
    return jax.shard_map(
        local,
        mesh=mesh,
        in_specs=(
            P(("dp", "expert"), None),
            P(("dp", "expert"), None),
            P(("dp", "expert"), None),
            P(("dp", "expert"), None),
            P("expert", None, None),
            P("expert", None, None),
        ),
        out_specs=(
            P(("dp", "expert"), None),
            P(("dp", "expert"), None),
            P(("dp", "expert"), None),
            P("expert", "dp", None),
            P("expert", "dp", None),
        ),
        check_vma=False,
    )
```

time: 387 us -> 244 us (0.63)
  waiting for transfers between devices: 265 us -> 140 us
  starting transfers between devices: 70.1 us -> 57.2 us
  local copies, waits for them, and re-layouts: 20.4 us -> 11.9 us
  other arithmetic: 2.38 us -> 8.49 us
    reduce_scatter x2 -> x1, waiting for transfers between devices: 146 us -> 31.8 us  [local(): lax.psum_scatter(pair, 'dp', scatter_dimension=0, tiled=True, axis_index_...]
    all_to_all x4 -> x2, starting transfers between devices: 70 us -> 55.2 us  [the longest x1 34.2 us: local(): lax.all_to_all(sent.reshape(columns, 2 * CAP, lat), 'expert', split_axis=...]
    all_to_all x4 -> x2, waiting for transfers between devices: 120 us -> 108 us  [the longest x1 55.3 us: local(): lax.all_to_all(jnp.concatenate([out.reshape(columns, CAP, lat), grad_rows...]
    gather x5 -> x0, local copies, waits for them, and re-layouts: 8.91 us -> none  [local(): position = jnp.take_along_axis(earlier, expert_ids, axis=1)]
    convert_element_type x0 -> x3, other arithmetic: none -> 4.38 us  [the longest x1 3.93 us: local(): (mine.astype(F32) + swapped.astype(F32)).astype(BF16)]
    broadcast_in_dim x0 -> x3, local copies, waits for them, and re-layouts: none -> 4.02 us  [the longest x1 1.57 us: local(): summed[None, :, :2 * ffw]]
    dot_general x11 -> x12, matrix products: 12.9 us -> 9.74 us  [mm(): lax.dot_general(a, b, (((ca,), (cb,)), ((), ())), preferred_element_type=...]
  transfers between devices with their start and end apart: 6 -> 4, of which waited for: 6 -> 3; matrix products, arithmetic and copies ran while one was open for 4% -> 6% of each run, Pallas kernels for 0% -> 0%
where the time goes in v1:
time: 244 us; the launch traced here: 242 us
  waiting for transfers between devices  140 us (57%)
  starting transfers between devices  57.2 us (23%)
  between operations  14.3 us (6%)
  local copies, waits for them, and re-layouts  11.9 us (5%)
  matrix products  9.74 us (4%)
  other arithmetic  8.49 us (3%)
    all_to_all x1, waiting for transfers between devices, local(): lax.all_to_all(jnp.concatenate([out.reshape(columns, CAP, lat), grad_rows...  55.3 us
    all_to_all x1, waiting for transfers between devices, local(): lax.all_to_all(sent.reshape(columns, 2 * CAP, lat), 'expert', split_axis=...  53.1 us
    all_to_all x1, starting transfers between devices, local(): lax.all_to_all(sent.reshape(columns, 2 * CAP, lat), 'expert', split_axis=...  34.2 us
    reduce_scatter x1, waiting for transfers between devices, local(): lax.psum_scatter(pair, 'dp', scatter_dimension=0, tiled=True, axis_index_...  31.8 us
    all_to_all x1, starting transfers between devices, local(): lax.all_to_all(jnp.concatenate([out.reshape(columns, CAP, lat), grad_rows...  21 us
    dot_general x12, matrix products, mm(): lax.dot_general(a, b, (((ca,), (cb,)), ((), ())), preferred_element_type=...  9.74 us
  transfers between devices with their start and end apart: 4, of which 3 were waited for; matrix products, arithmetic and copies ran while one was open for 6% of the time, Pallas kernels for 0%

profile of v1, /device:TPU:24, one launch (start us, length us, event | category | flops | bytes accessed | tf_op | source)
XLA Modules:
  0.0 241.8 jit_solution(4025676264389566716)
XLA Ops:
  7.3 1.0 slice_bitcast_fusion.17
  8.2 1.0 slice_bitcast_fusion.9
  9.2 0.8 subtract_convert_fusion.1
  11.0 1.0 reshape.42
  11.9 34.2 %all-to-all-start = ((bf16[64,4,1024]{2,1,0:T(4,128)(2,1)}), bf16[64,4,1024]{2,1,0:T(4,128)(2,1)S(1)}, u32[]{:S(2)}, u32[]{:S(2)}) async-start(bf16[64,4,1024]{2,1,0:T(4,128)(2,1)} %reshape.42), calls=%async_computation | async-start | bytes 1048576 | tf_op jit(solution)/shard_map/all_to_all | solution.py:60
  46.2 53.1 %all-to-all-done = bf16[64,4,1024]{2,1,0:T(4,128)(2,1)S(1)} async-done(((bf16[64,4,1024]{2,1,0:T(4,128)(2,1)}), bf16[64,4,1024]{2,1,0:T(4,128)(2,1)S(1)}, u32[]{:S(2)}, u32[]{:S(2)}) %all-to-all-start) | async-done | bytes 524320 | tf_op jit(solution)/shard_map/all_to_all | solution.py:60
  100.5 0.8 copy.12
  101.3 1.6 multiply_convert_fusion.1
  102.9 0.8 fusion.8
  104.9 1.7 fusion.5
  106.6 1.9 collective-permute-start
  108.5 1.2 convolution_convert_fusion.4
  109.7 1.7 reshape.44
  111.4 0.8 reshape.46
  112.2 2.4 pad_maximum_fusion.1
  114.6 21.0 %all-to-all-start.1 = ((bf16[64,4,1024]{2,1,0:T(4,128)(2,1)}), bf16[64,4,1024]{2,1,0:T(4,128)(2,1)}, u32[]{:S(2)}, u32[]{:S(2)}) async-start(bf16[64,4,1024]{2,1,0:T(4,128)(2,1)} %pad_maximum_fusion.1), calls=%async_computation.1 | async-start | bytes 1048576 | tf_op jit(solution)/shard_map/all_to_all | solution.py:77
  135.7 3.9 %fusion = bf16[8,64,1536]{2,1,0:T(8,128)(2,1)} fusion(bf16[8,64,1536]{2,1,0:T(8,128)(2,1)} %collective-permute-done, pred[]{:T(512)S(6)} %eq.149, bf16[8,2,64,512]{3,2,1,0:T(8,128)(2,1)S(1)} %convolution_convert_fusion.1, bf16[8,2,64,1024]{3,2,1,0:T(8,128)(2,1)} %copy-done.1), kind=kLoop, calls=%fused_computation.3 | loop fusion | flops 10223616 | bytes 6291457 | tf_op jit(solution)/shard_map/convert_element_type | solution.py:92
  139.7 55.3 %all-to-all-done.1 = bf16[64,4,1024]{2,1,0:T(4,128)(2,1)} async-done(((bf16[64,4,1024]{2,1,0:T(4,128)(2,1)}), bf16[64,4,1024]{2,1,0:T(4,128)(2,1)}, u32[]{:S(2)}, u32[]{:S(2)}) %all-to-all-start.1) | async-done | bytes 524320 | tf_op jit(solution)/shard_map/all_to_all | solution.py:77
  195.0 1.2 reshape.47
  197.2 1.1 convolution_convert_fusion.3
  198.9 1.3 fusion.11
  200.1 31.8 %reduce-scatter.2.cloned.1.call-done = bf16[64,1536]{1,0:T(8,128)(2,1)} async-done(((bf16[512,1536]{1,0:T(8,128)(2,1)}), bf16[64,1536]{1,0:T(8,128)(2,1)}) %reduce-scatter.2.cloned.1.call-update) | async-done | bytes 196624 | tf_op jit(solution)/shard_map/reduce_scatter | solution.py:93
  231.9 1.6 slice_bitcast_fusion
  233.5 1.5 slice_bitcast_fusion.1
  (35 shorter events, 4.9 us)
Async XLA Ops:
  7.2 92.7 %copy-start = (bf16[1,1024,1024]{2,1,0:T(8,128)(2,1)S(1)}, bf16[1,1024,1024]{2,1,0:T(8,128)(2,1)}, u32[]{:S(2)}) copy-start(bf16[1,1024,1024]{2,1,0:T(8,128)(2,1)} %param.10) | copy-start | bytes 6291460
  7.2 3.3 %copy-start.4 = (bf16[128,1024]{1,0:T(8,128)(2,1)S(1)}, bf16[128,1024]{1,0:T(8,128)(2,1)}, u32[]{:S(2)}) copy-start(bf16[128,1024]{1,0:T(8,128)(2,1)} %param.6) | copy-start | bytes 786436
  7.2 3.3 %copy-start.5 = (bf16[128,1024]{1,0:T(8,128)(2,1)S(1)}, bf16[128,1024]{1,0:T(8,128)(2,1)}, u32[]{:S(2)}) copy-start(bf16[128,1024]{1,0:T(8,128)(2,1)} %param.9) | copy-start | bytes 786436
  11.9 87.3 %all-to-all-start = ((bf16[64,4,1024]{2,1,0:T(4,128)(2,1)}), bf16[64,4,1024]{2,1,0:T(4,128)(2,1)S(1)}, u32[]{:S(2)}, u32[]{:S(2)}) async-start(bf16[64,4,1024]{2,1,0:T(4,128)(2,1)} %reshape.42), calls=%async_computation | async-start | bytes 1048576 | tf_op jit(solution)/shard_map/all_to_all | solution.py:60
  102.9 1.5 copy-start.3
  104.4 2.2 copy-start.1
  104.9 3.6 %copy-start.2 = (bf16[1,1024,512]{2,1,0:T(8,128)(2,1)S(1)}, bf16[1,1024,512]{2,1,0:T(8,128)(2,1)}, u32[]{:S(2)}) copy-start(bf16[1,1024,512]{2,1,0:T(8,128)(2,1)} %param.11) | copy-start | bytes 3145732
  106.6 29.1 %collective-permute-start = (bf16[8,64,1536]{2,1,0:T(8,128)(2,1)}, bf16[8,64,1536]{2,1,0:T(8,128)(2,1)}, u32[]{:S(2)}, u32[]{:S(2)}) collective-permute-start(bf16[8,64,1536]{2,1,0:T(8,128)(2,1)} %fusion.5), channel_id=1, source_target_pairs={{0,64},{64,0},{128,192},{192,128},{256,320},{320,256},{384,448},{4... | collective-permute-start | bytes 4718600 | tf_op jit(solution)/shard_map/ppermute | solution.py:91
  114.6 80.3 %all-to-all-start.1 = ((bf16[64,4,1024]{2,1,0:T(4,128)(2,1)}), bf16[64,4,1024]{2,1,0:T(4,128)(2,1)}, u32[]{:S(2)}, u32[]{:S(2)}) async-start(bf16[64,4,1024]{2,1,0:T(4,128)(2,1)} %pad_maximum_fusion.1), calls=%async_computation.1 | async-start | bytes 1048576 | tf_op jit(solution)/shard_map/all_to_all | solution.py:77
  135.7 96.3 %reduce-scatter.2.cloned.1.call-start = ((), (), s32[]{:S(2)}) async-start(), calls=%async_computation.3 | async-start | bytes 1769472 | tf_op jit(solution)/shard_map/reduce_scatter | solution.py:93
  139.6 56.5 %copy-start.6 = (bf16[128,1024]{1,0:T(8,128)(2,1)S(1)}, bf16[128,1024]{1,0:T(8,128)(2,1)}, u32[]{:S(2)}) copy-start(bf16[128,1024]{1,0:T(8,128)(2,1)} %param.9) | copy-start | bytes 786436
Sparse Core Ops, SparseCore 0:
  139.9 91.9 reduce-scatter.1

commit v2 on v1

v2 whole, which is shorter than its diff:
```python
import jax
import jax.numpy as jnp
from jax import lax
from jax.experimental import pallas as pl
from jax.experimental.pallas import tpu as pltpu
from jax.sharding import PartitionSpec as P

EXP_DEV = 4
CAP = 2
GROUP = 4 * CAP
F32 = jnp.float32
BF16 = jnp.bfloat16
VMEM_BYTES = 48 << 20


def mm(a, b, ca=1, cb=0):
    return lax.dot_general(a, b, (((ca,), (cb,)), ((), ())), preferred_element_type=F32)


def iota(shape, dim):
    return lax.broadcasted_iota(jnp.int32, shape, dim)


def halves(value):
    high = value.astype(BF16)
    return high, (value - high.astype(F32)).astype(BF16)


def routing(ids_ref, probs_ref, rows):
    tokens = ids_ref.shape[1]
    row = iota((rows, tokens), 0)
    expert = (row // GROUP) * EXP_DEV
    named = jnp.zeros((rows, tokens), F32)
    gate = jnp.zeros((rows, tokens), F32)
    for slot in range(ids_ref.shape[0]):
        hit = ids_ref[slot : slot + 1, :] == expert
        named = jnp.where(hit, 1.0, named)
        gate = jnp.where(hit, probs_ref[slot : slot + 1, :], gate)
    before = iota((tokens, tokens), 0)
    after = iota((tokens, tokens), 1)
    earlier = mm(named.astype(BF16), jnp.where(before < after, 1.0, 0.0).astype(BF16))
    pick = (named > 0.5) & (earlier == (row & 1).astype(F32))
    kind = (row & 2) == 0
    half = (row & 4) == 0
    return pick, gate, kind, half, expert


def zero_one(mask):
    return jnp.where(mask, 1.0, 0.0).astype(BF16)


def pack_kernel(ids_ref, probs_ref, latent_ref, cot_ref, sent_ref):
    rows, wide = sent_ref.shape
    pick, gate, first, low, _ = routing(ids_ref, probs_ref, rows)
    token = jnp.where(pick & first, 1.0, 0.0)
    weight = jnp.where(pick & ~first, gate, 0.0)
    total = jnp.zeros((rows, wide), F32)
    for h in range(2):
        here = low if h == 0 else ~low
        high, rest = halves(jnp.where(here, weight, 0.0))
        picks = jnp.concatenate([jnp.where(here, token, 0.0).astype(BF16), high, rest], axis=1)
        cols = pl.ds(h * wide, wide)
        cot = cot_ref[:, cols]
        total = total + mm(picks, jnp.concatenate([latent_ref[:, cols], cot, cot], axis=0))
    sent_ref[...] = total.astype(BF16)


def sorted_position(index, slots):
    group = index // GROUP
    return ((index & 2) + ((index >> 2) & 1)) * slots + group * CAP + (index & 1)


def expert_kernel(core_ref, there_ref, win_ref, wout_ref, back_ref, mine_ref, other_ref, terms_ref):
    rows, wide = there_ref.shape
    slots = rows // 4
    ffw = wout_ref.shape[1]
    share = mine_ref.shape[1]
    sort = zero_one(iota((rows, rows), 0) == sorted_position(iota((rows, rows), 1), slots))
    data = mm(sort, there_ref[...]).astype(BF16)
    vec = [data[:slots], data[slots : 2 * slots]]
    cot = [data[2 * slots : 3 * slots], data[3 * slots :]]
    top = [pl.ds(0, wide), pl.ds(wide, wide)]

    hidden = mm(vec[0], win_ref[top[0], :]) + mm(vec[1], win_ref[top[1], :])
    g = hidden[:, :ffw]
    u = hidden[:, ffw:]
    s = 1.0 / (1.0 + jnp.exp(-g))
    act = (g * s * u).astype(BF16)
    grad_act = mm(cot[0], wout_ref[top[0], :]) + mm(cot[1], wout_ref[top[1], :])
    grad_hidden = jnp.concatenate(
        [grad_act * u * s * (1.0 + g * (1.0 - s)), grad_act * g * s], axis=1
    ).astype(BF16)

    for h in range(2):
        terms_ref[top[h], : 2 * ffw] = mm(vec[h], grad_hidden, 0, 0).astype(BF16)
        terms_ref[top[h], 2 * ffw :] = mm(cot[h], act, 0, 0).astype(BF16)
    even = core_ref[0] == 0
    for block in range(mine_ref.shape[0]):
        a = terms_ref[pl.ds(2 * block * share, share), :]
        b = terms_ref[pl.ds((2 * block + 1) * share, share), :]
        mine_ref[block] = jnp.where(even, a, b)
        other_ref[block] = jnp.where(even, b, a)

    result = jnp.concatenate(
        [mm(act, wout_ref[top[h], :], 1, 1).astype(BF16) for h in range(2)]
        + [mm(grad_hidden, win_ref[top[h], :], 1, 1).astype(BF16) for h in range(2)],
        axis=0,
    )
    unsort = zero_one(iota((rows, rows), 1) == sorted_position(iota((rows, rows), 0), slots))
    back_ref[...] = mm(unsort, result).astype(BF16)


def add_kernel(a_ref, b_ref, out_ref):
    out_ref[...] = (a_ref[...].astype(F32) + b_ref[...].astype(F32)).astype(BF16)


def combine_kernel(ids_ref, probs_ref, cot_ref, home_ref, mixed_ref, latgrad_ref, gate_ref):
    rows, wide = home_ref.shape
    pick, gate, first, low, expert = routing(ids_ref, probs_ref, rows)
    home = home_ref[...]
    chosen = pick & first
    weight = jnp.where(chosen, gate, 0.0)
    token = jnp.where(pick & ~first, 1.0, 0.0)
    inner = jnp.zeros(weight.shape, F32)
    for h in range(2):
        here = low if h == 0 else ~low
        cols = pl.ds(h * wide, wide)
        high, rest = halves(jnp.where(here, weight, 0.0))
        mixed_ref[:, cols] = (mm(high, home, 0, 0) + mm(rest, home, 0, 0)).astype(BF16)
        latgrad_ref[:, cols] = mm(jnp.where(here, token, 0.0).astype(BF16), home, 0, 0).astype(BF16)
        inner = jnp.where(here & chosen, mm(home, cot_ref[:, cols], 1, 1), inner)
    for slot in range(ids_ref.shape[0]):
        hit = ids_ref[slot : slot + 1, :] == expert
        gate_ref[slot : slot + 1, :] = jnp.sum(jnp.where(hit, inner, 0.0), axis=0, keepdims=True)


def call(kernel, outs, scratch=(), specs=None):
    shapes = [jax.ShapeDtypeStruct(shape, dtype) for shape, dtype in outs]
    return pl.pallas_call(
        kernel,
        out_shape=shapes,
        in_specs=specs,
        out_specs=[pl.BlockSpec(memory_space=pltpu.VMEM)] * len(shapes),
        scratch_shapes=list(scratch),
        compiler_params=pltpu.CompilerParams(vmem_limit_bytes=VMEM_BYTES),
        name=kernel.__name__,
    )


def local(latent, expert_ids, gate_probs, cotangent, w_gate_up, w_down):
    tokens, lat = latent.shape
    top = expert_ids.shape[1]
    columns = lax.axis_size("expert")
    replicas = lax.axis_size("dp")
    ffw = w_down.shape[2]
    rows = columns * GROUP
    wide = lat // 2
    width = 3 * ffw
    share = lat // replicas
    ids = expert_ids.T
    probs = gate_probs.T
    vmem = pl.BlockSpec(memory_space=pltpu.VMEM)

    (sent,) = call(pack_kernel, [((rows, wide), BF16)], specs=[vmem] * 4)(ids, probs, latent, cotangent)
    there = exchange(sent, columns)

    core = (lax.axis_index("dp") % 2).astype(jnp.int32).reshape(1)
    half_terms = ((replicas // 2, share, width), BF16)
    back, mine, other = call(
        expert_kernel,
        [((rows, wide), BF16), half_terms, half_terms],
        scratch=[pltpu.VMEM((lat, width), BF16)],
        specs=[pl.BlockSpec(memory_space=pltpu.SMEM)] + [vmem] * 3,
    )(core, there, w_gate_up[0], w_down[0])

    swapped = lax.ppermute(other, "dp", [(i, i ^ 1) for i in range(replicas)])
    (pair,) = call(add_kernel, [half_terms], specs=[vmem] * 2)(mine, swapped)
    pair, back = lax.optimization_barrier((pair, back))
    summed = lax.psum_scatter(
        pair.reshape(lat // 2, width), "dp", scatter_dimension=0, tiled=True,
        axis_index_groups=[list(range(c, replicas, 2)) for c in range(2)],
    )
    home = exchange(back, columns)
    mixed, latent_gradient, gate_grad = call(
        combine_kernel,
        [((tokens, lat), BF16), ((tokens, lat), BF16), ((top, tokens), F32)],
        specs=[vmem] * 4,
    )(ids, probs, cotangent, home)
    return (
        mixed, latent_gradient, gate_grad.T, summed[None, :, : 2 * ffw], summed[None, :, 2 * ffw :]
    )


def exchange(message, columns):
    rows, wide = message.shape
    moved = lax.all_to_all(
        message.reshape(columns, rows // columns, wide), "expert", split_axis=0, concat_axis=0, tiled=True
    )
    return moved.reshape(rows, wide)


def solution(mesh):
    return jax.shard_map(
        local,
        mesh=mesh,
        in_specs=(
            P(("dp", "expert"), None),
            P(("dp", "expert"), None),
            P(("dp", "expert"), None),
            P(("dp", "expert"), None),
            P("expert", None, None),
            P("expert", None, None),
        ),
        out_specs=(
            P(("dp", "expert"), None),
            P(("dp", "expert"), None),
            P(("dp", "expert"), None),
            P("expert", "dp", None),
            P("expert", "dp", None),
        ),
        check_vma=False,
    )
```

time: 244 us -> 241 us (0.988)
  waiting for transfers between devices: 140 us -> 152 us
  Pallas kernels: 0 us -> 11.2 us
  matrix products: 9.74 us -> 0 us
  other arithmetic: 8.49 us -> 0 us
  local copies, waits for them, and re-layouts: 11.9 us -> 6.32 us
    reduce_scatter x1, waiting for transfers between devices: 31.8 us -> 94.6 us  [local(): lax.psum_scatter(pair.reshape(lat // 2, width), 'dp', scatter_dimension=0...]
    all_to_all x2, waiting for transfers between devices: 108 us -> 53.1 us  [exchange(): lax.all_to_all(message.reshape(columns, rows // columns, wide), 'expert',...]
    pallas_call x0 -> x4, Pallas kernels: none -> 11.2 us  [the longest x1 5.57 us: local(): call(expert_kernel, [((rows, wide), BF16), half_terms, half_terms], scrat...]
    dot_general x12 -> x0, matrix products: 9.74 us -> none  [mm(): lax.dot_general(a, b, (((ca,), (cb,)), ((), ())), preferred_element_type=...]
    reshape x8 -> x0, local copies, waits for them, and re-layouts: 5.91 us -> none  [the longest x1 1.75 us: local(): out.reshape(columns, CAP, lat)]
    convert_element_type x3 -> x0, other arithmetic: 4.38 us -> none  [the longest x1 3.93 us: local(): (mine.astype(F32) + swapped.astype(F32)).astype(BF16)]
    ppermute x1, waiting for transfers between devices: 0.01 us -> 3.38 us  [local(): swapped = lax.ppermute(other, 'dp', [(i, i ^ 1) for i in range(replicas)])]
    unnamed x14 -> x16, local copies, waits for them, and re-layouts: 0.04 us -> 3.28 us
  transfers between devices with their start and end apart: 4 -> 4, of which waited for: 3 -> 3; matrix products, arithmetic and copies ran while one was open for 6% -> 1% of each run, Pallas kernels for 0% -> 0%
where the time goes in v2:
time: 241 us; the launch traced here: 240 us
  waiting for transfers between devices  152 us (63%)
  starting transfers between devices  57.1 us (24%)
  between operations  14.1 us (6%)
  Pallas kernels  11.2 us (5%)
  local copies, waits for them, and re-layouts  6.32 us (3%)
    reduce_scatter x1, waiting for transfers between devices, local(): lax.psum_scatter(pair.reshape(lat // 2, width), 'dp', scatter_dimension=0...  94.6 us
    all_to_all x2, starting transfers between devices, exchange(): lax.all_to_all(message.reshape(columns, rows // columns, wide), 'expert',...  55.2 us
    all_to_all x2, waiting for transfers between devices, exchange(): lax.all_to_all(message.reshape(columns, rows // columns, wide), 'expert',...  53.1 us
    pallas_call x1, Pallas kernels, local(): call(expert_kernel, [((rows, wide), BF16), half_terms, half_terms], scrat...  5.57 us
  transfers between devices with their start and end apart: 4, of which 3 were waited for; matrix products, arithmetic and copies ran while one was open for 1% of the time, Pallas kernels for 0%

profile of v2, /device:TPU:24, one launch (start us, length us, event | category | flops | bytes accessed | tf_op | source)
XLA Modules:
  0.0 240.4 jit_solution(15349968741281229573)
XLA Ops:
  7.2 0.0 copy-start
  7.2 0.9 copy-done
  8.1 0.9 copy-done.3
  9.1 0.7 copy-done.4
  9.8 0.7 copy-done.6
  10.4 1.9 pack_kernel.1
  12.3 34.2 %all-to-all-start = ((bf16[64,8,512]{2,1,0:T(8,128)(2,1)}), bf16[64,8,512]{2,1,0:T(8,128)(2,1)S(1)}, u32[]{:S(2)}, u32[]{:S(2)}) async-start(bf16[64,8,512]{2,1,0:T(8,128)(2,1)} %bitcast.3), calls=%async_computation | async-start | bytes 1048576 | tf_op jit(solution)/shard_map/all_to_all | solution.py:196
  46.5 53.1 %all-to-all-done = bf16[64,8,512]{2,1,0:T(8,128)(2,1)S(1)} async-done(((bf16[64,8,512]{2,1,0:T(8,128)(2,1)}), bf16[64,8,512]{2,1,0:T(8,128)(2,1)S(1)}, u32[]{:S(2)}, u32[]{:S(2)}) %all-to-all-start) | async-done | bytes 524320 | tf_op jit(solution)/shard_map/all_to_all | solution.py:196
  99.6 0.0 copy-done.2
  99.6 5.6 %expert_kernel.1 = (bf16[512,512]{1,0:T(8,128)(2,1)}, bf16[8,64,1536]{2,1,0:T(8,128)(2,1)S(1)}, bf16[8,64,1536]{2,1,0:T(8,128)(2,1)S(1)}) custom-call(s32[1]{0:T(128)} %bitcast.2.core_ref, bf16[512,512]{1,0:T(8,128)(2,1)S(1)} %bitcast.16, bf16[1024,1024]{1,0:T(8,128)(2,1)} %bitcast.22, bf16[1024,512]{1,0:T(8,128)(2,1)S(1)} %bitcast.17), custom_call_target="tpu_custom_call" | custom-call | tf_op jit(solution)/shard_map/expert_kernel/pallas_call | solution.py:169
  105.2 1.9 collective-permute-start
  107.1 3.4 %collective-permute-done.b_ref = bf16[8,64,1536]{2,1,0:T(8,128)(2,1)S(1)} collective-permute-done((bf16[8,64,1536]{2,1,0:T(8,128)(2,1)S(1)}, bf16[8,64,1536]{2,1,0:T(8,128)(2,1)S(1)}, u32[]{:S(2)}, u32[]{:S(2)}) %collective-permute-start) | collective-permute-done | bytes 1572896 | tf_op jit(solution)/shard_map/ppermute | solution.py:176
  110.5 1.5 add_kernel.1
  112.0 20.9 %all-to-all-start.1 = ((bf16[64,8,512]{2,1,0:T(8,128)(2,1)}), bf16[64,8,512]{2,1,0:T(8,128)(2,1)S(1)}, u32[]{:S(2)}, u32[]{:S(2)}) async-start(bf16[64,8,512]{2,1,0:T(8,128)(2,1)} %bitcast.7), calls=%async_computation.1 | async-start | bytes 1048576 | tf_op jit(solution)/shard_map/all_to_all | solution.py:196
  133.0 0.0 reduce-scatter.2.cloned.1.call-start
  133.0 0.7 reduce-scatter.2.cloned.1.call-update
  133.7 94.6 %reduce-scatter.2.cloned.1.call-done = bf16[64,1536]{1,0:T(8,128)(2,1)} async-done(((bf16[512,1536]{1,0:T(8,128)(2,1)}), bf16[64,1536]{1,0:T(8,128)(2,1)}) %reduce-scatter.2.cloned.1.call-update) | async-done | bytes 196624 | tf_op jit(solution)/shard_map/reduce_scatter | solution.py:179
  228.3 1.5 slice_bitcast_fusion.1
  229.8 1.6 slice_bitcast_fusion
  231.4 0.0 all-to-all-done.1
  231.4 0.0 copy-done.1
  231.4 0.0 copy-done.5
  231.4 0.0 copy-done.7
  231.4 2.2 combine_kernel.1
  (7 shorter events, 0.0 us)
Async XLA Ops:
  7.2 1.0 copy-start
  8.1 0.9 copy-start.3
  9.1 0.7 copy-start.4
  9.8 0.7 copy-start.6
  10.4 89.2 %copy-start.2 = (bf16[1,1024,512]{2,1,0:T(8,128)(2,1)S(1)}, bf16[1,1024,512]{2,1,0:T(8,128)(2,1)}, u32[]{:S(2)}) copy-start(bf16[1,1024,512]{2,1,0:T(8,128)(2,1)} %param.11) | copy-start | bytes 3145732
  12.3 87.3 %all-to-all-start = ((bf16[64,8,512]{2,1,0:T(8,128)(2,1)}), bf16[64,8,512]{2,1,0:T(8,128)(2,1)S(1)}, u32[]{:S(2)}, u32[]{:S(2)}) async-start(bf16[64,8,512]{2,1,0:T(8,128)(2,1)} %bitcast.3), calls=%async_computation | async-start | bytes 1048576 | tf_op jit(solution)/shard_map/all_to_all | solution.py:196
  105.2 5.3 %collective-permute-start = (bf16[8,64,1536]{2,1,0:T(8,128)(2,1)S(1)}, bf16[8,64,1536]{2,1,0:T(8,128)(2,1)S(1)}, u32[]{:S(2)}, u32[]{:S(2)}) collective-permute-start(bf16[8,64,1536]{2,1,0:T(8,128)(2,1)S(1)} %get-tuple-element.14), channel_id=1, source_target_pairs={{0,64},{64,0},{128,192},{192,128},{256,320},{320,256},{384,448},{4... | collective-permute-start | bytes 4718600 | tf_op jit(solution)/shard_map/ppermute | solution.py:176
  112.0 119.4 %copy-start.1 = (bf16[128,1024]{1,0:T(8,128)(2,1)S(1)}, bf16[128,1024]{1,0:T(8,128)(2,1)}, u32[]{:S(2)}) copy-start(bf16[128,1024]{1,0:T(8,128)(2,1)} %cot_ref.3) | copy-start | bytes 786436
  112.0 119.4 %copy-start.5 = (s32[128,8]{0,1:T(8,128)S(1)}, s32[128,8]{0,1:T(8,128)}, u32[]{:S(2)}) copy-start(s32[128,8]{0,1:T(8,128)} %param.7) | copy-start | bytes 12292
  112.0 119.4 %copy-start.7 = (f32[128,8]{0,1:T(8,128)S(1)}, f32[128,8]{0,1:T(8,128)}, u32[]{:S(2)}) copy-start(f32[128,8]{0,1:T(8,128)} %param.8) | copy-start | bytes 12292
  112.0 119.3 %all-to-all-start.1 = ((bf16[64,8,512]{2,1,0:T(8,128)(2,1)}), bf16[64,8,512]{2,1,0:T(8,128)(2,1)S(1)}, u32[]{:S(2)}, u32[]{:S(2)}) async-start(bf16[64,8,512]{2,1,0:T(8,128)(2,1)} %bitcast.7), calls=%async_computation.1 | async-start | bytes 1048576 | tf_op jit(solution)/shard_map/all_to_all | solution.py:196
  133.0 95.4 %reduce-scatter.2.cloned.1.call-start = ((), (), s32[]{:S(2)}) async-start(), calls=%async_computation.3 | async-start | bytes 1769472 | tf_op jit(solution)/shard_map/reduce_scatter | solution.py:179
Sparse Core Ops, SparseCore 0:
  137.2 91.0 reduce-scatter.1

commit v3 on v2

--- a/solution.py
+++ b/solution.py
@@ -11,6 +11,7 @@
 F32 = jnp.float32
 BF16 = jnp.bfloat16
 VMEM_BYTES = 48 << 20
+ALL_VMEM_BYTES = 63 << 20
 
 
 def mm(a, b, ca=1, cb=0):
@@ -49,11 +50,19 @@
     return jnp.where(mask, 1.0, 0.0).astype(BF16)
 
 
-def pack_kernel(ids_ref, probs_ref, latent_ref, cot_ref, sent_ref):
+def pack_kernel(ids_hbm, probs_hbm, latent_hbm, cot_hbm, sent_ref, ids_ref, probs_ref, latent_ref, cot_ref, sems):
     rows, wide = sent_ref.shape
+    pairs = [(ids_hbm, ids_ref), (probs_hbm, probs_ref), (latent_hbm, latent_ref), (cot_hbm, cot_ref)]
+    copies = [pltpu.make_async_copy(a, b, sems.at[i]) for i, (a, b) in enumerate(pairs)]
+    for copy in copies:
+        copy.start()
+    copies[0].wait()
+    copies[1].wait()
     pick, gate, first, low, _ = routing(ids_ref, probs_ref, rows)
     token = jnp.where(pick & first, 1.0, 0.0)
     weight = jnp.where(pick & ~first, gate, 0.0)
+    copies[2].wait()
+    copies[3].wait()
     total = jnp.zeros((rows, wide), F32)
     for h in range(2):
         here = low if h == 0 else ~low
@@ -70,7 +79,9 @@
     return ((index & 2) + ((index >> 2) & 1)) * slots + group * CAP + (index & 1)
 
 
-def expert_kernel(core_ref, there_ref, win_ref, wout_ref, back_ref, mine_ref, other_ref, terms_ref):
+def expert_kernel(
+    core_ref, there_ref, win_ref, wout_ref, mine_ref, other_ref, act_ref, grad_ref, terms_ref
+):
     rows, wide = there_ref.shape
     slots = rows // 4
     ffw = wout_ref.shape[1]
@@ -90,6 +101,8 @@
     grad_hidden = jnp.concatenate(
         [grad_act * u * s * (1.0 + g * (1.0 - s)), grad_act * g * s], axis=1
     ).astype(BF16)
+    act_ref[...] = act
+    grad_ref[...] = grad_hidden
 
     for h in range(2):
         terms_ref[top[h], : 2 * ffw] = mm(vec[h], grad_hidden, 0, 0).astype(BF16)
@@ -101,6 +114,13 @@
         mine_ref[block] = jnp.where(even, a, b)
         other_ref[block] = jnp.where(even, b, a)
 
+
+def return_kernel(act_ref, grad_ref, win_ref, wout_ref, back_ref):
+    rows, wide = back_ref.shape
+    slots = rows // 4
+    top = [pl.ds(0, wide), pl.ds(wide, wide)]
+    act = act_ref[...]
+    grad_hidden = grad_ref[...]
     result = jnp.concatenate(
         [mm(act, wout_ref[top[h], :], 1, 1).astype(BF16) for h in range(2)]
         + [mm(grad_hidden, win_ref[top[h], :], 1, 1).astype(BF16) for h in range(2)],
@@ -110,17 +130,39 @@
     back_ref[...] = mm(unsort, result).astype(BF16)
 
 
+def split_kernel(sum_hbm, gate_up_ref, down_ref, sems):
+    cut = gate_up_ref.shape[1]
+    copies = [
+        pltpu.make_async_copy(sum_hbm.at[:, pl.ds(0, cut)], gate_up_ref, sems.at[0]),
+        pltpu.make_async_copy(sum_hbm.at[:, pl.ds(cut, down_ref.shape[1])], down_ref, sems.at[1]),
+    ]
+    for copy in copies:
+        copy.start()
+    for copy in copies:
+        copy.wait()
+
+
 def add_kernel(a_ref, b_ref, out_ref):
     out_ref[...] = (a_ref[...].astype(F32) + b_ref[...].astype(F32)).astype(BF16)
 
 
-def combine_kernel(ids_ref, probs_ref, cot_ref, home_ref, mixed_ref, latgrad_ref, gate_ref):
+def mask_kernel(ids_ref, probs_ref, pick_ref, weight_ref):
+    pick, gate, first, _, _ = routing(ids_ref, probs_ref, weight_ref.shape[0])
+    pick_ref[...] = zero_one(pick)
+    weight_ref[...] = jnp.where(pick & first, gate, 0.0)
+
+
+def combine_kernel(ids_ref, pick_ref, weight_ref, cot_ref, home_ref, mixed_ref, latgrad_ref, gate_ref):
     rows, wide = home_ref.shape
-    pick, gate, first, low, expert = routing(ids_ref, probs_ref, rows)
+    weight = weight_ref[...]
+    pick = pick_ref[...].astype(F32)
+    row = iota(weight.shape, 0)
+    expert = (row // GROUP) * EXP_DEV
+    first = (row & 2) == 0
+    low = (row & 4) == 0
     home = home_ref[...]
-    chosen = pick & first
-    weight = jnp.where(chosen, gate, 0.0)
-    token = jnp.where(pick & ~first, 1.0, 0.0)
+    chosen = jnp.where(first, pick, 0.0)
+    token = pick - chosen
     inner = jnp.zeros(weight.shape, F32)
     for h in range(2):
         here = low if h == 0 else ~low
@@ -128,13 +170,14 @@
         high, rest = halves(jnp.where(here, weight, 0.0))
         mixed_ref[:, cols] = (mm(high, home, 0, 0) + mm(rest, home, 0, 0)).astype(BF16)
         latgrad_ref[:, cols] = mm(jnp.where(here, token, 0.0).astype(BF16), home, 0, 0).astype(BF16)
-        inner = jnp.where(here & chosen, mm(home, cot_ref[:, cols], 1, 1), inner)
+        inner = jnp.where(here, mm(home, cot_ref[:, cols], 1, 1), inner)
+    inner = jnp.where(chosen > 0.5, inner, 0.0)
     for slot in range(ids_ref.shape[0]):
         hit = ids_ref[slot : slot + 1, :] == expert
         gate_ref[slot : slot + 1, :] = jnp.sum(jnp.where(hit, inner, 0.0), axis=0, keepdims=True)
 
 
-def call(kernel, outs, scratch=(), specs=None):
+def call(kernel, outs, scratch=(), specs=None, vmem=VMEM_BYTES):
     shapes = [jax.ShapeDtypeStruct(shape, dtype) for shape, dtype in outs]
     return pl.pallas_call(
         kernel,
@@ -142,7 +185,7 @@
         in_specs=specs,
         out_specs=[pl.BlockSpec(memory_space=pltpu.VMEM)] * len(shapes),
         scratch_shapes=list(scratch),
-        compiler_params=pltpu.CompilerParams(vmem_limit_bytes=VMEM_BYTES),
+        compiler_params=pltpu.CompilerParams(vmem_limit_bytes=vmem),
         name=kernel.__name__,
     )
 
@@ -161,34 +204,56 @@
     probs = gate_probs.T
     vmem = pl.BlockSpec(memory_space=pltpu.VMEM)
 
-    (sent,) = call(pack_kernel, [((rows, wide), BF16)], specs=[vmem] * 4)(ids, probs, latent, cotangent)
+    (sent,) = call(
+        pack_kernel,
+        [((rows, wide), BF16)],
+        scratch=[pltpu.VMEM(a.shape, a.dtype) for a in (ids, probs, latent, cotangent)]
+        + [pltpu.SemaphoreType.DMA((4,))],
+        specs=[pl.BlockSpec(memory_space=pl.ANY)] * 4,
+        vmem=ALL_VMEM_BYTES,
+    )(ids, probs, latent, cotangent)
     there = exchange(sent, columns)
 
     core = (lax.axis_index("dp") % 2).astype(jnp.int32).reshape(1)
     half_terms = ((replicas // 2, share, width), BF16)
-    back, mine, other = call(
+    slots = columns * CAP
+    mine, other, act, grad_hidden = call(
         expert_kernel,
-        [((rows, wide), BF16), half_terms, half_terms],
+        [half_terms, half_terms, ((slots, ffw), BF16), ((slots, 2 * ffw), BF16)],
         scratch=[pltpu.VMEM((lat, width), BF16)],
         specs=[pl.BlockSpec(memory_space=pltpu.SMEM)] + [vmem] * 3,
     )(core, there, w_gate_up[0], w_down[0])
 
     swapped = lax.ppermute(other, "dp", [(i, i ^ 1) for i in range(replicas)])
+    (back,) = call(return_kernel, [((rows, wide), BF16)], specs=[vmem] * 4)(
+        act, grad_hidden, w_gate_up[0], w_down[0]
+    )
     (pair,) = call(add_kernel, [half_terms], specs=[vmem] * 2)(mine, swapped)
     pair, back = lax.optimization_barrier((pair, back))
     summed = lax.psum_scatter(
         pair.reshape(lat // 2, width), "dp", scatter_dimension=0, tiled=True,
         axis_index_groups=[list(range(c, replicas, 2)) for c in range(2)],
     )
-    home = exchange(back, columns)
+    home = lax.cond(core[0] < 2, lambda b: exchange(b, columns), lambda b: b, back)
+    pick, weight = call(
+        mask_kernel, [((rows, tokens), BF16), ((rows, tokens), F32)], specs=[vmem] * 2
+    )(ids, probs)
     mixed, latent_gradient, gate_grad = call(
         combine_kernel,
         [((tokens, lat), BF16), ((tokens, lat), BF16), ((top, tokens), F32)],
-        specs=[vmem] * 4,
-    )(ids, probs, cotangent, home)
-    return (
-        mixed, latent_gradient, gate_grad.T, summed[None, :, : 2 * ffw], summed[None, :, 2 * ffw :]
-    )
+        specs=[vmem] * 5,
+    )(ids, pick, weight, cotangent, home)
+    summed, mixed, latent_gradient, gate_grad = lax.optimization_barrier(
+        (summed, mixed, latent_gradient, gate_grad)
+    )
+    gate_up_grad, down_grad = call(
+        split_kernel,
+        [((share, 2 * ffw), BF16), ((share, ffw), BF16)],
+        scratch=[pltpu.SemaphoreType.DMA((2,))],
+        specs=[pl.BlockSpec(memory_space=pl.ANY)],
+        vmem=ALL_VMEM_BYTES,
+    )(summed)
+    return (mixed, latent_gradient, gate_grad.T, gate_up_grad[None], down_grad[None])
 
 
 def exchange(message, columns):

time: 241 us -> 227 us (0.942)
  blocking collectives: 0 us -> 78.3 us
  waiting for transfers between devices: 152 us -> 84.4 us
  starting transfers between devices: 57.1 us -> 36.3 us
  local copies, waits for them, and re-layouts: 6.32 us -> 0.72 us
    all_to_all x0 -> x1, blocking collectives: none -> 78.3 us  [exchange(): lax.all_to_all(message.reshape(columns, rows // columns, wide), 'expert',...]
    reduce_scatter x1, waiting for transfers between devices: 94.6 us -> 29.4 us  [local(): lax.psum_scatter(pair.reshape(lat // 2, width), 'dp', scatter_dimension=0...]
    all_to_all x2 -> x1, starting transfers between devices: 55.2 us -> 34.4 us  [exchange(): lax.all_to_all(message.reshape(columns, rows // columns, wide), 'expert',...]
    broadcast_in_dim x2 -> x0, local copies, waits for them, and re-layouts: 3.04 us -> none  [the longest x1 1.57 us: local(): summed[None, :, :2 * ffw]]
    unnamed x16 -> x10, local copies, waits for them, and re-layouts: 3.28 us -> 0.69 us
    pallas_call x2 -> x5, Pallas kernels: 7.43 us -> 9.91 us  [the longest x1 3.64 us: local(): call(expert_kernel, [half_terms, half_terms, ((slots, ffw), BF16), ((slot...]
    all_to_all x2 -> x1, waiting for transfers between devices: 53.1 us -> 53 us  [exchange(): lax.all_to_all(message.reshape(columns, rows // columns, wide), 'expert',...]
  transfers between devices with their start and end apart: 4 -> 3, of which waited for: 3 -> 3; matrix products, arithmetic and copies ran while one was open for 1% -> 0% of each run, Pallas kernels for 0% -> 2%
where the time goes in v3:
time: 227 us
  waiting for transfers between devices  84.4 us (37%)
  blocking collectives  78.3 us (34%)
  starting transfers between devices  36.3 us (16%)
  between operations  14.1 us (6%)
  Pallas kernels  13.3 us (6%)
    all_to_all x1, blocking collectives, exchange(): lax.all_to_all(message.reshape(columns, rows // columns, wide), 'expert',...  78.3 us
    all_to_all x1, waiting for transfers between devices, exchange(): lax.all_to_all(message.reshape(columns, rows // columns, wide), 'expert',...  53 us
    all_to_all x1, starting transfers between devices, exchange(): lax.all_to_all(message.reshape(columns, rows // columns, wide), 'expert',...  34.4 us
    reduce_scatter x1, waiting for transfers between devices, local(): lax.psum_scatter(pair.reshape(lat // 2, width), 'dp', scatter_dimension=0...  29.4 us
  transfers between devices with their start and end apart: 3, of which 3 were waited for; matrix products, arithmetic and copies ran while one was open for 0% of the time, Pallas kernels for 2%

profile of v3, /device:TPU:24, one launch (start us, length us, event | category | flops | bytes accessed | tf_op | source)
XLA Modules:
  0.0 227.1 jit_solution(6299566747025923293)
XLA Ops:
  7.2 2.8 %pack_kernel.1 = bf16[512,512]{1,0:T(8,128)(2,1)} custom-call(s32[8,128]{1,0:T(8,128)} %bitcast.18, f32[8,128]{1,0:T(8,128)} %bitcast.21, bf16[128,1024]{1,0:T(8,128)(2,1)} %latent_hbm.1, bf16[128,1024]{1,0:T(8,128)(2,1)} %cot_ref.1), custom_call_target="tpu_custom_call" | custom-call | tf_op jit(solution)/shard_map/pack_kernel/pallas_call | solution.py:207
  10.0 0.0 copy-start.1
  10.0 34.4 %all-to-all-start.1 = ((bf16[64,8,512]{2,1,0:T(8,128)(2,1)}), bf16[64,8,512]{2,1,0:T(8,128)(2,1)S(1)}, u32[]{:S(2)}, u32[]{:S(2)}) async-start(bf16[64,8,512]{2,1,0:T(8,128)(2,1)} %bitcast.25), calls=%async_computation.1 | async-start | bytes 1048576 | tf_op jit(solution)/shard_map/all_to_all | solution.py:261
  44.3 0.0 reduce-scatter.2.cloned.1.call-start
  44.4 53.0 %all-to-all-done.1 = bf16[64,8,512]{2,1,0:T(8,128)(2,1)S(1)} async-done(((bf16[64,8,512]{2,1,0:T(8,128)(2,1)}), bf16[64,8,512]{2,1,0:T(8,128)(2,1)S(1)}, u32[]{:S(2)}, u32[]{:S(2)}) %all-to-all-start.1) | async-done | bytes 524320 | tf_op jit(solution)/shard_map/all_to_all | solution.py:261
  97.4 0.0 copy-done.1
  97.4 0.0 copy-start
  97.4 3.6 %expert_kernel.1 = (bf16[8,64,1536]{2,1,0:T(8,128)(2,1)S(1)}, bf16[8,64,1536]{2,1,0:T(8,128)(2,1)S(1)}, bf16[128,512]{1,0:T(8,128)(2,1)S(1)}, bf16[128,1024]{1,0:T(8,128)(2,1)S(1)}) custom-call(s32[1]{0:T(128)} %bitcast.2.core_ref, bf16[512,512]{1,0:T(8,128)(2,1)S(1)} %bitcast.17, bf16[1024,1024]{1,0:T(8,128)(2,1)} %bitcast.13, bf16[1024,512]{1,0:T(8,128)(2,1)S(1)} %bitcast.15), custom_call_target="tpu_custom_call" | custom-call | tf_op jit(solution)/shard_map/expert_kernel/pallas_call | solution.py:220
  101.1 1.9 collective-permute-start
  103.0 0.0 copy-done
  103.0 1.4 return_kernel.1
  104.5 1.9 collective-permute-done.b_ref
  106.4 1.5 add_kernel.1
  107.9 0.0 copy-start.3
  107.9 0.0 reduce-scatter.2.cloned.1.call-update
  107.9 0.7 copy-done.3
  108.6 0.0 copy-done.4
  108.6 0.4 mask_kernel.1
  109.1 78.3 %conditional.1 = (bf16[512,512]{1,0:T(8,128)(2,1)S(1)}) conditional(s32[]{:T(128)} %convert_element_type.3, bf16[512,512]{1,0:T(8,128)(2,1)S(1)} %return_kernel.1, bf16[512,512]{1,0:T(8,128)(2,1)S(1)} %return_kernel.1), branch_computations={%region_1.2_spmd, %region_2.3_spmd} | conditional | bytes 2097160 | solution.py:237
  109.1 78.3 %all_to_all.9 = bf16[64,8,512]{2,1,0:T(8,128)(2,1)S(1)} all-to-all(bf16[64,8,512]{2,1,0:T(8,128)(2,1)S(1)} %copy.13), channel_id=1, replica_groups=mesh['dp'=16,'expert'=64] {'expert'}, dimensions={0} | all-to-all | bytes 1048576 | tf_op jit(solution)/shard_map/cond/branch_1_fun/all_to_all | solution.py:261
  187.4 0.0 copy-done.2
  187.4 1.9 combine_kernel.1
  189.3 29.4 %reduce-scatter.2.cloned.1.call-done.sum_hbm = bf16[64,1536]{1,0:T(8,128)(2,1)} async-done(((bf16[512,1536]{1,0:T(8,128)(2,1)}), bf16[64,1536]{1,0:T(8,128)(2,1)}) %reduce-scatter.2.cloned.1.call-update) | async-done | bytes 196624 | tf_op jit(solution)/shard_map/reduce_scatter | solution.py:233
  218.7 1.6 split_kernel.1
  (3 shorter events, 0.0 us)
Async XLA Ops:
  10.0 87.5 %copy-start.1 = (bf16[1,1024,512]{2,1,0:T(8,128)(2,1)S(1)}, bf16[1,1024,512]{2,1,0:T(8,128)(2,1)}, u32[]{:S(2)}) copy-start(bf16[1,1024,512]{2,1,0:T(8,128)(2,1)} %param.13) | copy-start | bytes 3145732
  10.0 87.4 %all-to-all-start.1 = ((bf16[64,8,512]{2,1,0:T(8,128)(2,1)}), bf16[64,8,512]{2,1,0:T(8,128)(2,1)S(1)}, u32[]{:S(2)}, u32[]{:S(2)}) async-start(bf16[64,8,512]{2,1,0:T(8,128)(2,1)} %bitcast.25), calls=%async_computation.1 | async-start | bytes 1048576 | tf_op jit(solution)/shard_map/all_to_all | solution.py:261
  44.3 174.3 %reduce-scatter.2.cloned.1.call-start = ((), (), s32[]{:S(2)}) async-start(), calls=%async_computation.3 | async-start | bytes 1769472 | tf_op jit(solution)/shard_map/reduce_scatter | solution.py:233
  97.4 5.6 %copy-start = (bf16[1,1024,1024]{2,1,0:T(8,128)(2,1)S(1)}, bf16[1,1024,1024]{2,1,0:T(8,128)(2,1)}, u32[]{:S(2)}) copy-start(bf16[1,1024,1024]{2,1,0:T(8,128)(2,1)} %param.12) | copy-start | bytes 6291460
  101.1 5.3 %collective-permute-start = (bf16[8,64,1536]{2,1,0:T(8,128)(2,1)S(1)}, bf16[8,64,1536]{2,1,0:T(8,128)(2,1)S(1)}, u32[]{:S(2)}, u32[]{:S(2)}) collective-permute-start(bf16[8,64,1536]{2,1,0:T(8,128)(2,1)S(1)} %get-tuple-element.28), channel_id=1, source_target_pairs={{0,64},{64,0},{128,192},{192,128},{256,320},{320,256},{384,448},{4... | collective-permute-start | bytes 4718600 | tf_op jit(solution)/shard_map/ppermute | solution.py:227
  107.9 0.7 copy-start.3
  107.9 0.7 copy-start.4
  107.9 79.5 %copy-start.2 = (bf16[128,1024]{1,0:T(8,128)(2,1)S(1)}, bf16[128,1024]{1,0:T(8,128)(2,1)}, u32[]{:S(2)}) copy-start(bf16[128,1024]{1,0:T(8,128)(2,1)} %cot_ref.1) | copy-start | bytes 786436
Sparse Core Ops, SparseCore 0:
  108.0 110.5 reduce-scatter.1

commit v4 on v3

--- a/solution.py
+++ b/solution.py
@@ -8,6 +8,7 @@
 EXP_DEV = 4
 CAP = 2
 GROUP = 4 * CAP
+RING = 4
 F32 = jnp.float32
 BF16 = jnp.bfloat16
 VMEM_BYTES = 48 << 20
@@ -27,10 +28,24 @@
     return high, (value - high.astype(F32)).astype(BF16)
 
 
-def routing(ids_ref, probs_ref, rows):
-    tokens = ids_ref.shape[1]
+def leaving(row, rows):
+    part = rows // RING
+    return row // part, (row % part) // GROUP
+
+
+def arriving(row):
+    piece = (row // GROUP) % RING
+    step = jnp.where(piece == 0, 0, jnp.where(piece == 1, RING - 1, piece - 1))
+    return step, row // (GROUP * RING)
+
+
+def expert_id(step, place, plane, rows):
+    return (((plane + step) % RING) * (rows // (GROUP * RING)) + place) * EXP_DEV
+
+
+def routing(ids_ref, probs_ref, expert):
+    rows, tokens = expert.shape
     row = iota((rows, tokens), 0)
-    expert = (row // GROUP) * EXP_DEV
     named = jnp.zeros((rows, tokens), F32)
     gate = jnp.zeros((rows, tokens), F32)
     for slot in range(ids_ref.shape[0]):
@@ -43,22 +58,36 @@
     pick = (named > 0.5) & (earlier == (row & 1).astype(F32))
     kind = (row & 2) == 0
     half = (row & 4) == 0
-    return pick, gate, kind, half, expert
+    return pick, gate, kind, half
 
 
 def zero_one(mask):
     return jnp.where(mask, 1.0, 0.0).astype(BF16)
 
 
-def pack_kernel(ids_hbm, probs_hbm, latent_hbm, cot_hbm, sent_ref, ids_ref, probs_ref, latent_ref, cot_ref, sems):
-    rows, wide = sent_ref.shape
+def store_leaving(message, stay_ref, right_ref, left_ref):
+    part = stay_ref.shape[0]
+    middle = 2 * part + part // 2
+    stay_ref[...] = message[:part]
+    right_ref[...] = message[part:middle]
+    left_ref[...] = message[middle:]
+
+
+def pack_kernel(
+    plane_ref, ids_hbm, probs_hbm, latent_hbm, cot_hbm, stay_ref, right_ref, left_ref,
+    ids_ref, probs_ref, latent_ref, cot_ref, sems
+):
+    part, wide = stay_ref.shape
+    rows = RING * part
     pairs = [(ids_hbm, ids_ref), (probs_hbm, probs_ref), (latent_hbm, latent_ref), (cot_hbm, cot_ref)]
     copies = [pltpu.make_async_copy(a, b, sems.at[i]) for i, (a, b) in enumerate(pairs)]
     for copy in copies:
         copy.start()
     copies[0].wait()
     copies[1].wait()
-    pick, gate, first, low, _ = routing(ids_ref, probs_ref, rows)
+    step, place = leaving(iota((rows, ids_ref.shape[1]), 0), rows)
+    expert = expert_id(step, place, plane_ref[0], rows)
+    pick, gate, first, low = routing(ids_ref, probs_ref, expert)
     token = jnp.where(pick & first, 1.0, 0.0)
     weight = jnp.where(pick & ~first, gate, 0.0)
     copies[2].wait()
@@ -71,7 +100,7 @@
         cols = pl.ds(h * wide, wide)
         cot = cot_ref[:, cols]
         total = total + mm(picks, jnp.concatenate([latent_ref[:, cols], cot, cot], axis=0))
-    sent_ref[...] = total.astype(BF16)
+    store_leaving(total.astype(BF16), stay_ref, right_ref, left_ref)
 
 
 def sorted_position(index, slots):
@@ -115,8 +144,9 @@
         other_ref[block] = jnp.where(even, b, a)
 
 
-def return_kernel(act_ref, grad_ref, win_ref, wout_ref, back_ref):
-    rows, wide = back_ref.shape
+def return_kernel(act_ref, grad_ref, win_ref, wout_ref, stay_ref, right_ref, left_ref):
+    part, wide = stay_ref.shape
+    rows = RING * part
     slots = rows // 4
     top = [pl.ds(0, wide), pl.ds(wide, wide)]
     act = act_ref[...]
@@ -126,8 +156,12 @@
         + [mm(grad_hidden, win_ref[top[h], :], 1, 1).astype(BF16) for h in range(2)],
         axis=0,
     )
-    unsort = zero_one(iota((rows, rows), 1) == sorted_position(iota((rows, rows), 0), slots))
-    back_ref[...] = mm(unsort, result).astype(BF16)
+    row = iota((rows, rows), 0)
+    step, place = leaving(row, rows)
+    piece = jnp.where(step == 0, 0, jnp.where(step == RING - 1, 1, step + 1))
+    source = (place * RING + piece) * GROUP + row % GROUP
+    unsort = zero_one(iota((rows, rows), 1) == sorted_position(source, slots))
+    store_leaving(mm(unsort, result).astype(BF16), stay_ref, right_ref, left_ref)
 
 
 def split_kernel(sum_hbm, gate_up_ref, down_ref, sems):
@@ -146,18 +180,21 @@
     out_ref[...] = (a_ref[...].astype(F32) + b_ref[...].astype(F32)).astype(BF16)
 
 
-def mask_kernel(ids_ref, probs_ref, pick_ref, weight_ref):
-    pick, gate, first, _, _ = routing(ids_ref, probs_ref, weight_ref.shape[0])
+def mask_kernel(plane_ref, ids_ref, probs_ref, pick_ref, weight_ref):
+    step, place = arriving(iota(weight_ref.shape, 0))
+    expert = expert_id(step, place, plane_ref[0], weight_ref.shape[0])
+    pick, gate, first, _ = routing(ids_ref, probs_ref, expert)
     pick_ref[...] = zero_one(pick)
     weight_ref[...] = jnp.where(pick & first, gate, 0.0)
 
 
-def combine_kernel(ids_ref, pick_ref, weight_ref, cot_ref, home_ref, mixed_ref, latgrad_ref, gate_ref):
+def combine_kernel(plane_ref, ids_ref, pick_ref, weight_ref, cot_ref, home_ref, mixed_ref, latgrad_ref, gate_ref):
     rows, wide = home_ref.shape
     weight = weight_ref[...]
     pick = pick_ref[...].astype(F32)
     row = iota(weight.shape, 0)
-    expert = (row // GROUP) * EXP_DEV
+    step, place = arriving(row)
+    expert = expert_id(step, place, plane_ref[0], rows)
     first = (row & 2) == 0
     low = (row & 4) == 0
     home = home_ref[...]
@@ -204,15 +241,20 @@
     probs = gate_probs.T
     vmem = pl.BlockSpec(memory_space=pltpu.VMEM)
 
-    (sent,) = call(
+    smem = pl.BlockSpec(memory_space=pltpu.SMEM)
+    plane = (lax.axis_index("expert") // (columns // RING)).astype(jnp.int32).reshape(1)
+    part = rows // RING
+    leave = [((part, wide), BF16), ((part + part // 2, wide), BF16), ((part + part // 2, wide), BF16)]
+
+    sent = call(
         pack_kernel,
-        [((rows, wide), BF16)],
+        leave,
         scratch=[pltpu.VMEM(a.shape, a.dtype) for a in (ids, probs, latent, cotangent)]
         + [pltpu.SemaphoreType.DMA((4,))],
-        specs=[pl.BlockSpec(memory_space=pl.ANY)] * 4,
+        specs=[smem] + [pl.BlockSpec(memory_space=pl.ANY)] * 4,
         vmem=ALL_VMEM_BYTES,
-    )(ids, probs, latent, cotangent)
-    there = exchange(sent, columns)
+    )(plane, ids, probs, latent, cotangent)
+    there = exchange(*sent)
 
     core = (lax.axis_index("dp") % 2).astype(jnp.int32).reshape(1)
     half_terms = ((replicas // 2, share, width), BF16)
@@ -221,28 +263,33 @@
         expert_kernel,
         [half_terms, half_terms, ((slots, ffw), BF16), ((slots, 2 * ffw), BF16)],
         scratch=[pltpu.VMEM((lat, width), BF16)],
-        specs=[pl.BlockSpec(memory_space=pltpu.SMEM)] + [vmem] * 3,
+        specs=[smem] + [vmem] * 3,
     )(core, there, w_gate_up[0], w_down[0])
 
     swapped = lax.ppermute(other, "dp", [(i, i ^ 1) for i in range(replicas)])
-    (back,) = call(return_kernel, [((rows, wide), BF16)], specs=[vmem] * 4)(
+    back = call(return_kernel, leave, specs=[vmem] * 4)(
         act, grad_hidden, w_gate_up[0], w_down[0]
     )
     (pair,) = call(add_kernel, [half_terms], specs=[vmem] * 2)(mine, swapped)
-    pair, back = lax.optimization_barrier((pair, back))
+    pair, *back = lax.optimization_barrier((pair, *back))
     summed = lax.psum_scatter(
         pair.reshape(lat // 2, width), "dp", scatter_dimension=0, tiled=True,
         axis_index_groups=[list(range(c, replicas, 2)) for c in range(2)],
     )
-    home = lax.cond(core[0] < 2, lambda b: exchange(b, columns), lambda b: b, back)
+    home = lax.cond(
+        core[0] < 2,
+        lambda stay, right, left: exchange(stay, right, left),
+        lambda stay, right, left: jnp.concatenate([stay, right, left], axis=0),
+        *back,
+    )
     pick, weight = call(
-        mask_kernel, [((rows, tokens), BF16), ((rows, tokens), F32)], specs=[vmem] * 2
-    )(ids, probs)
+        mask_kernel, [((rows, tokens), BF16), ((rows, tokens), F32)], specs=[smem] + [vmem] * 2
+    )(plane, ids, probs)
     mixed, latent_gradient, gate_grad = call(
         combine_kernel,
         [((tokens, lat), BF16), ((tokens, lat), BF16), ((top, tokens), F32)],
-        specs=[vmem] * 5,
-    )(ids, pick, weight, cotangent, home)
+        specs=[smem] + [vmem] * 5,
+    )(plane, ids, pick, weight, cotangent, home)
     summed, mixed, latent_gradient, gate_grad = lax.optimization_barrier(
         (summed, mixed, latent_gradient, gate_grad)
     )
@@ -256,12 +303,24 @@
     return (mixed, latent_gradient, gate_grad.T, gate_up_grad[None], down_grad[None])
 
 
-def exchange(message, columns):
-    rows, wide = message.shape
+def exchange(stay, right, left):
+    part, wide = stay.shape
+    columns = lax.axis_size("expert")
+    places = columns // RING
+    up = [(e, (e + places) % columns) for e in range(columns)]
+    down = [(e, (e - places) % columns) for e in range(columns)]
+    half = part // 2
+    one_right = lax.ppermute(right, "expert", up)
+    one_left = lax.ppermute(left, "expert", down)
+    two_right = lax.ppermute(one_right[part:], "expert", up)
+    two_left = lax.ppermute(one_left[:half], "expert", down)
+    pieces = [stay, one_right[:part], one_left[half:], jnp.concatenate([two_right, two_left], axis=0)]
+    merged = jnp.concatenate([piece.reshape(places, GROUP, wide) for piece in pieces], axis=1)
     moved = lax.all_to_all(
-        message.reshape(columns, rows // columns, wide), "expert", split_axis=0, concat_axis=0, tiled=True
-    )
-    return moved.reshape(rows, wide)
+        merged, "expert", split_axis=0, concat_axis=0, tiled=True,
+        axis_index_groups=[list(range(z * places, (z + 1) * places)) for z in range(RING)],
+    )
+    return moved.reshape(RING * part, wide)
 
 
 def solution(mesh):

time: 227 us -> 233 us (1.026)
  blocking collectives: 78.3 us -> 14.9 us
  starting transfers between devices: 36.3 us -> 87.8 us
  waiting for transfers between devices: 84.4 us -> 99 us
    ppermute x0 -> x8, starting transfers between devices: none -> 78.5 us  [the longest x2 29.1 us: exchange(): one_left = lax.ppermute(left, 'expert', down)]
    ppermute x0 -> x8, waiting for transfers between devices: none -> 72.8 us  [the longest x2 53 us: exchange(): one_left = lax.ppermute(left, 'expert', down)]
    all_to_all x1, blocking collectives: 78.3 us -> 14.9 us  [exchange(): lax.all_to_all(merged, 'expert', split_axis=0, concat_axis=0, tiled=True,...]
    all_to_all x1, waiting for transfers between devices: 53 us -> 9.07 us  [exchange(): lax.all_to_all(merged, 'expert', split_axis=0, concat_axis=0, tiled=True,...]
    all_to_all x1, starting transfers between devices: 34.4 us -> 7.35 us  [exchange(): lax.all_to_all(merged, 'expert', split_axis=0, concat_axis=0, tiled=True,...]
    reduce_scatter x1, waiting for transfers between devices: 29.4 us -> 15.4 us  [local(): lax.psum_scatter(pair.reshape(lat // 2, width), 'dp', scatter_dimension=0...]
  transfers between devices with their start and end apart: 3 -> 11, of which waited for: 3 -> 8; matrix products, arithmetic and copies ran while one was open for 0% -> 0% of each run, Pallas kernels for 2% -> 2%
where the time goes in v4:
time: 233 us; the launch traced here: 232 us
  waiting for transfers between devices  99 us (42%)
  starting transfers between devices  87.8 us (38%)
  blocking collectives  14.9 us (6%)
  between operations  14.2 us (6%)
  Pallas kernels  13.6 us (6%)
    ppermute x2, waiting for transfers between devices, exchange(): one_left = lax.ppermute(left, 'expert', down)  53 us
    ppermute x2, starting transfers between devices, exchange(): one_left = lax.ppermute(left, 'expert', down)  29.1 us
    ppermute x2, starting transfers between devices, exchange(): two_left = lax.ppermute(one_left[:half], 'expert', down)  20.1 us
    ppermute x2, waiting for transfers between devices, exchange(): two_right = lax.ppermute(one_right[part:], 'expert', up)  18.9 us
    ppermute x2, starting transfers between devices, exchange(): two_right = lax.ppermute(one_right[part:], 'expert', up)  18.6 us
    reduce_scatter x1, waiting for transfers between devices, local(): lax.psum_scatter(pair.reshape(lat // 2, width), 'dp', scatter_dimension=0...  15.4 us
    all_to_all x1, blocking collectives, exchange(): lax.all_to_all(merged, 'expert', split_axis=0, concat_axis=0, tiled=True,...  14.9 us
    ppermute x2, starting transfers between devices, exchange(): one_right = lax.ppermute(right, 'expert', up)  10.6 us
  transfers between devices with their start and end apart: 11, of which 8 were waited for; matrix products, arithmetic and copies ran while one was open for 0% of the time, Pallas kernels for 2%

profile of v4, /device:TPU:24, one launch (start us, length us, event | category | flops | bytes accessed | tf_op | source)
XLA Modules:
  0.0 232.3 jit_solution(17766506929561805545)
XLA Ops:
  7.2 2.8 %pack_kernel.1 = (bf16[128,512]{1,0:T(8,128)(2,1)}, bf16[192,512]{1,0:T(8,128)(2,1)}, bf16[192,512]{1,0:T(8,128)(2,1)}) custom-call(s32[1]{0:T(128)} %bitcast.6.plane_ref, s32[8,128]{1,0:T(8,128)} %bitcast.31, f32[8,128]{1,0:T(8,128)} %bitcast.34, bf16[128,1024]{1,0:T(8,128)(2,1)} %latent_hbm.1, bf16[128,1024]{1,0:T(8,128)(2,1)} %cot_ref.1), custom_call_target="tpu_custom_call" | custom-call | tf_op jit(solution)/shard_map/pack_kernel/pallas_call | solution.py:249
  10.0 23.0 %collective-permute-start.5 = (bf16[192,512]{1,0:T(8,128)(2,1)}, bf16[192,512]{1,0:T(8,128)(2,1)S(1)}, u32[]{:S(2)}, u32[]{:S(2)}) collective-permute-start(bf16[192,512]{1,0:T(8,128)(2,1)} %get-tuple-element.53), channel_id=1, source_target_pairs={{0,48},{1,49},{2,50},{3,51},{4,52},{5,53},{6,54},{7,55},{8,56},{9,... | collective-permute-start | bytes 589832 | tf_op jit(solution)/shard_map/ppermute | solution.py:314
  33.0 2.1 collective-permute-start.4
  35.1 33.6 %collective-permute-done.5 = bf16[192,512]{1,0:T(8,128)(2,1)S(1)} collective-permute-done((bf16[192,512]{1,0:T(8,128)(2,1)}, bf16[192,512]{1,0:T(8,128)(2,1)S(1)}, u32[]{:S(2)}, u32[]{:S(2)}) %collective-permute-start.5) | collective-permute-done | bytes 196640 | tf_op jit(solution)/shard_map/ppermute | solution.py:314
  68.7 13.1 %collective-permute-start.7 = (bf16[64,512]{1,0:T(8,128)(2,1)S(1)}, bf16[64,512]{1,0:T(8,128)(2,1)S(1)}, u32[]{:S(2)}, u32[]{:S(2)}) collective-permute-start(bf16[64,512]{1,0:T(8,128)(2,1)S(1)} %slice.35), channel_id=1, source_target_pairs={{0,48},{1,49},{2,50},{3,51},{4,52},{5,53},{6,54},{7,55},{8,56},{9,... | collective-permute-start | bytes 196616 | tf_op jit(solution)/shard_map/ppermute | solution.py:316
  81.8 1.9 collective-permute-start.6
  84.8 13.1 %collective-permute-done.6 = bf16[64,512]{1,0:T(8,128)(2,1)S(1)} collective-permute-done((bf16[64,512]{1,0:T(8,128)(2,1)S(1)}, bf16[64,512]{1,0:T(8,128)(2,1)S(1)}, u32[]{:S(2)}, u32[]{:S(2)}) %collective-permute-start.6) | collective-permute-done | bytes 65568 | tf_op jit(solution)/shard_map/ppermute | solution.py:315
  97.9 1.8 pad_maximum_fusion.2
  99.7 7.4 %all-to-all-start.1 = ((bf16[16,32,512]{2,1,0:T(8,128)(2,1)}), bf16[16,32,512]{2,1,0:T(8,128)(2,1)S(1)}, u32[]{:S(2)}, u32[]{:S(2)}) async-start(bf16[16,32,512]{2,1,0:T(8,128)(2,1)} %pad_maximum_fusion.2), calls=%async_computation.1 | async-start | bytes 1048576 | tf_op jit(solution)/shard_map/all_to_all | solution.py:319
  107.1 9.1 %all-to-all-done.1 = bf16[16,32,512]{2,1,0:T(8,128)(2,1)S(1)} async-done(((bf16[16,32,512]{2,1,0:T(8,128)(2,1)}), bf16[16,32,512]{2,1,0:T(8,128)(2,1)S(1)}, u32[]{:S(2)}, u32[]{:S(2)}) %all-to-all-start.1) | async-done | bytes 524320 | tf_op jit(solution)/shard_map/all_to_all | solution.py:319
  116.2 3.6 %expert_kernel.1 = (bf16[8,64,1536]{2,1,0:T(8,128)(2,1)S(1)}, bf16[8,64,1536]{2,1,0:T(8,128)(2,1)S(1)}, bf16[128,512]{1,0:T(8,128)(2,1)S(1)}, bf16[128,1024]{1,0:T(8,128)(2,1)S(1)}) custom-call(s32[1]{0:T(128)} %bitcast.5.core_ref, bf16[512,512]{1,0:T(8,128)(2,1)S(1)} %bitcast.30, bf16[1024,1024]{1,0:T(8,128)(2,1)} %bitcast.26, bf16[1024,512]{1,0:T(8,128)(2,1)S(1)} %bitcast.28), custom_call_target="tpu_custom_call" | custom-call | tf_op jit(solution)/shard_map/expert_kernel/pallas_call | solution.py:262
  119.8 1.9 collective-permute-start.8
  123.3 1.8 collective-permute-done.8.b_ref
  127.9 78.6 %conditional.1 = (bf16[512,512]{1,0:T(8,128)(2,1)S(1)}) conditional(s32[]{:T(128)} %convert_element_type.3, (bf16[128,512]{1,0:T(8,128)(2,1)S(1)}, bf16[192,512]{1,0:T(8,128)(2,1)S(1)}, bf16[192,512]{1,0:T(8,128)(2,1)S(1)}) %return_kernel.1, (bf16[128,512]{1,0:T(8,128)(2,1)S(1)}, bf16[192,512]{1,0:T(8,128)(2,1)S(1)}, ...), branch_computations={%region_1.2_spmd, %region_2.3_spmd} | conditional | flops 2359296 | bytes 5243048 | solution.py:279
  127.9 6.1 %collective-permute-start.1 = (bf16[192,512]{1,0:T(8,128)(2,1)S(1)}, bf16[192,512]{1,0:T(8,128)(2,1)S(1)}, u32[]{:S(2)}, u32[]{:S(2)}) collective-permute-start(bf16[192,512]{1,0:T(8,128)(2,1)S(1)} %get-tuple-element.20), channel_id=1, source_target_pairs={{0,48},{1,49},{2,50},{3,51},{4,52},{5,53},{6,54},{7,55},{8,56},{9,... | collective-permute-start | bytes 589832 | tf_op jit(solution)/shard_map/cond/branch_1_fun/ppermute | solution.py:314
  134.1 8.5 %collective-permute-start = (bf16[192,512]{1,0:T(8,128)(2,1)S(1)}, bf16[192,512]{1,0:T(8,128)(2,1)S(1)}, u32[]{:S(2)}, u32[]{:S(2)}) collective-permute-start(bf16[192,512]{1,0:T(8,128)(2,1)S(1)} %get-tuple-element.19), channel_id=1, source_target_pairs={{0,16},{1,17},{2,18},{3,19},{4,20},{5,21},{6,22},{7,23},{8,24},{9,... | collective-permute-start | bytes 589832 | tf_op jit(solution)/shard_map/cond/branch_1_fun/ppermute | solution.py:313
  142.6 19.3 %collective-permute-done.1 = bf16[192,512]{1,0:T(8,128)(2,1)S(1)} collective-permute-done((bf16[192,512]{1,0:T(8,128)(2,1)S(1)}, bf16[192,512]{1,0:T(8,128)(2,1)S(1)}, u32[]{:S(2)}, u32[]{:S(2)}) %collective-permute-start.1) | collective-permute-done | bytes 196640 | tf_op jit(solution)/shard_map/cond/branch_1_fun/ppermute | solution.py:314
  162.0 7.0 %collective-permute-start.3 = (bf16[64,512]{1,0:T(8,128)(2,1)S(1)}, bf16[64,512]{1,0:T(8,128)(2,1)S(1)}, u32[]{:S(2)}, u32[]{:S(2)}) collective-permute-start(bf16[64,512]{1,0:T(8,128)(2,1)S(1)} %slice.31), channel_id=1, source_target_pairs={{0,48},{1,49},{2,50},{3,51},{4,52},{5,53},{6,54},{7,55},{8,56},{9,... | collective-permute-start | bytes 196616 | tf_op jit(solution)/shard_map/cond/branch_1_fun/ppermute | solution.py:316
  169.0 16.7 %collective-permute-start.2 = (bf16[64,512]{1,0:T(8,128)(2,1)S(1)}, bf16[64,512]{1,0:T(8,128)(2,1)S(1)}, u32[]{:S(2)}, u32[]{:S(2)}) collective-permute-start(bf16[64,512]{1,0:T(8,128)(2,1)S(1)} %slice.30), channel_id=1, source_target_pairs={{0,16},{1,17},{2,18},{3,19},{4,20},{5,21},{6,22},{7,23},{8,24},{9,... | collective-permute-start | bytes 196616 | tf_op jit(solution)/shard_map/cond/branch_1_fun/ppermute | solution.py:315
  185.7 5.7 %collective-permute-done.2 = bf16[64,512]{1,0:T(8,128)(2,1)S(1)} collective-permute-done((bf16[64,512]{1,0:T(8,128)(2,1)S(1)}, bf16[64,512]{1,0:T(8,128)(2,1)S(1)}, u32[]{:S(2)}, u32[]{:S(2)}) %collective-permute-start.2) | collective-permute-done | bytes 65568 | tf_op jit(solution)/shard_map/cond/branch_1_fun/ppermute | solution.py:315
  191.5 14.9 %all_to_all.9 = bf16[16,32,512]{2,1,0:T(8,128)(2,1)S(1)} all-to-all(bf16[16,32,512]{2,1,0:T(8,128)(2,1)S(1)} %pad_maximum_fusion.1), channel_id=1, replica_groups={{0,1,2,3,4,5,6,7,8,9,10,11,12,13,14,15},{16,17,18,19,20,21,22,23,24,25,..., dimensions={0} | all-to-all | bytes 1048576 | tf_op jit(solution)/shard_map/cond/branch_1_fun/all_to_all | solution.py:319
  206.5 1.9 combine_kernel.1
  208.4 15.4 %reduce-scatter.2.cloned.1.call-done.sum_hbm = bf16[64,1536]{1,0:T(8,128)(2,1)} async-done(((bf16[512,1536]{1,0:T(8,128)(2,1)}), bf16[64,1536]{1,0:T(8,128)(2,1)}) %reduce-scatter.2.cloned.1.call-update) | async-done | bytes 196624 | tf_op jit(solution)/shard_map/reduce_scatter | solution.py:275
  223.8 1.6 split_kernel.1
  (30 shorter events, 5.5 us)
Async XLA Ops:
  10.0 58.7 %collective-permute-start.5 = (bf16[192,512]{1,0:T(8,128)(2,1)}, bf16[192,512]{1,0:T(8,128)(2,1)S(1)}, u32[]{:S(2)}, u32[]{:S(2)}) collective-permute-start(bf16[192,512]{1,0:T(8,128)(2,1)} %get-tuple-element.53), channel_id=1, source_target_pairs={{0,48},{1,49},{2,50},{3,51},{4,52},{5,53},{6,54},{7,55},{8,56},{9,... | collective-permute-start | bytes 589832 | tf_op jit(solution)/shard_map/ppermute | solution.py:314
  33.0 83.2 %copy-start.1 = (bf16[1,1024,512]{2,1,0:T(8,128)(2,1)S(1)}, bf16[1,1024,512]{2,1,0:T(8,128)(2,1)}, u32[]{:S(2)}) copy-start(bf16[1,1024,512]{2,1,0:T(8,128)(2,1)} %param.13) | copy-start | bytes 3145732
  33.0 48.8 %collective-permute-start.4 = (bf16[192,512]{1,0:T(8,128)(2,1)}, bf16[192,512]{1,0:T(8,128)(2,1)S(1)}, u32[]{:S(2)}, u32[]{:S(2)}) collective-permute-start(bf16[192,512]{1,0:T(8,128)(2,1)} %get-tuple-element.52), channel_id=1, source_target_pairs={{0,16},{1,17},{2,18},{3,19},{4,20},{5,21},{6,22},{7,23},{8,24},{9,... | collective-permute-start | bytes 589832 | tf_op jit(solution)/shard_map/ppermute | solution.py:313
  68.7 16.1 %collective-permute-start.7 = (bf16[64,512]{1,0:T(8,128)(2,1)S(1)}, bf16[64,512]{1,0:T(8,128)(2,1)S(1)}, u32[]{:S(2)}, u32[]{:S(2)}) collective-permute-start(bf16[64,512]{1,0:T(8,128)(2,1)S(1)} %slice.35), channel_id=1, source_target_pairs={{0,48},{1,49},{2,50},{3,51},{4,52},{5,53},{6,54},{7,55},{8,56},{9,... | collective-permute-start | bytes 196616 | tf_op jit(solution)/shard_map/ppermute | solution.py:316
  81.8 16.1 %collective-permute-start.6 = (bf16[64,512]{1,0:T(8,128)(2,1)S(1)}, bf16[64,512]{1,0:T(8,128)(2,1)S(1)}, u32[]{:S(2)}, u32[]{:S(2)}) collective-permute-start(bf16[64,512]{1,0:T(8,128)(2,1)S(1)} %slice.34), channel_id=1, source_target_pairs={{0,16},{1,17},{2,18},{3,19},{4,20},{5,21},{6,22},{7,23},{8,24},{9,... | collective-permute-start | bytes 196616 | tf_op jit(solution)/shard_map/ppermute | solution.py:315
  99.7 16.5 %all-to-all-start.1 = ((bf16[16,32,512]{2,1,0:T(8,128)(2,1)}), bf16[16,32,512]{2,1,0:T(8,128)(2,1)S(1)}, u32[]{:S(2)}, u32[]{:S(2)}) async-start(bf16[16,32,512]{2,1,0:T(8,128)(2,1)} %pad_maximum_fusion.2), calls=%async_computation.1 | async-start | bytes 1048576 | tf_op jit(solution)/shard_map/all_to_all | solution.py:319
  107.0 116.8 %reduce-scatter.2.cloned.1.call-start = ((), (), s32[]{:S(2)}) async-start(), calls=%async_computation.3 | async-start | bytes 1769472 | tf_op jit(solution)/shard_map/reduce_scatter | solution.py:275
  116.2 5.6 %copy-start = (bf16[1,1024,1024]{2,1,0:T(8,128)(2,1)S(1)}, bf16[1,1024,1024]{2,1,0:T(8,128)(2,1)}, u32[]{:S(2)}) copy-start(bf16[1,1024,1024]{2,1,0:T(8,128)(2,1)} %param.12) | copy-start | bytes 6291460
  119.8 5.3 %collective-permute-start.8 = (bf16[8,64,1536]{2,1,0:T(8,128)(2,1)S(1)}, bf16[8,64,1536]{2,1,0:T(8,128)(2,1)S(1)}, u32[]{:S(2)}, u32[]{:S(2)}) collective-permute-start(bf16[8,64,1536]{2,1,0:T(8,128)(2,1)S(1)} %get-tuple-element.55), channel_id=1, source_target_pairs={{0,64},{64,0},{128,192},{192,128},{256,320},{320,256},{384,448},{4... | collective-permute-start | bytes 4718600 | tf_op jit(solution)/shard_map/ppermute | solution.py:269
  126.6 0.7 copy-start.3
  126.6 0.7 copy-start.4
  127.9 78.6 %copy-start.2 = (bf16[128,1024]{1,0:T(8,128)(2,1)S(1)}, bf16[128,1024]{1,0:T(8,128)(2,1)}, u32[]{:S(2)}) copy-start(bf16[128,1024]{1,0:T(8,128)(2,1)} %cot_ref.1) | copy-start | bytes 786436
  127.9 34.1 %collective-permute-start.1 = (bf16[192,512]{1,0:T(8,128)(2,1)S(1)}, bf16[192,512]{1,0:T(8,128)(2,1)S(1)}, u32[]{:S(2)}, u32[]{:S(2)}) collective-permute-start(bf16[192,512]{1,0:T(8,128)(2,1)S(1)} %get-tuple-element.20), channel_id=1, source_target_pairs={{0,48},{1,49},{2,50},{3,51},{4,52},{5,53},{6,54},{7,55},{8,56},{9,... | collective-permute-start | bytes 589832 | tf_op jit(solution)/shard_map/cond/branch_1_fun/ppermute | solution.py:314
  134.1 34.9 %collective-permute-start = (bf16[192,512]{1,0:T(8,128)(2,1)S(1)}, bf16[192,512]{1,0:T(8,128)(2,1)S(1)}, u32[]{:S(2)}, u32[]{:S(2)}) collective-permute-start(bf16[192,512]{1,0:T(8,128)(2,1)S(1)} %get-tuple-element.19), channel_id=1, source_target_pairs={{0,16},{1,17},{2,18},{3,19},{4,20},{5,21},{6,22},{7,23},{8,24},{9,... | collective-permute-start | bytes 589832 | tf_op jit(solution)/shard_map/cond/branch_1_fun/ppermute | solution.py:313
  162.0 23.8 %collective-permute-start.3 = (bf16[64,512]{1,0:T(8,128)(2,1)S(1)}, bf16[64,512]{1,0:T(8,128)(2,1)S(1)}, u32[]{:S(2)}, u32[]{:S(2)}) collective-permute-start(bf16[64,512]{1,0:T(8,128)(2,1)S(1)} %slice.31), channel_id=1, source_target_pairs={{0,48},{1,49},{2,50},{3,51},{4,52},{5,53},{6,54},{7,55},{8,56},{9,... | collective-permute-start | bytes 196616 | tf_op jit(solution)/shard_map/cond/branch_1_fun/ppermute | solution.py:316
  169.0 22.5 %collective-permute-start.2 = (bf16[64,512]{1,0:T(8,128)(2,1)S(1)}, bf16[64,512]{1,0:T(8,128)(2,1)S(1)}, u32[]{:S(2)}, u32[]{:S(2)}) collective-permute-start(bf16[64,512]{1,0:T(8,128)(2,1)S(1)} %slice.30), channel_id=1, source_target_pairs={{0,16},{1,17},{2,18},{3,19},{4,20},{5,21},{6,22},{7,23},{8,24},{9,... | collective-permute-start | bytes 196616 | tf_op jit(solution)/shard_map/cond/branch_1_fun/ppermute | solution.py:315
Sparse Core Ops, SparseCore 0:
  126.8 96.9 reduce-scatter.1

commit v5 on v4

--- a/solution.py
+++ b/solution.py
@@ -39,8 +39,8 @@
     return step, row // (GROUP * RING)
 
 
-def expert_id(step, place, plane, rows):
-    return (((plane + step) % RING) * (rows // (GROUP * RING)) + place) * EXP_DEV
+def block_index(step, place, plane, rows):
+    return ((plane + step) % RING) * (rows // (GROUP * RING)) + place
 
 
 def routing(ids_ref, probs_ref, expert):
@@ -73,20 +73,15 @@
     left_ref[...] = message[middle:]
 
 
-def pack_kernel(
-    plane_ref, ids_hbm, probs_hbm, latent_hbm, cot_hbm, stay_ref, right_ref, left_ref,
-    ids_ref, probs_ref, latent_ref, cot_ref, sems
-):
-    part, wide = stay_ref.shape
-    rows = RING * part
+def pack_kernel(ids_hbm, probs_hbm, latent_hbm, cot_hbm, sent_ref, ids_ref, probs_ref, latent_ref, cot_ref, sems):
+    rows, wide = sent_ref.shape
     pairs = [(ids_hbm, ids_ref), (probs_hbm, probs_ref), (latent_hbm, latent_ref), (cot_hbm, cot_ref)]
     copies = [pltpu.make_async_copy(a, b, sems.at[i]) for i, (a, b) in enumerate(pairs)]
     for copy in copies:
         copy.start()
     copies[0].wait()
     copies[1].wait()
-    step, place = leaving(iota((rows, ids_ref.shape[1]), 0), rows)
-    expert = expert_id(step, place, plane_ref[0], rows)
+    expert = iota((rows, ids_ref.shape[1]), 0) // GROUP * EXP_DEV
     pick, gate, first, low = routing(ids_ref, probs_ref, expert)
     token = jnp.where(pick & first, 1.0, 0.0)
     weight = jnp.where(pick & ~first, gate, 0.0)
@@ -100,7 +95,7 @@
         cols = pl.ds(h * wide, wide)
         cot = cot_ref[:, cols]
         total = total + mm(picks, jnp.concatenate([latent_ref[:, cols], cot, cot], axis=0))
-    store_leaving(total.astype(BF16), stay_ref, right_ref, left_ref)
+    sent_ref[...] = total.astype(BF16)
 
 
 def sorted_position(index, slots):
@@ -144,7 +139,7 @@
         other_ref[block] = jnp.where(even, b, a)
 
 
-def return_kernel(act_ref, grad_ref, win_ref, wout_ref, stay_ref, right_ref, left_ref):
+def return_kernel(plane_ref, act_ref, grad_ref, win_ref, wout_ref, stay_ref, right_ref, left_ref):
     part, wide = stay_ref.shape
     rows = RING * part
     slots = rows // 4
@@ -158,8 +153,7 @@
     )
     row = iota((rows, rows), 0)
     step, place = leaving(row, rows)
-    piece = jnp.where(step == 0, 0, jnp.where(step == RING - 1, 1, step + 1))
-    source = (place * RING + piece) * GROUP + row % GROUP
+    source = block_index(step, place, plane_ref[0], rows) * GROUP + row % GROUP
     unsort = zero_one(iota((rows, rows), 1) == sorted_position(source, slots))
     store_leaving(mm(unsort, result).astype(BF16), stay_ref, right_ref, left_ref)
 
@@ -182,7 +176,7 @@
 
 def mask_kernel(plane_ref, ids_ref, probs_ref, pick_ref, weight_ref):
     step, place = arriving(iota(weight_ref.shape, 0))
-    expert = expert_id(step, place, plane_ref[0], weight_ref.shape[0])
+    expert = block_index(step, place, plane_ref[0], weight_ref.shape[0]) * EXP_DEV
     pick, gate, first, _ = routing(ids_ref, probs_ref, expert)
     pick_ref[...] = zero_one(pick)
     weight_ref[...] = jnp.where(pick & first, gate, 0.0)
@@ -194,7 +188,7 @@
     pick = pick_ref[...].astype(F32)
     row = iota(weight.shape, 0)
     step, place = arriving(row)
-    expert = expert_id(step, place, plane_ref[0], rows)
+    expert = block_index(step, place, plane_ref[0], rows) * EXP_DEV
     first = (row & 2) == 0
     low = (row & 4) == 0
     home = home_ref[...]
@@ -246,15 +240,17 @@
     part = rows // RING
     leave = [((part, wide), BF16), ((part + part // 2, wide), BF16), ((part + part // 2, wide), BF16)]
 
-    sent = call(
+    (sent,) = call(
         pack_kernel,
-        leave,
+        [((rows, wide), BF16)],
         scratch=[pltpu.VMEM(a.shape, a.dtype) for a in (ids, probs, latent, cotangent)]
         + [pltpu.SemaphoreType.DMA((4,))],
-        specs=[smem] + [pl.BlockSpec(memory_space=pl.ANY)] * 4,
+        specs=[pl.BlockSpec(memory_space=pl.ANY)] * 4,
         vmem=ALL_VMEM_BYTES,
-    )(plane, ids, probs, latent, cotangent)
-    there = exchange(*sent)
+    )(ids, probs, latent, cotangent)
+    there = lax.all_to_all(
+        sent.reshape(columns, GROUP, wide), "expert", split_axis=0, concat_axis=0, tiled=True
+    ).reshape(rows, wide)
 
     core = (lax.axis_index("dp") % 2).astype(jnp.int32).reshape(1)
     half_terms = ((replicas // 2, share, width), BF16)
@@ -267,8 +263,8 @@
     )(core, there, w_gate_up[0], w_down[0])
 
     swapped = lax.ppermute(other, "dp", [(i, i ^ 1) for i in range(replicas)])
-    back = call(return_kernel, leave, specs=[vmem] * 4)(
-        act, grad_hidden, w_gate_up[0], w_down[0]
+    back = call(return_kernel, leave, specs=[smem] + [vmem] * 4)(
+        plane, act, grad_hidden, w_gate_up[0], w_down[0]
     )
     (pair,) = call(add_kernel, [half_terms], specs=[vmem] * 2)(mine, swapped)
     pair, *back = lax.optimization_barrier((pair, *back))

time: 233 us -> 231 us (level)
  the two profiles are of different devices: /device:TPU:24 before, /device:TPU:96 now
where the time goes in v5:
time: 231 us; the launch traced here: 230 us
  waiting for transfers between devices  113 us (49%)
  starting transfers between devices  64.2 us (28%)
  blocking collectives  17.8 us (8%)
  Pallas kernels  17 us (7%)
  between operations  14.2 us (6%)
  local copies, waits for them, and re-layouts  3.75 us (2%)
    all_to_all x1, waiting for transfers between devices, local(): lax.all_to_all(sent.reshape(columns, GROUP, wide), 'expert', split_axis=0...  63.9 us
    ppermute x1, waiting for transfers between devices, exchange(): one_left = lax.ppermute(left, 'expert', down)  34.4 us
    all_to_all x1, starting transfers between devices, local(): lax.all_to_all(sent.reshape(columns, GROUP, wide), 'expert', split_axis=0...  31.9 us
    all_to_all x1, blocking collectives, exchange(): lax.all_to_all(merged, 'expert', split_axis=0, concat_axis=0, tiled=True,...  17.8 us
    ppermute x1, waiting for transfers between devices, exchange(): two_right = lax.ppermute(one_right[part:], 'expert', up)  13.6 us
    ppermute x1, starting transfers between devices, exchange(): one_right = lax.ppermute(right, 'expert', up)  12.6 us
    ppermute x1, starting transfers between devices, exchange(): two_left = lax.ppermute(one_left[:half], 'expert', down)  10.4 us
    ppermute x1, starting transfers between devices, exchange(): two_right = lax.ppermute(one_right[part:], 'expert', up)  5.23 us
  transfers between devices with their start and end apart: 7, of which 4 were waited for; matrix products, arithmetic and copies ran while one was open for 0% of the time, Pallas kernels for 2%

profile of v5, /device:TPU:96, one launch (start us, length us, event | category | flops | bytes accessed | tf_op | source)
XLA Modules:
  0.0 230.3 jit_solution(11709860611784490393)
XLA Ops:
  7.2 2.8 %pack_kernel.1 = bf16[512,512]{1,0:T(8,128)(2,1)} custom-call(s32[8,128]{1,0:T(8,128)} %bitcast.25, f32[8,128]{1,0:T(8,128)} %bitcast.28, bf16[128,1024]{1,0:T(8,128)(2,1)} %latent_hbm.1, bf16[128,1024]{1,0:T(8,128)(2,1)} %cot_ref.1), custom_call_target="tpu_custom_call" | custom-call | tf_op jit(solution)/shard_map/pack_kernel/pallas_call | solution.py:243
  10.0 31.9 %all-to-all-start.1 = ((bf16[64,8,512]{2,1,0:T(8,128)(2,1)}), bf16[64,8,512]{2,1,0:T(8,128)(2,1)S(1)}, u32[]{:S(2)}, u32[]{:S(2)}) async-start(bf16[64,8,512]{2,1,0:T(8,128)(2,1)} %bitcast.30), calls=%async_computation.1 | async-start | bytes 1048576 | tf_op jit(solution)/shard_map/all_to_all | solution.py:251
  41.9 0.0 reduce-scatter.2.cloned.1.call-start
  41.9 63.9 %all-to-all-done.1 = bf16[64,8,512]{2,1,0:T(8,128)(2,1)S(1)} async-done(((bf16[64,8,512]{2,1,0:T(8,128)(2,1)}), bf16[64,8,512]{2,1,0:T(8,128)(2,1)S(1)}, u32[]{:S(2)}, u32[]{:S(2)}) %all-to-all-start.1) | async-done | bytes 524320 | tf_op jit(solution)/shard_map/all_to_all | solution.py:251
  105.8 0.8 copy-done.2
  106.7 1.0 copy-done.3
  107.7 4.8 %expert_kernel.1 = (bf16[8,64,1536]{2,1,0:T(8,128)(2,1)S(1)}, bf16[8,64,1536]{2,1,0:T(8,128)(2,1)}, bf16[128,512]{1,0:T(8,128)(2,1)S(1)}, bf16[128,1024]{1,0:T(8,128)(2,1)S(1)}) custom-call(s32[1]{0:T(128)} %bitcast.5.core_ref, bf16[512,512]{1,0:T(8,128)(2,1)S(1)} %bitcast.24, bf16[1024,1024]{1,0:T(8,128)(2,1)} %bitcast.20, bf16[1024,512]{1,0:T(8,128)(2,1)S(1)} %bitcast.22), custom_call_target="tpu_custom_call" | custom-call | tf_op jit(solution)/shard_map/expert_kernel/pallas_call | solution.py:258
  112.5 1.2 copy-done.4
  113.7 1.9 collective-permute-start.4
  115.6 2.4 %return_kernel.1 = (bf16[128,512]{1,0:T(8,128)(2,1)}, bf16[192,512]{1,0:T(8,128)(2,1)}, bf16[192,512]{1,0:T(8,128)(2,1)}) custom-call(s32[1]{0:T(128)} %bitcast.12.plane_ref, bf16[128,512]{1,0:T(8,128)(2,1)S(1)} %get-tuple-element.50.act_ref, bf16[128,1024]{1,0:T(8,128)(2,1)S(1)} %get-tuple-element.51.grad_ref, bf16[1024,1024]{1,0:T(8,128)(2,1)S(1)} %bitcast.21, ...), custom_call_target="tpu_custom_call" | custom-call | tf_op jit(solution)/shard_map/return_kernel/pallas_call | solution.py:266
  118.0 1.3 collective-permute-done.4.b_ref
  119.3 2.9 %add_kernel.1 = bf16[8,64,1536]{2,1,0:T(8,128)(2,1)} custom-call(bf16[8,64,1536]{2,1,0:T(8,128)(2,1)S(1)} %copy-done.5, bf16[8,64,1536]{2,1,0:T(8,128)(2,1)} %collective-permute-done.4.b_ref), custom_call_target="tpu_custom_call" | custom-call | tf_op jit(solution)/shard_map/add_kernel/pallas_call | solution.py:269
  122.3 0.6 copy-done.7
  122.9 0.5 mask_kernel.1
  123.5 96.4 %conditional.1 = (bf16[512,512]{1,0:T(8,128)(2,1)S(1)}) conditional(s32[]{:T(128)} %convert_element_type.3, (bf16[128,512]{1,0:T(8,128)(2,1)S(1)}, bf16[192,512]{1,0:T(8,128)(2,1)S(1)}, bf16[192,512]{1,0:T(8,128)(2,1)S(1)}) %tuple.28, (bf16[128,512]{1,0:T(8,128)(2,1)S(1)}, bf16[192,512]{1,0:T(8,128)(2,1)S(1)}, bf16[192,512]{1,0:T(8,128)(2,1)S(1)}) %tuple.29), branch_computations={%region_1.2_spmd, %region_2.3_spmd} | conditional | flops 2359296 | bytes 5243048 | solution.py:275
  123.5 2.1 collective-permute-start.1
  125.6 12.6 %collective-permute-start = (bf16[192,512]{1,0:T(8,128)(2,1)S(1)}, bf16[192,512]{1,0:T(8,128)(2,1)S(1)}, u32[]{:S(2)}, u32[]{:S(2)}) collective-permute-start(bf16[192,512]{1,0:T(8,128)(2,1)S(1)} %get-tuple-element.19), channel_id=1, source_target_pairs={{0,16},{1,17},{2,18},{3,19},{4,20},{5,21},{6,22},{7,23},{8,24},{9,... | collective-permute-start | bytes 589832 | tf_op jit(solution)/shard_map/cond/branch_1_fun/ppermute | solution.py:309
  138.2 34.4 %collective-permute-done.1 = bf16[192,512]{1,0:T(8,128)(2,1)S(1)} collective-permute-done((bf16[192,512]{1,0:T(8,128)(2,1)S(1)}, bf16[192,512]{1,0:T(8,128)(2,1)S(1)}, u32[]{:S(2)}, u32[]{:S(2)}) %collective-permute-start.1) | collective-permute-done | bytes 196640 | tf_op jit(solution)/shard_map/cond/branch_1_fun/ppermute | solution.py:310
  172.7 10.4 %collective-permute-start.3 = (bf16[64,512]{1,0:T(8,128)(2,1)S(1)}, bf16[64,512]{1,0:T(8,128)(2,1)S(1)}, u32[]{:S(2)}, u32[]{:S(2)}) collective-permute-start(bf16[64,512]{1,0:T(8,128)(2,1)S(1)} %slice.15), channel_id=1, source_target_pairs={{0,48},{1,49},{2,50},{3,51},{4,52},{5,53},{6,54},{7,55},{8,56},{9,... | collective-permute-start | bytes 196616 | tf_op jit(solution)/shard_map/cond/branch_1_fun/ppermute | solution.py:312
  183.1 5.2 %collective-permute-start.2 = (bf16[64,512]{1,0:T(8,128)(2,1)S(1)}, bf16[64,512]{1,0:T(8,128)(2,1)S(1)}, u32[]{:S(2)}, u32[]{:S(2)}) collective-permute-start(bf16[64,512]{1,0:T(8,128)(2,1)S(1)} %slice.14), channel_id=1, source_target_pairs={{0,16},{1,17},{2,18},{3,19},{4,20},{5,21},{6,22},{7,23},{8,24},{9,... | collective-permute-start | bytes 196616 | tf_op jit(solution)/shard_map/cond/branch_1_fun/ppermute | solution.py:311
  188.4 13.6 %collective-permute-done.2 = bf16[64,512]{1,0:T(8,128)(2,1)S(1)} collective-permute-done((bf16[64,512]{1,0:T(8,128)(2,1)S(1)}, bf16[64,512]{1,0:T(8,128)(2,1)S(1)}, u32[]{:S(2)}, u32[]{:S(2)}) %collective-permute-start.2) | collective-permute-done | bytes 65568 | tf_op jit(solution)/shard_map/cond/branch_1_fun/ppermute | solution.py:311
  202.1 17.8 %all_to_all.9 = bf16[16,32,512]{2,1,0:T(8,128)(2,1)S(1)} all-to-all(bf16[16,32,512]{2,1,0:T(8,128)(2,1)S(1)} %pad_maximum_fusion.1), channel_id=1, replica_groups={{0,1,2,3,4,5,6,7,8,9,10,11,12,13,14,15},{16,17,18,19,20,21,22,23,24,25,..., dimensions={0} | all-to-all | bytes 1048576 | tf_op jit(solution)/shard_map/cond/branch_1_fun/all_to_all | solution.py:315
  219.9 1.9 combine_kernel.1
  221.8 1.6 split_kernel.1
  (30 shorter events, 0.2 us)
Async XLA Ops:
  10.0 96.7 %copy-start.1 = (bf16[1,1024,512]{2,1,0:T(8,128)(2,1)S(1)}, bf16[1,1024,512]{2,1,0:T(8,128)(2,1)}, u32[]{:S(2)}) copy-start(bf16[1,1024,512]{2,1,0:T(8,128)(2,1)} %param.13) | copy-start | bytes 3145732
  10.0 95.8 %all-to-all-start.1 = ((bf16[64,8,512]{2,1,0:T(8,128)(2,1)}), bf16[64,8,512]{2,1,0:T(8,128)(2,1)S(1)}, u32[]{:S(2)}, u32[]{:S(2)}) async-start(bf16[64,8,512]{2,1,0:T(8,128)(2,1)} %bitcast.30), calls=%async_computation.1 | async-start | bytes 1048576 | tf_op jit(solution)/shard_map/all_to_all | solution.py:251
  41.9 179.9 %reduce-scatter.2.cloned.1.call-start = ((), (), s32[]{:S(2)}) async-start(), calls=%async_computation.3 | async-start | bytes 1769472 | tf_op jit(solution)/shard_map/reduce_scatter | solution.py:271
  105.8 0.8 copy-start.2
  106.7 1.0 copy-start.3
  107.7 7.9 %copy-start = (bf16[1,1024,1024]{2,1,0:T(8,128)(2,1)S(1)}, bf16[1,1024,1024]{2,1,0:T(8,128)(2,1)}, u32[]{:S(2)}) copy-start(bf16[1,1024,1024]{2,1,0:T(8,128)(2,1)} %param.12) | copy-start | bytes 6291460
  112.5 1.2 copy-start.4
  113.7 5.6 %collective-permute-start.4 = (bf16[8,64,1536]{2,1,0:T(8,128)(2,1)}, bf16[8,64,1536]{2,1,0:T(8,128)(2,1)}, u32[]{:S(2)}, u32[]{:S(2)}) collective-permute-start(bf16[8,64,1536]{2,1,0:T(8,128)(2,1)} %get-tuple-element.49), channel_id=1, source_target_pairs={{0,64},{64,0},{128,192},{192,128},{256,320},{320,256},{384,448},{4... | collective-permute-start | bytes 4718600 | tf_op jit(solution)/shard_map/ppermute | solution.py:265
  115.6 3.7 %copy-start.5 = (bf16[8,64,1536]{2,1,0:T(8,128)(2,1)S(1)}, bf16[8,64,1536]{2,1,0:T(8,128)(2,1)}, u32[]{:S(2)}) copy-start(bf16[8,64,1536]{2,1,0:T(8,128)(2,1)} %copy-done.4) | copy-start | bytes 4718596
  122.2 0.7 copy-start.7
  122.2 0.7 copy-start.8
  122.2 1.2 copy-start.9
  122.2 1.3 copy-start.10
  122.2 1.3 copy-start.11
  123.5 96.4 %copy-start.6 = (bf16[128,1024]{1,0:T(8,128)(2,1)S(1)}, bf16[128,1024]{1,0:T(8,128)(2,1)}, u32[]{:S(2)}) copy-start(bf16[128,1024]{1,0:T(8,128)(2,1)} %cot_ref.1) | copy-start | bytes 786436
  123.5 49.1 %collective-permute-start.1 = (bf16[192,512]{1,0:T(8,128)(2,1)S(1)}, bf16[192,512]{1,0:T(8,128)(2,1)S(1)}, u32[]{:S(2)}, u32[]{:S(2)}) collective-permute-start(bf16[192,512]{1,0:T(8,128)(2,1)S(1)} %get-tuple-element.20), channel_id=1, source_target_pairs={{0,48},{1,49},{2,50},{3,51},{4,52},{5,53},{6,54},{7,55},{8,56},{9,... | collective-permute-start | bytes 589832 | tf_op jit(solution)/shard_map/cond/branch_1_fun/ppermute | solution.py:310
  125.6 57.5 %collective-permute-start = (bf16[192,512]{1,0:T(8,128)(2,1)S(1)}, bf16[192,512]{1,0:T(8,128)(2,1)S(1)}, u32[]{:S(2)}, u32[]{:S(2)}) collective-permute-start(bf16[192,512]{1,0:T(8,128)(2,1)S(1)} %get-tuple-element.19), channel_id=1, source_target_pairs={{0,16},{1,17},{2,18},{3,19},{4,20},{5,21},{6,22},{7,23},{8,24},{9,... | collective-permute-start | bytes 589832 | tf_op jit(solution)/shard_map/cond/branch_1_fun/ppermute | solution.py:309
  172.7 15.7 %collective-permute-start.3 = (bf16[64,512]{1,0:T(8,128)(2,1)S(1)}, bf16[64,512]{1,0:T(8,128)(2,1)S(1)}, u32[]{:S(2)}, u32[]{:S(2)}) collective-permute-start(bf16[64,512]{1,0:T(8,128)(2,1)S(1)} %slice.15), channel_id=1, source_target_pairs={{0,48},{1,49},{2,50},{3,51},{4,52},{5,53},{6,54},{7,55},{8,56},{9,... | collective-permute-start | bytes 196616 | tf_op jit(solution)/shard_map/cond/branch_1_fun/ppermute | solution.py:312
  183.1 18.9 %collective-permute-start.2 = (bf16[64,512]{1,0:T(8,128)(2,1)S(1)}, bf16[64,512]{1,0:T(8,128)(2,1)S(1)}, u32[]{:S(2)}, u32[]{:S(2)}) collective-permute-start(bf16[64,512]{1,0:T(8,128)(2,1)S(1)} %slice.14), channel_id=1, source_target_pairs={{0,16},{1,17},{2,18},{3,19},{4,20},{5,21},{6,22},{7,23},{8,24},{9,... | collective-permute-start | bytes 196616 | tf_op jit(solution)/shard_map/cond/branch_1_fun/ppermute | solution.py:311
Sparse Core Ops, SparseCore 0:
  122.4 81.4 reduce-scatter.1

commit v6 on v3

--- a/solution.py
+++ b/solution.py
@@ -130,20 +130,18 @@
     back_ref[...] = mm(unsort, result).astype(BF16)
 
 
-def split_kernel(sum_hbm, gate_up_ref, down_ref, sems):
+def add_kernel(bit_ref, a_ref, b_ref, out_ref):
+    bit = bit_ref[0]
+    for block in range(out_ref.shape[0]):
+        index = 2 * block + bit
+        out_ref[block] = (a_ref[index].astype(F32) + b_ref[index].astype(F32)).astype(BF16)
+
+
+def last_add_kernel(a_ref, b_ref, gate_up_ref, down_ref):
     cut = gate_up_ref.shape[1]
-    copies = [
-        pltpu.make_async_copy(sum_hbm.at[:, pl.ds(0, cut)], gate_up_ref, sems.at[0]),
-        pltpu.make_async_copy(sum_hbm.at[:, pl.ds(cut, down_ref.shape[1])], down_ref, sems.at[1]),
-    ]
-    for copy in copies:
-        copy.start()
-    for copy in copies:
-        copy.wait()
-
-
-def add_kernel(a_ref, b_ref, out_ref):
-    out_ref[...] = (a_ref[...].astype(F32) + b_ref[...].astype(F32)).astype(BF16)
+    total = (a_ref[0].astype(F32) + b_ref[0].astype(F32)).astype(BF16)
+    gate_up_ref[...] = total[:, :cut]
+    down_ref[...] = total[:, cut:]
 
 
 def mask_kernel(ids_ref, probs_ref, pick_ref, weight_ref):
@@ -203,6 +201,7 @@
     ids = expert_ids.T
     probs = gate_probs.T
     vmem = pl.BlockSpec(memory_space=pltpu.VMEM)
+    smem = pl.BlockSpec(memory_space=pltpu.SMEM)
 
     (sent,) = call(
         pack_kernel,
@@ -221,20 +220,32 @@
         expert_kernel,
         [half_terms, half_terms, ((slots, ffw), BF16), ((slots, 2 * ffw), BF16)],
         scratch=[pltpu.VMEM((lat, width), BF16)],
-        specs=[pl.BlockSpec(memory_space=pltpu.SMEM)] + [vmem] * 3,
+        specs=[smem] + [vmem] * 3,
     )(core, there, w_gate_up[0], w_down[0])
 
-    swapped = lax.ppermute(other, "dp", [(i, i ^ 1) for i in range(replicas)])
+    position = lax.axis_index("dp") // 2
+    chips = replicas // 2
+    arrived = lax.ppermute(other, "dp", [(i, i ^ 1) for i in range(replicas)])
+    kept = mine
     (back,) = call(return_kernel, [((rows, wide), BF16)], specs=[vmem] * 4)(
         act, grad_hidden, w_gate_up[0], w_down[0]
     )
-    (pair,) = call(add_kernel, [half_terms], specs=[vmem] * 2)(mine, swapped)
-    pair, back = lax.optimization_barrier((pair, back))
-    summed = lax.psum_scatter(
-        pair.reshape(lat // 2, width), "dp", scatter_dimension=0, tiled=True,
-        axis_index_groups=[list(range(c, replicas, 2)) for c in range(2)],
-    )
-    home = lax.cond(core[0] < 2, lambda b: exchange(b, columns), lambda b: b, back)
+    home = None
+    distance = 1
+    while distance < chips:
+        blocks = ((chips // (2 * distance), share, width), BF16)
+        bit = (position // distance % 2).astype(jnp.int32).reshape(1)
+        (send,) = call(add_kernel, [blocks], specs=[smem] + [vmem] * 2)(1 - bit, kept, arrived)
+        moving = lax.ppermute(send, "dp", [(i, i ^ (2 * distance)) for i in range(replicas)])
+        kept, send = lax.optimization_barrier((kept, send))
+        (kept,) = call(add_kernel, [blocks], specs=[smem] + [vmem] * 2)(bit, kept, arrived)
+        arrived = moving
+        if home is None:
+            kept, back = lax.optimization_barrier((kept, back))
+            home = exchange(back, columns)
+        distance *= 2
+    if home is None:
+        home = exchange(back, columns)
     pick, weight = call(
         mask_kernel, [((rows, tokens), BF16), ((rows, tokens), F32)], specs=[vmem] * 2
     )(ids, probs)
@@ -243,16 +254,9 @@
         [((tokens, lat), BF16), ((tokens, lat), BF16), ((top, tokens), F32)],
         specs=[vmem] * 5,
     )(ids, pick, weight, cotangent, home)
-    summed, mixed, latent_gradient, gate_grad = lax.optimization_barrier(
-        (summed, mixed, latent_gradient, gate_grad)
-    )
     gate_up_grad, down_grad = call(
-        split_kernel,
-        [((share, 2 * ffw), BF16), ((share, ffw), BF16)],
-        scratch=[pltpu.SemaphoreType.DMA((2,))],
-        specs=[pl.BlockSpec(memory_space=pl.ANY)],
-        vmem=ALL_VMEM_BYTES,
-    )(summed)
+        last_add_kernel, [((share, 2 * ffw), BF16), ((share, ffw), BF16)], specs=[vmem] * 2
+    )(kept, arrived)
     return (mixed, latent_gradient, gate_grad.T, gate_up_grad[None], down_grad[None])
 
 

time: 227 us -> 239 us (1.053); the launches traced: 227 us -> 236 us
  blocking collectives: 78.3 us -> 0 us
  waiting for transfers between devices: 84.4 us -> 151 us
  starting transfers between devices: 36.3 us -> 65 us
  between operations: 14.1 us -> 0.91 us
  Pallas kernels: 13.3 us -> 16.3 us
    ppermute x1 -> x4, waiting for transfers between devices: 1.93 us -> 98.1 us  [the longest x3 96.7 us: local(): lax.ppermute(send, 'dp', [(i, i ^ 2 * distance) for i in range(replicas)])]
    all_to_all x1 -> x0, blocking collectives: 78.3 us -> none  [exchange(): lax.all_to_all(message.reshape(columns, rows // columns, wide), 'expert',...]
    reduce_scatter x1 -> x0, waiting for transfers between devices: 29.4 us -> none  [local(): lax.psum_scatter(pair.reshape(lat // 2, width), 'dp', scatter_dimension=0...]
    all_to_all x1 -> x2, starting transfers between devices: 34.4 us -> 55.2 us  [exchange(): lax.all_to_all(message.reshape(columns, rows // columns, wide), 'expert',...]
    ppermute x1 -> x4, starting transfers between devices: 1.92 us -> 9.82 us  [the longest x3 7.91 us: local(): lax.ppermute(send, 'dp', [(i, i ^ 2 * distance) for i in range(replicas)])]
    all_to_all x1 -> x2, waiting for transfers between devices: 53 us -> 53.1 us  [exchange(): lax.all_to_all(message.reshape(columns, rows // columns, wide), 'expert',...]
  transfers between devices with their start and end apart: 3 -> 6, of which waited for: 3 -> 5; matrix products, arithmetic and copies ran while one was open for 0% -> 0% of each run, Pallas kernels for 2% -> 2%
where the time goes in v6:
time: 239 us; the launch traced here: 236 us
  waiting for transfers between devices  151 us (63%)
  starting transfers between devices  65 us (27%)
  Pallas kernels  16.3 us (7%)
  local copies, waits for them, and re-layouts  3.01 us (1%)
    ppermute x3, waiting for transfers between devices, local(): lax.ppermute(send, 'dp', [(i, i ^ 2 * distance) for i in range(replicas)])  96.7 us
    all_to_all x2, starting transfers between devices, exchange(): lax.all_to_all(message.reshape(columns, rows // columns, wide), 'expert',...  55.2 us
    all_to_all x2, waiting for transfers between devices, exchange(): lax.all_to_all(message.reshape(columns, rows // columns, wide), 'expert',...  53.1 us
    ppermute x3, starting transfers between devices, local(): lax.ppermute(send, 'dp', [(i, i ^ 2 * distance) for i in range(replicas)])  7.91 us
    pallas_call x1, Pallas kernels, local(): call(expert_kernel, [half_terms, half_terms, ((slots, ffw), BF16), ((slot...  4.81 us
  transfers between devices with their start and end apart: 6, of which 5 were waited for; matrix products, arithmetic and copies ran while one was open for 0% of the time, Pallas kernels for 2%

profile of v6, /device:TPU:24, one launch (start us, length us, event | category | flops | bytes accessed | tf_op | source)
XLA Modules:
  0.0 236.5 jit_solution(2809949843686444515)
XLA Ops:
  0.6 2.8 %pack_kernel.1 = bf16[512,512]{1,0:T(8,128)(2,1)} custom-call(s32[8,128]{1,0:T(8,128)} %bitcast.21, f32[8,128]{1,0:T(8,128)} %bitcast.24, bf16[128,1024]{1,0:T(8,128)(2,1)} %latent_hbm.1, bf16[128,1024]{1,0:T(8,128)(2,1)} %cot_ref.1), custom_call_target="tpu_custom_call" | custom-call | tf_op jit(solution)/shard_map/pack_kernel/pallas_call | solution.py:206
  3.4 34.4 %all-to-all-start = ((bf16[64,8,512]{2,1,0:T(8,128)(2,1)}), bf16[64,8,512]{2,1,0:T(8,128)(2,1)S(1)}, u32[]{:S(2)}, u32[]{:S(2)}) async-start(bf16[64,8,512]{2,1,0:T(8,128)(2,1)} %bitcast.26), calls=%async_computation | async-start | bytes 1048576 | tf_op jit(solution)/shard_map/all_to_all | solution.py:265
  37.8 53.1 %all-to-all-done = bf16[64,8,512]{2,1,0:T(8,128)(2,1)S(1)} async-done(((bf16[64,8,512]{2,1,0:T(8,128)(2,1)}), bf16[64,8,512]{2,1,0:T(8,128)(2,1)S(1)}, u32[]{:S(2)}, u32[]{:S(2)}) %all-to-all-start) | async-done | bytes 524320 | tf_op jit(solution)/shard_map/all_to_all | solution.py:265
  90.9 0.8 copy-done.4
  91.7 1.0 copy-done.5
  92.7 4.8 %expert_kernel.1 = (bf16[8,64,1536]{2,1,0:T(8,128)(2,1)S(1)}, bf16[8,64,1536]{2,1,0:T(8,128)(2,1)}, bf16[128,512]{1,0:T(8,128)(2,1)S(1)}, bf16[128,1024]{1,0:T(8,128)(2,1)S(1)}) custom-call(s32[1]{0:T(128)} %bitcast.3.core_ref, bf16[512,512]{1,0:T(8,128)(2,1)S(1)} %bitcast.20, bf16[1024,1024]{1,0:T(8,128)(2,1)} %bitcast.15, bf16[1024,512]{1,0:T(8,128)(2,1)S(1)} %bitcast.17), custom_call_target="tpu_custom_call" | custom-call | tf_op jit(solution)/shard_map/expert_kernel/pallas_call | solution.py:219
  97.5 1.1 copy-done.1
  98.7 1.9 collective-permute-start
  100.6 2.2 return_kernel.1
  102.9 1.4 collective-permute-done.b_ref
  104.3 1.6 add_kernel.6
  105.9 1.6 add_kernel.7.a_ref
  107.5 20.8 %all-to-all-start.1 = ((bf16[64,8,512]{2,1,0:T(8,128)(2,1)}), bf16[64,8,512]{2,1,0:T(8,128)(2,1)S(1)}, u32[]{:S(2)}, u32[]{:S(2)}) async-start(bf16[64,8,512]{2,1,0:T(8,128)(2,1)} %bitcast.8), calls=%async_computation.1 | async-start | bytes 1048576 | tf_op jit(solution)/shard_map/all_to_all | solution.py:265
  128.3 1.9 collective-permute-start.1
  130.3 59.7 %collective-permute-done.1.b_ref = bf16[4,64,1536]{2,1,0:T(8,128)(2,1)S(1)} collective-permute-done((bf16[4,64,1536]{2,1,0:T(8,128)(2,1)S(1)}, bf16[4,64,1536]{2,1,0:T(8,128)(2,1)S(1)}, u32[]{:S(2)}, u32[]{:S(2)}) %collective-permute-start.1) | collective-permute-done | bytes 786464 | tf_op jit(solution)/shard_map/ppermute | solution.py:239
  190.1 0.1 add_kernel.8
  190.2 2.2 collective-permute-start.2
  192.5 0.1 add_kernel.9.a_ref
  192.6 18.9 %collective-permute-done.2.b_ref = bf16[2,64,1536]{2,1,0:T(8,128)(2,1)S(1)} collective-permute-done((bf16[2,64,1536]{2,1,0:T(8,128)(2,1)S(1)}, bf16[2,64,1536]{2,1,0:T(8,128)(2,1)S(1)}, u32[]{:S(2)}, u32[]{:S(2)}) %collective-permute-start.2) | collective-permute-done | bytes 393248 | tf_op jit(solution)/shard_map/ppermute | solution.py:239
  211.5 3.8 %collective-permute-start.3 = (bf16[1,64,1536]{2,1,0:T(8,128)(2,1)S(1)}, bf16[1,64,1536]{2,1,0:T(8,128)(2,1)S(1)}, u32[]{:S(2)}, u32[]{:S(2)}) collective-permute-start(bf16[1,64,1536]{2,1,0:T(8,128)(2,1)S(1)} %add_kernel.10), channel_id=1, source_target_pairs={{0,512},{64,576},{128,640},{192,704},{256,768},{320,832},{384,896}... | collective-permute-start | bytes 589832 | tf_op jit(solution)/shard_map/ppermute | solution.py:239
  215.3 0.4 mask_kernel.1
  215.8 18.1 %collective-permute-done.3.b_ref = bf16[1,64,1536]{2,1,0:T(8,128)(2,1)S(1)} collective-permute-done((bf16[1,64,1536]{2,1,0:T(8,128)(2,1)S(1)}, bf16[1,64,1536]{2,1,0:T(8,128)(2,1)S(1)}, u32[]{:S(2)}, u32[]{:S(2)}) %collective-permute-start.3) | collective-permute-done | bytes 196640 | tf_op jit(solution)/shard_map/ppermute | solution.py:239
  233.9 0.7 last_add_kernel.1
  234.6 1.9 combine_kernel.1
  (18 shorter events, 0.2 us)
Async XLA Ops:
  3.4 88.2 %copy-start.3 = (bf16[1,1024,512]{2,1,0:T(8,128)(2,1)S(1)}, bf16[1,1024,512]{2,1,0:T(8,128)(2,1)}, u32[]{:S(2)}) copy-start(bf16[1,1024,512]{2,1,0:T(8,128)(2,1)} %param.11) | copy-start | bytes 3145732
  3.4 87.4 %all-to-all-start = ((bf16[64,8,512]{2,1,0:T(8,128)(2,1)}), bf16[64,8,512]{2,1,0:T(8,128)(2,1)S(1)}, u32[]{:S(2)}, u32[]{:S(2)}) async-start(bf16[64,8,512]{2,1,0:T(8,128)(2,1)} %bitcast.26), calls=%async_computation | async-start | bytes 1048576 | tf_op jit(solution)/shard_map/all_to_all | solution.py:265
  90.9 0.8 copy-start.4
  91.7 1.0 copy-start.5
  92.7 7.9 %copy-start = (bf16[1,1024,1024]{2,1,0:T(8,128)(2,1)S(1)}, bf16[1,1024,1024]{2,1,0:T(8,128)(2,1)}, u32[]{:S(2)}) copy-start(bf16[1,1024,1024]{2,1,0:T(8,128)(2,1)} %param.10) | copy-start | bytes 6291460
  97.5 1.1 copy-start.1
  98.7 5.6 %collective-permute-start = (bf16[8,64,1536]{2,1,0:T(8,128)(2,1)}, bf16[8,64,1536]{2,1,0:T(8,128)(2,1)}, u32[]{:S(2)}, u32[]{:S(2)}) collective-permute-start(bf16[8,64,1536]{2,1,0:T(8,128)(2,1)} %get-tuple-element.24), channel_id=1, source_target_pairs={{0,64},{64,0},{128,192},{192,128},{256,320},{320,256},{384,448},{4... | collective-permute-start | bytes 4718600 | tf_op jit(solution)/shard_map/ppermute | solution.py:228
  100.6 3.7 %copy-start.2 = (bf16[8,64,1536]{2,1,0:T(8,128)(2,1)S(1)}, bf16[8,64,1536]{2,1,0:T(8,128)(2,1)}, u32[]{:S(2)}) copy-start(bf16[8,64,1536]{2,1,0:T(8,128)(2,1)} %copy-done.1) | copy-start | bytes 4718596
  107.5 127.1 %all-to-all-start.1 = ((bf16[64,8,512]{2,1,0:T(8,128)(2,1)}), bf16[64,8,512]{2,1,0:T(8,128)(2,1)S(1)}, u32[]{:S(2)}, u32[]{:S(2)}) async-start(bf16[64,8,512]{2,1,0:T(8,128)(2,1)} %bitcast.8), calls=%async_computation.1 | async-start | bytes 1048576 | tf_op jit(solution)/shard_map/all_to_all | solution.py:265
  128.3 61.7 %collective-permute-start.1 = (bf16[4,64,1536]{2,1,0:T(8,128)(2,1)S(1)}, bf16[4,64,1536]{2,1,0:T(8,128)(2,1)S(1)}, u32[]{:S(2)}, u32[]{:S(2)}) collective-permute-start(bf16[4,64,1536]{2,1,0:T(8,128)(2,1)S(1)} %add_kernel.6), channel_id=1, source_target_pairs={{0,128},{64,192},{128,0},{192,64},{256,384},{320,448},{384,256},{4... | collective-permute-start | bytes 2359304 | tf_op jit(solution)/shard_map/ppermute | solution.py:239
  190.2 25.1 %copy-start.7 = (s32[128,8]{0,1:T(8,128)S(1)}, s32[128,8]{0,1:T(8,128)}, u32[]{:S(2)}) copy-start(s32[128,8]{0,1:T(8,128)} %param.7) | copy-start | bytes 12292
  190.2 25.1 %copy-start.8 = (f32[128,8]{0,1:T(8,128)S(1)}, f32[128,8]{0,1:T(8,128)}, u32[]{:S(2)}) copy-start(f32[128,8]{0,1:T(8,128)} %param.8) | copy-start | bytes 12292
  190.2 21.3 %collective-permute-start.2 = (bf16[2,64,1536]{2,1,0:T(8,128)(2,1)S(1)}, bf16[2,64,1536]{2,1,0:T(8,128)(2,1)S(1)}, u32[]{:S(2)}, u32[]{:S(2)}) collective-permute-start(bf16[2,64,1536]{2,1,0:T(8,128)(2,1)S(1)} %add_kernel.8), channel_id=1, source_target_pairs={{0,256},{64,320},{128,384},{192,448},{256,0},{320,64},{384,128},{4... | collective-permute-start | bytes 1179656 | tf_op jit(solution)/shard_map/ppermute | solution.py:239
  192.6 42.0 %copy-start.6 = (bf16[128,1024]{1,0:T(8,128)(2,1)S(1)}, bf16[128,1024]{1,0:T(8,128)(2,1)}, u32[]{:S(2)}) copy-start(bf16[128,1024]{1,0:T(8,128)(2,1)} %cot_ref.1) | copy-start | bytes 786436
  211.5 22.4 %collective-permute-start.3 = (bf16[1,64,1536]{2,1,0:T(8,128)(2,1)S(1)}, bf16[1,64,1536]{2,1,0:T(8,128)(2,1)S(1)}, u32[]{:S(2)}, u32[]{:S(2)}) collective-permute-start(bf16[1,64,1536]{2,1,0:T(8,128)(2,1)S(1)} %add_kernel.10), channel_id=1, source_target_pairs={{0,512},{64,576},{128,640},{192,704},{256,768},{320,832},{384,896}... | collective-permute-start | bytes 589832 | tf_op jit(solution)/shard_map/ppermute | solution.py:239

commit v7 on v5

--- a/solution.py
+++ b/solution.py
@@ -158,20 +158,18 @@
     store_leaving(mm(unsort, result).astype(BF16), stay_ref, right_ref, left_ref)
 
 
-def split_kernel(sum_hbm, gate_up_ref, down_ref, sems):
+def add_kernel(bit_ref, a_ref, b_ref, out_ref):
+    bit = bit_ref[0]
+    for block in range(out_ref.shape[0]):
+        index = 2 * block + bit
+        out_ref[block] = (a_ref[index].astype(F32) + b_ref[index].astype(F32)).astype(BF16)
+
+
+def last_add_kernel(a_ref, b_ref, gate_up_ref, down_ref):
     cut = gate_up_ref.shape[1]
-    copies = [
-        pltpu.make_async_copy(sum_hbm.at[:, pl.ds(0, cut)], gate_up_ref, sems.at[0]),
-        pltpu.make_async_copy(sum_hbm.at[:, pl.ds(cut, down_ref.shape[1])], down_ref, sems.at[1]),
-    ]
-    for copy in copies:
-        copy.start()
-    for copy in copies:
-        copy.wait()
-
-
-def add_kernel(a_ref, b_ref, out_ref):
-    out_ref[...] = (a_ref[...].astype(F32) + b_ref[...].astype(F32)).astype(BF16)
+    total = (a_ref[0].astype(F32) + b_ref[0].astype(F32)).astype(BF16)
+    gate_up_ref[...] = total[:, :cut]
+    down_ref[...] = total[:, cut:]
 
 
 def mask_kernel(plane_ref, ids_ref, probs_ref, pick_ref, weight_ref):
@@ -262,22 +260,30 @@
         specs=[smem] + [vmem] * 3,
     )(core, there, w_gate_up[0], w_down[0])
 
-    swapped = lax.ppermute(other, "dp", [(i, i ^ 1) for i in range(replicas)])
+    position = lax.axis_index("dp") // 2
+    chips = replicas // 2
+    arrived = lax.ppermute(other, "dp", [(i, i ^ 1) for i in range(replicas)])
+    kept = mine
     back = call(return_kernel, leave, specs=[smem] + [vmem] * 4)(
         plane, act, grad_hidden, w_gate_up[0], w_down[0]
     )
-    (pair,) = call(add_kernel, [half_terms], specs=[vmem] * 2)(mine, swapped)
-    pair, *back = lax.optimization_barrier((pair, *back))
-    summed = lax.psum_scatter(
-        pair.reshape(lat // 2, width), "dp", scatter_dimension=0, tiled=True,
-        axis_index_groups=[list(range(c, replicas, 2)) for c in range(2)],
-    )
-    home = lax.cond(
-        core[0] < 2,
-        lambda stay, right, left: exchange(stay, right, left),
-        lambda stay, right, left: jnp.concatenate([stay, right, left], axis=0),
-        *back,
-    )
+    steps = exchange(*back)
+    carried = next(steps)
+    distance = 1
+    while distance < chips:
+        blocks = ((chips // (2 * distance), share, width), BF16)
+        bit = (position // distance % 2).astype(jnp.int32).reshape(1)
+        (send,) = call(add_kernel, [blocks], specs=[smem] + [vmem] * 2)(1 - bit, kept, arrived)
+        moving = lax.ppermute(send, "dp", [(i, i ^ (2 * distance)) for i in range(replicas)])
+        kept, send = lax.optimization_barrier((kept, send))
+        (kept,) = call(add_kernel, [blocks], specs=[smem] + [vmem] * 2)(bit, kept, arrived)
+        arrived = moving
+        distance *= 2
+        if carried is not None and distance < chips:
+            arrived, carried = lax.optimization_barrier((arrived, carried))
+            home, carried = carried, steps.send(carried)
+    while carried is not None:
+        home, carried = carried, steps.send(carried)
     pick, weight = call(
         mask_kernel, [((rows, tokens), BF16), ((rows, tokens), F32)], specs=[smem] + [vmem] * 2
     )(plane, ids, probs)
@@ -286,16 +292,9 @@
         [((tokens, lat), BF16), ((tokens, lat), BF16), ((top, tokens), F32)],
         specs=[smem] + [vmem] * 5,
     )(plane, ids, pick, weight, cotangent, home)
-    summed, mixed, latent_gradient, gate_grad = lax.optimization_barrier(
-        (summed, mixed, latent_gradient, gate_grad)
-    )
     gate_up_grad, down_grad = call(
-        split_kernel,
-        [((share, 2 * ffw), BF16), ((share, ffw), BF16)],
-        scratch=[pltpu.SemaphoreType.DMA((2,))],
-        specs=[pl.BlockSpec(memory_space=pl.ANY)],
-        vmem=ALL_VMEM_BYTES,
-    )(summed)
+        last_add_kernel, [((share, 2 * ffw), BF16), ((share, ffw), BF16)], specs=[vmem] * 2
+    )(kept, arrived)
     return (mixed, latent_gradient, gate_grad.T, gate_up_grad[None], down_grad[None])
 
 
@@ -306,17 +305,18 @@
     up = [(e, (e + places) % columns) for e in range(columns)]
     down = [(e, (e - places) % columns) for e in range(columns)]
     half = part // 2
-    one_right = lax.ppermute(right, "expert", up)
-    one_left = lax.ppermute(left, "expert", down)
-    two_right = lax.ppermute(one_right[part:], "expert", up)
-    two_left = lax.ppermute(one_left[:half], "expert", down)
+    one_right, one_left = yield lax.ppermute(right, "expert", up), lax.ppermute(left, "expert", down)
+    two_right, two_left = yield (
+        lax.ppermute(one_right[part:], "expert", up), lax.ppermute(one_left[:half], "expert", down)
+    )
     pieces = [stay, one_right[:part], one_left[half:], jnp.concatenate([two_right, two_left], axis=0)]
     merged = jnp.concatenate([piece.reshape(places, GROUP, wide) for piece in pieces], axis=1)
     moved = lax.all_to_all(
         merged, "expert", split_axis=0, concat_axis=0, tiled=True,
         axis_index_groups=[list(range(z * places, (z + 1) * places)) for z in range(RING)],
     )
-    return moved.reshape(RING * part, wide)
+    yield moved.reshape(RING * part, wide)
+    yield None
 
 
 def solution(mesh):

time: 231 us -> 242 us (1.048)
  the two profiles are of different devices: /device:TPU:96 before, /device:TPU:24 now
where the time goes in v7:
time: 242 us; the launch traced here: 241 us
  waiting for transfers between devices  119 us (49%)
  starting transfers between devices  93.4 us (39%)
  Pallas kernels  16.8 us (7%)
  local copies, waits for them, and re-layouts  9.57 us (4%)
    all_to_all x1, waiting for transfers between devices, local(): lax.all_to_all(sent.reshape(columns, GROUP, wide), 'expert', split_axis=0...  53.1 us
    all_to_all x1, starting transfers between devices, local(): lax.all_to_all(sent.reshape(columns, GROUP, wide), 'expert', split_axis=0...  34.4 us
    ppermute x1, waiting for transfers between devices, exchange(): lax.ppermute(right, 'expert', up)  30.2 us
    ppermute x3, starting transfers between devices, local(): lax.ppermute(send, 'dp', [(i, i ^ 2 * distance) for i in range(replicas)])  20.1 us
    ppermute x3, waiting for transfers between devices, local(): lax.ppermute(send, 'dp', [(i, i ^ 2 * distance) for i in range(replicas)])  18.7 us
    ppermute x1, starting transfers between devices, exchange(): lax.ppermute(one_right[part:], 'expert', up)  11.8 us
    ppermute x1, starting transfers between devices, exchange(): lax.ppermute(left, 'expert', down)  11.1 us
    ppermute x1, waiting for transfers between devices, exchange(): lax.ppermute(one_right[part:], 'expert', up)  9.72 us
  transfers between devices with their start and end apart: 10, of which 7 were waited for; matrix products, arithmetic and copies ran while one was open for 0% of the time, Pallas kernels for 2%

profile of v7, /device:TPU:24, one launch (start us, length us, event | category | flops | bytes accessed | tf_op | source)
XLA Modules:
  0.0 241.1 jit_solution(11603563949476438935)
XLA Ops:
  0.6 2.8 %pack_kernel.1 = bf16[512,512]{1,0:T(8,128)(2,1)} custom-call(s32[8,128]{1,0:T(8,128)} %bitcast.29, f32[8,128]{1,0:T(8,128)} %bitcast.32, bf16[128,1024]{1,0:T(8,128)(2,1)} %latent_hbm.1, bf16[128,1024]{1,0:T(8,128)(2,1)} %cot_ref.1), custom_call_target="tpu_custom_call" | custom-call | tf_op jit(solution)/shard_map/pack_kernel/pallas_call | solution.py:241
  3.5 34.4 %all-to-all-start = ((bf16[64,8,512]{2,1,0:T(8,128)(2,1)}), bf16[64,8,512]{2,1,0:T(8,128)(2,1)S(1)}, u32[]{:S(2)}, u32[]{:S(2)}) async-start(bf16[64,8,512]{2,1,0:T(8,128)(2,1)} %bitcast.34), calls=%async_computation | async-start | bytes 1048576 | tf_op jit(solution)/shard_map/all_to_all | solution.py:249
  37.9 53.1 %all-to-all-done = bf16[64,8,512]{2,1,0:T(8,128)(2,1)S(1)} async-done(((bf16[64,8,512]{2,1,0:T(8,128)(2,1)}), bf16[64,8,512]{2,1,0:T(8,128)(2,1)S(1)}, u32[]{:S(2)}, u32[]{:S(2)}) %all-to-all-start) | async-done | bytes 524320 | tf_op jit(solution)/shard_map/all_to_all | solution.py:249
  90.9 4.6 %expert_kernel.1 = (bf16[8,64,1536]{2,1,0:T(8,128)(2,1)S(1)}, bf16[8,64,1536]{2,1,0:T(8,128)(2,1)}, bf16[128,512]{1,0:T(8,128)(2,1)S(1)}, bf16[128,1024]{1,0:T(8,128)(2,1)S(1)}) custom-call(s32[1]{0:T(128)} %bitcast.3.core_ref, bf16[512,512]{1,0:T(8,128)(2,1)S(1)} %bitcast.27, bf16[1024,1024]{1,0:T(8,128)(2,1)} %bitcast.22, bf16[1024,512]{1,0:T(8,128)(2,1)S(1)} %bitcast.24), custom_call_target="tpu_custom_call" | custom-call | tf_op jit(solution)/shard_map/expert_kernel/pallas_call | solution.py:256
  97.4 1.9 collective-permute-start
  99.3 3.6 %collective-permute-done.b_ref = bf16[8,64,1536]{2,1,0:T(8,128)(2,1)S(1)} collective-permute-done((bf16[8,64,1536]{2,1,0:T(8,128)(2,1)}, bf16[8,64,1536]{2,1,0:T(8,128)(2,1)S(1)}, u32[]{:S(2)}, u32[]{:S(2)}) %collective-permute-start) | collective-permute-done | bytes 1572896 | tf_op jit(solution)/shard_map/ppermute | solution.py:265
  104.0 1.4 copy-done.2
  105.4 1.4 copy-done.5
  107.9 14.9 %collective-permute-start.1 = (bf16[4,64,1536]{2,1,0:T(8,128)(2,1)}, bf16[4,64,1536]{2,1,0:T(8,128)(2,1)}, u32[]{:S(2)}, u32[]{:S(2)}) collective-permute-start(bf16[4,64,1536]{2,1,0:T(8,128)(2,1)} %add_kernel.6), channel_id=1, source_target_pairs={{0,128},{64,192},{128,0},{192,64},{256,384},{320,448},{384,256},{4... | collective-permute-start | bytes 2359304 | tf_op jit(solution)/shard_map/ppermute | solution.py:277
  123.8 2.4 return_kernel.1
  126.2 3.4 %collective-permute-start.2 = (bf16[192,512]{1,0:T(8,128)(2,1)}, bf16[192,512]{1,0:T(8,128)(2,1)S(1)}, u32[]{:S(2)}, u32[]{:S(2)}) collective-permute-start(bf16[192,512]{1,0:T(8,128)(2,1)} %get-tuple-element.35), channel_id=1, source_target_pairs={{0,16},{1,17},{2,18},{3,19},{4,20},{5,21},{6,22},{7,23},{8,24},{9,... | collective-permute-start | bytes 589832 | tf_op jit(solution)/shard_map/ppermute | solution.py:308
  129.6 11.1 %collective-permute-start.3 = (bf16[192,512]{1,0:T(8,128)(2,1)}, bf16[192,512]{1,0:T(8,128)(2,1)S(1)}, u32[]{:S(2)}, u32[]{:S(2)}) collective-permute-start(bf16[192,512]{1,0:T(8,128)(2,1)} %get-tuple-element.36), channel_id=1, source_target_pairs={{0,48},{1,49},{2,50},{3,51},{4,52},{5,53},{6,54},{7,55},{8,56},{9,... | collective-permute-start | bytes 589832 | tf_op jit(solution)/shard_map/ppermute | solution.py:308
  140.8 1.4 copy-done.3
  142.2 1.4 copy-done.6
  143.8 30.2 %collective-permute-done.2 = bf16[192,512]{1,0:T(8,128)(2,1)S(1)} collective-permute-done((bf16[192,512]{1,0:T(8,128)(2,1)}, bf16[192,512]{1,0:T(8,128)(2,1)S(1)}, u32[]{:S(2)}, u32[]{:S(2)}) %collective-permute-start.2) | collective-permute-done | bytes 196640 | tf_op jit(solution)/shard_map/ppermute | solution.py:308
  176.4 1.9 collective-permute-start.4
  178.4 11.8 %collective-permute-start.5 = (bf16[64,512]{1,0:T(8,128)(2,1)S(1)}, bf16[64,512]{1,0:T(8,128)(2,1)S(1)}, u32[]{:S(2)}, u32[]{:S(2)}) collective-permute-start(bf16[64,512]{1,0:T(8,128)(2,1)S(1)} %slice.14), channel_id=1, source_target_pairs={{0,16},{1,17},{2,18},{3,19},{4,20},{5,21},{6,22},{7,23},{8,24},{9,... | collective-permute-start | bytes 196616 | tf_op jit(solution)/shard_map/ppermute | solution.py:310
  190.2 2.8 %collective-permute-start.6 = (bf16[64,512]{1,0:T(8,128)(2,1)S(1)}, bf16[64,512]{1,0:T(8,128)(2,1)S(1)}, u32[]{:S(2)}, u32[]{:S(2)}) collective-permute-start(bf16[64,512]{1,0:T(8,128)(2,1)S(1)} %slice.15), channel_id=1, source_target_pairs={{0,48},{1,49},{2,50},{3,51},{4,52},{5,53},{6,54},{7,55},{8,56},{9,... | collective-permute-start | bytes 196616 | tf_op jit(solution)/shard_map/ppermute | solution.py:310
  193.0 9.7 %collective-permute-done.5 = bf16[64,512]{1,0:T(8,128)(2,1)S(1)} collective-permute-done((bf16[64,512]{1,0:T(8,128)(2,1)S(1)}, bf16[64,512]{1,0:T(8,128)(2,1)S(1)}, u32[]{:S(2)}, u32[]{:S(2)}) %collective-permute-start.5) | collective-permute-done | bytes 65568 | tf_op jit(solution)/shard_map/ppermute | solution.py:310
  202.7 3.0 %collective-permute-done.6 = bf16[64,512]{1,0:T(8,128)(2,1)S(1)} collective-permute-done((bf16[64,512]{1,0:T(8,128)(2,1)S(1)}, bf16[64,512]{1,0:T(8,128)(2,1)S(1)}, u32[]{:S(2)}, u32[]{:S(2)}) %collective-permute-start.6) | collective-permute-done | bytes 65568 | tf_op jit(solution)/shard_map/ppermute | solution.py:310
  206.6 7.9 %all-to-all-start.1 = ((bf16[16,32,512]{2,1,0:T(8,128)(2,1)}), bf16[16,32,512]{2,1,0:T(8,128)(2,1)S(1)}, u32[]{:S(2)}, u32[]{:S(2)}) async-start(bf16[16,32,512]{2,1,0:T(8,128)(2,1)} %pad_maximum_fusion), calls=%async_computation.1 | async-start | bytes 1048576 | tf_op jit(solution)/shard_map/all_to_all | solution.py:314
  215.8 3.3 %collective-permute-start.7 = (bf16[1,64,1536]{2,1,0:T(8,128)(2,1)S(1)}, bf16[1,64,1536]{2,1,0:T(8,128)(2,1)S(1)}, u32[]{:S(2)}, u32[]{:S(2)}) collective-permute-start(bf16[1,64,1536]{2,1,0:T(8,128)(2,1)S(1)} %add_kernel.10), channel_id=1, source_target_pairs={{0,512},{64,576},{128,640},{192,704},{256,768},{320,832},{384,896}... | collective-permute-start | bytes 589832 | tf_op jit(solution)/shard_map/ppermute | solution.py:277
  219.8 18.7 %collective-permute-done.7.b_ref = bf16[1,64,1536]{2,1,0:T(8,128)(2,1)S(1)} collective-permute-done((bf16[1,64,1536]{2,1,0:T(8,128)(2,1)S(1)}, bf16[1,64,1536]{2,1,0:T(8,128)(2,1)S(1)}, u32[]{:S(2)}, u32[]{:S(2)}) %collective-permute-start.7) | collective-permute-done | bytes 196640 | tf_op jit(solution)/shard_map/ppermute | solution.py:277
  239.2 1.9 combine_kernel.1
  (39 shorter events, 11.2 us)
Async XLA Ops:
  3.5 87.5 %copy-start.7 = (bf16[1,1024,512]{2,1,0:T(8,128)(2,1)S(1)}, bf16[1,1024,512]{2,1,0:T(8,128)(2,1)}, u32[]{:S(2)}) copy-start(bf16[1,1024,512]{2,1,0:T(8,128)(2,1)} %param.11) | copy-start | bytes 3145732
  3.5 87.4 %all-to-all-start = ((bf16[64,8,512]{2,1,0:T(8,128)(2,1)}), bf16[64,8,512]{2,1,0:T(8,128)(2,1)S(1)}, u32[]{:S(2)}, u32[]{:S(2)}) async-start(bf16[64,8,512]{2,1,0:T(8,128)(2,1)} %bitcast.34), calls=%async_computation | async-start | bytes 1048576 | tf_op jit(solution)/shard_map/all_to_all | solution.py:249
  95.5 1.2 copy-start.1
  96.7 0.7 copy-start.9
  97.4 5.5 %collective-permute-start = (bf16[8,64,1536]{2,1,0:T(8,128)(2,1)}, bf16[8,64,1536]{2,1,0:T(8,128)(2,1)S(1)}, u32[]{:S(2)}, u32[]{:S(2)}) collective-permute-start(bf16[8,64,1536]{2,1,0:T(8,128)(2,1)} %get-tuple-element.34), channel_id=1, source_target_pairs={{0,64},{64,0},{128,192},{192,128},{256,320},{320,256},{384,448},{4... | collective-permute-start | bytes 4718600 | tf_op jit(solution)/shard_map/ppermute | solution.py:265
  102.9 1.1 copy-start.4
  104.0 1.4 copy-start.2
  105.4 1.4 copy-start.5
  106.9 16.0 %copy-start = (bf16[1,1024,1024]{2,1,0:T(8,128)(2,1)S(1)}, bf16[1,1024,1024]{2,1,0:T(8,128)(2,1)}, u32[]{:S(2)}) copy-start(bf16[1,1024,1024]{2,1,0:T(8,128)(2,1)} %param.10) | copy-start | bytes 6291460
  107.9 67.3 %collective-permute-start.1 = (bf16[4,64,1536]{2,1,0:T(8,128)(2,1)}, bf16[4,64,1536]{2,1,0:T(8,128)(2,1)}, u32[]{:S(2)}, u32[]{:S(2)}) collective-permute-start(bf16[4,64,1536]{2,1,0:T(8,128)(2,1)} %add_kernel.6), channel_id=1, source_target_pairs={{0,128},{64,192},{128,0},{192,64},{256,384},{320,448},{384,256},{4... | collective-permute-start | bytes 2359304 | tf_op jit(solution)/shard_map/ppermute | solution.py:277
  122.9 0.9 copy-start.10
  126.2 47.8 %collective-permute-start.2 = (bf16[192,512]{1,0:T(8,128)(2,1)}, bf16[192,512]{1,0:T(8,128)(2,1)S(1)}, u32[]{:S(2)}, u32[]{:S(2)}) collective-permute-start(bf16[192,512]{1,0:T(8,128)(2,1)} %get-tuple-element.35), channel_id=1, source_target_pairs={{0,16},{1,17},{2,18},{3,19},{4,20},{5,21},{6,22},{7,23},{8,24},{9,... | collective-permute-start | bytes 589832 | tf_op jit(solution)/shard_map/ppermute | solution.py:308
  129.6 45.6 %collective-permute-start.3 = (bf16[192,512]{1,0:T(8,128)(2,1)}, bf16[192,512]{1,0:T(8,128)(2,1)S(1)}, u32[]{:S(2)}, u32[]{:S(2)}) collective-permute-start(bf16[192,512]{1,0:T(8,128)(2,1)} %get-tuple-element.36), channel_id=1, source_target_pairs={{0,48},{1,49},{2,50},{3,51},{4,52},{5,53},{6,54},{7,55},{8,56},{9,... | collective-permute-start | bytes 589832 | tf_op jit(solution)/shard_map/ppermute | solution.py:308
  140.8 1.4 copy-start.3
  142.2 1.4 copy-start.6
  176.4 29.2 %collective-permute-start.4 = (bf16[2,64,1536]{2,1,0:T(8,128)(2,1)S(1)}, bf16[2,64,1536]{2,1,0:T(8,128)(2,1)S(1)}, u32[]{:S(2)}, u32[]{:S(2)}) collective-permute-start(bf16[2,64,1536]{2,1,0:T(8,128)(2,1)S(1)} %add_kernel.8), channel_id=1, source_target_pairs={{0,256},{64,320},{128,384},{192,448},{256,0},{320,64},{384,128},{4... | collective-permute-start | bytes 1179656 | tf_op jit(solution)/shard_map/ppermute | solution.py:277
  178.4 24.3 %collective-permute-start.5 = (bf16[64,512]{1,0:T(8,128)(2,1)S(1)}, bf16[64,512]{1,0:T(8,128)(2,1)S(1)}, u32[]{:S(2)}, u32[]{:S(2)}) collective-permute-start(bf16[64,512]{1,0:T(8,128)(2,1)S(1)} %slice.14), channel_id=1, source_target_pairs={{0,16},{1,17},{2,18},{3,19},{4,20},{5,21},{6,22},{7,23},{8,24},{9,... | collective-permute-start | bytes 196616 | tf_op jit(solution)/shard_map/ppermute | solution.py:310
  190.2 15.5 %collective-permute-start.6 = (bf16[64,512]{1,0:T(8,128)(2,1)S(1)}, bf16[64,512]{1,0:T(8,128)(2,1)S(1)}, u32[]{:S(2)}, u32[]{:S(2)}) collective-permute-start(bf16[64,512]{1,0:T(8,128)(2,1)S(1)} %slice.15), channel_id=1, source_target_pairs={{0,48},{1,49},{2,50},{3,51},{4,52},{5,53},{6,54},{7,55},{8,56},{9,... | collective-permute-start | bytes 196616 | tf_op jit(solution)/shard_map/ppermute | solution.py:310
  206.6 32.6 %all-to-all-start.1 = ((bf16[16,32,512]{2,1,0:T(8,128)(2,1)}), bf16[16,32,512]{2,1,0:T(8,128)(2,1)S(1)}, u32[]{:S(2)}, u32[]{:S(2)}) async-start(bf16[16,32,512]{2,1,0:T(8,128)(2,1)} %pad_maximum_fusion), calls=%async_computation.1 | async-start | bytes 1048576 | tf_op jit(solution)/shard_map/all_to_all | solution.py:314
  214.5 4.7 %copy-start.11 = (s32[128,8]{0,1:T(8,128)S(1)}, s32[128,8]{0,1:T(8,128)}, u32[]{:S(2)}) copy-start(s32[128,8]{0,1:T(8,128)} %param.7) | copy-start | bytes 12292
  214.5 4.7 %copy-start.12 = (f32[128,8]{0,1:T(8,128)S(1)}, f32[128,8]{0,1:T(8,128)}, u32[]{:S(2)}) copy-start(f32[128,8]{0,1:T(8,128)} %param.8) | copy-start | bytes 12292
  215.8 23.4 %copy-start.8 = (bf16[128,1024]{1,0:T(8,128)(2,1)S(1)}, bf16[128,1024]{1,0:T(8,128)(2,1)}, u32[]{:S(2)}) copy-start(bf16[128,1024]{1,0:T(8,128)(2,1)} %cot_ref.1) | copy-start | bytes 786436
  215.8 22.6 %collective-permute-start.7 = (bf16[1,64,1536]{2,1,0:T(8,128)(2,1)S(1)}, bf16[1,64,1536]{2,1,0:T(8,128)(2,1)S(1)}, u32[]{:S(2)}, u32[]{:S(2)}) collective-permute-start(bf16[1,64,1536]{2,1,0:T(8,128)(2,1)S(1)} %add_kernel.10), channel_id=1, source_target_pairs={{0,512},{64,576},{128,640},{192,704},{256,768},{320,832},{384,896}... | collective-permute-start | bytes 589832 | tf_op jit(solution)/shard_map/ppermute | solution.py:277

commit v8 on v6

--- a/solution.py
+++ b/solution.py
@@ -137,11 +137,20 @@
         out_ref[block] = (a_ref[index].astype(F32) + b_ref[index].astype(F32)).astype(BF16)
 
 
-def last_add_kernel(a_ref, b_ref, gate_up_ref, down_ref):
+def spread_kernel(place_ref, a_ref, b_ref, *out_refs):
+    for step, out_ref in enumerate(out_refs):
+        index = place_ref[step]
+        out_ref[...] = (a_ref[index].astype(F32) + b_ref[index].astype(F32)).astype(BF16)
+
+
+def last_add_kernel(*refs):
+    *term_refs, gate_up_ref, down_ref = refs
     cut = gate_up_ref.shape[1]
-    total = (a_ref[0].astype(F32) + b_ref[0].astype(F32)).astype(BF16)
-    gate_up_ref[...] = total[:, :cut]
-    down_ref[...] = total[:, cut:]
+    total = term_refs[0][...].astype(F32)
+    for ref in term_refs[1:]:
+        total = total + ref[...].astype(F32)
+    gate_up_ref[...] = total[:, :cut].astype(BF16)
+    down_ref[...] = total[:, cut:].astype(BF16)
 
 
 def mask_kernel(ids_ref, probs_ref, pick_ref, weight_ref):
@@ -230,33 +239,33 @@
     (back,) = call(return_kernel, [((rows, wide), BF16)], specs=[vmem] * 4)(
         act, grad_hidden, w_gate_up[0], w_down[0]
     )
-    home = None
-    distance = 1
-    while distance < chips:
-        blocks = ((chips // (2 * distance), share, width), BF16)
-        bit = (position // distance % 2).astype(jnp.int32).reshape(1)
-        (send,) = call(add_kernel, [blocks], specs=[smem] + [vmem] * 2)(1 - bit, kept, arrived)
-        moving = lax.ppermute(send, "dp", [(i, i ^ (2 * distance)) for i in range(replicas)])
-        kept, send = lax.optimization_barrier((kept, send))
-        (kept,) = call(add_kernel, [blocks], specs=[smem] + [vmem] * 2)(bit, kept, arrived)
-        arrived = moving
-        if home is None:
-            kept, back = lax.optimization_barrier((kept, back))
-            home = exchange(back, columns)
-        distance *= 2
-    if home is None:
-        home = exchange(back, columns)
+    half_blocks = ((chips // 2, share, width), BF16)
+    bit = (position % 2).astype(jnp.int32).reshape(1)
+    (send,) = call(add_kernel, [half_blocks], specs=[smem] + [vmem] * 2)(1 - bit, kept, arrived)
+    moving = lax.ppermute(send, "dp", [(i, i ^ 2) for i in range(replicas)])
+    kept, send = lax.optimization_barrier((kept, send))
+    (kept,) = call(add_kernel, [half_blocks], specs=[smem] + [vmem] * 2)(bit, kept, arrived)
+    kept, back = lax.optimization_barrier((kept, back))
+    home = lax.cond(core[0] < 2, lambda b: exchange(b, columns), lambda b: b, back)
     pick, weight = call(
         mask_kernel, [((rows, tokens), BF16), ((rows, tokens), F32)], specs=[vmem] * 2
     )(ids, probs)
+    block = ((share, width), BF16)
+    places = ((position // 2) ^ jnp.arange(chips // 2)).astype(jnp.int32)
+    moving, home = lax.optimization_barrier((moving, home))
+    terms = call(spread_kernel, [block] * (chips // 2), specs=[smem] + [vmem] * 2)(places, kept, moving)
+    arrivals = [
+        lax.ppermute(terms[step], "dp", [(i, i ^ (4 * step)) for i in range(replicas)])
+        for step in range(1, chips // 2)
+    ]
+    gate_up_grad, down_grad = call(
+        last_add_kernel, [((share, 2 * ffw), BF16), ((share, ffw), BF16)], specs=[vmem] * (chips // 2)
+    )(terms[0], *arrivals)
     mixed, latent_gradient, gate_grad = call(
         combine_kernel,
         [((tokens, lat), BF16), ((tokens, lat), BF16), ((top, tokens), F32)],
         specs=[vmem] * 5,
     )(ids, pick, weight, cotangent, home)
-    gate_up_grad, down_grad = call(
-        last_add_kernel, [((share, 2 * ffw), BF16), ((share, ffw), BF16)], specs=[vmem] * 2
-    )(kept, arrived)
     return (mixed, latent_gradient, gate_grad.T, gate_up_grad[None], down_grad[None])
 
 

time: 239 us -> 243 us (1.017)
  waiting for transfers between devices: 151 us -> 83.2 us
  blocking collectives: 0 us -> 67.2 us
  local copies, waits for them, and re-layouts: 3.01 us -> 6.24 us
    ppermute x3 -> x4, waiting for transfers between devices: 96.7 us -> 26.6 us  [the longest x3 26.6 us: local(): lax.ppermute(terms[step], 'dp', [(i, i ^ 4 * step) for i in range(replica...]
    all_to_all x0 -> x1, blocking collectives: none -> 67.2 us  [exchange(): lax.all_to_all(message.reshape(columns, rows // columns, wide), 'expert',...]
    ppermute x3 -> x4, starting transfers between devices: 7.91 us -> 30.3 us  [the longest x3 15.4 us: local(): lax.ppermute(terms[step], 'dp', [(i, i ^ 4 * step) for i in range(replica...]
    all_to_all x2 -> x1, starting transfers between devices: 55.2 us -> 34.4 us  [exchange(): lax.all_to_all(message.reshape(columns, rows // columns, wide), 'expert',...]
    unnamed x18 -> x24, local copies, waits for them, and re-layouts: 3.01 us -> 5.16 us
    all_to_all x2 -> x1, waiting for transfers between devices: 53.1 us -> 53.1 us  [exchange(): lax.all_to_all(message.reshape(columns, rows // columns, wide), 'expert',...]
  transfers between devices with their start and end apart: 6 -> 6, of which waited for: 5 -> 3; matrix products, arithmetic and copies ran while one was open for 0% -> 0% of each run, Pallas kernels for 2% -> 2%
where the time goes in v8:
time: 243 us; the launch traced here: 240 us
  waiting for transfers between devices  83.2 us (34%)
  blocking collectives  67.2 us (28%)
  starting transfers between devices  66.5 us (27%)
  Pallas kernels  15.4 us (6%)
  local copies, waits for them, and re-layouts  6.24 us (3%)
    all_to_all x1, blocking collectives, exchange(): lax.all_to_all(message.reshape(columns, rows // columns, wide), 'expert',...  67.2 us
    all_to_all x1, waiting for transfers between devices, exchange(): lax.all_to_all(message.reshape(columns, rows // columns, wide), 'expert',...  53.1 us
    all_to_all x1, starting transfers between devices, exchange(): lax.all_to_all(message.reshape(columns, rows // columns, wide), 'expert',...  34.4 us
    ppermute x3, waiting for transfers between devices, local(): lax.ppermute(terms[step], 'dp', [(i, i ^ 4 * step) for i in range(replica...  26.6 us
    ppermute x3, starting transfers between devices, local(): lax.ppermute(terms[step], 'dp', [(i, i ^ 4 * step) for i in range(replica...  15.4 us
    ppermute x1, starting transfers between devices, local(): moving = lax.ppermute(send, 'dp', [(i, i ^ 2) for i in range(replicas)])  14.9 us
    unnamed x24, local copies, waits for them, and re-layouts  5.16 us
  transfers between devices with their start and end apart: 6, of which 3 were waited for; matrix products, arithmetic and copies ran while one was open for 0% of the time, Pallas kernels for 2%

profile of v8, /device:TPU:24, one launch (start us, length us, event | category | flops | bytes accessed | tf_op | source)
XLA Modules:
  0.0 239.5 jit_solution(11812983597383536952)
XLA Ops:
  0.6 2.8 %pack_kernel.1 = bf16[512,512]{1,0:T(8,128)(2,1)} custom-call(s32[8,128]{1,0:T(8,128)} %bitcast.18, f32[8,128]{1,0:T(8,128)} %bitcast.21, bf16[128,1024]{1,0:T(8,128)(2,1)} %latent_hbm.1, bf16[128,1024]{1,0:T(8,128)(2,1)} %cot_ref.1), custom_call_target="tpu_custom_call" | custom-call | tf_op jit(solution)/shard_map/pack_kernel/pallas_call | solution.py:215
  3.5 34.4 %all-to-all-start.1 = ((bf16[64,8,512]{2,1,0:T(8,128)(2,1)}), bf16[64,8,512]{2,1,0:T(8,128)(2,1)S(1)}, u32[]{:S(2)}, u32[]{:S(2)}) async-start(bf16[64,8,512]{2,1,0:T(8,128)(2,1)} %bitcast.25), calls=%async_computation.1 | async-start | bytes 1048576 | tf_op jit(solution)/shard_map/all_to_all | solution.py:274
  37.8 53.1 %all-to-all-done.1 = bf16[64,8,512]{2,1,0:T(8,128)(2,1)S(1)} async-done(((bf16[64,8,512]{2,1,0:T(8,128)(2,1)}), bf16[64,8,512]{2,1,0:T(8,128)(2,1)S(1)}, u32[]{:S(2)}, u32[]{:S(2)}) %all-to-all-start.1) | async-done | bytes 524320 | tf_op jit(solution)/shard_map/all_to_all | solution.py:274
  90.9 4.6 %expert_kernel.1 = (bf16[8,64,1536]{2,1,0:T(8,128)(2,1)S(1)}, bf16[8,64,1536]{2,1,0:T(8,128)(2,1)}, bf16[128,512]{1,0:T(8,128)(2,1)S(1)}, bf16[128,1024]{1,0:T(8,128)(2,1)S(1)}) custom-call(s32[1]{0:T(128)} %bitcast.5.core_ref, bf16[512,512]{1,0:T(8,128)(2,1)S(1)} %bitcast.17, bf16[1024,1024]{1,0:T(8,128)(2,1)} %bitcast.13, bf16[1024,512]{1,0:T(8,128)(2,1)S(1)} %bitcast.15), custom_call_target="tpu_custom_call" | custom-call | tf_op jit(solution)/shard_map/expert_kernel/pallas_call | solution.py:228
  95.5 1.2 copy-done.1
  96.7 1.9 collective-permute-start
  98.7 3.6 %collective-permute-done.b_ref = bf16[8,64,1536]{2,1,0:T(8,128)(2,1)S(1)} collective-permute-done((bf16[8,64,1536]{2,1,0:T(8,128)(2,1)}, bf16[8,64,1536]{2,1,0:T(8,128)(2,1)S(1)}, u32[]{:S(2)}, u32[]{:S(2)}) %collective-permute-start) | collective-permute-done | bytes 1572896 | tf_op jit(solution)/shard_map/ppermute | solution.py:237
  102.2 1.1 copy-done.4
  103.4 1.4 copy-done.2
  104.8 1.4 copy-done.5
  106.2 1.1 add_kernel.2
  107.2 14.9 %collective-permute-start.1 = (bf16[4,64,1536]{2,1,0:T(8,128)(2,1)}, bf16[4,64,1536]{2,1,0:T(8,128)(2,1)}, u32[]{:S(2)}, u32[]{:S(2)}) collective-permute-start(bf16[4,64,1536]{2,1,0:T(8,128)(2,1)} %add_kernel.2), channel_id=1, source_target_pairs={{0,128},{64,192},{128,0},{192,64},{256,384},{320,448},{384,256},{4... | collective-permute-start | bytes 2359304 | tf_op jit(solution)/shard_map/ppermute | solution.py:245
  122.2 2.3 return_kernel.1
  124.7 68.3 %conditional.1 = (bf16[512,512]{1,0:T(8,128)(2,1)}) conditional(s32[]{:T(128)} %convert_element_type.3, bf16[512,512]{1,0:T(8,128)(2,1)} %return_kernel.1, bf16[512,512]{1,0:T(8,128)(2,1)} %return_kernel.1), branch_computations={%region_0.1_spmd, %region_1.2_spmd} | conditional | bytes 2097160 | solution.py:249
  124.8 1.1 copy.13
  125.8 67.2 %all_to_all.9 = bf16[64,8,512]{2,1,0:T(8,128)(2,1)} all-to-all(bf16[64,8,512]{2,1,0:T(8,128)(2,1)S(1)} %copy.13), channel_id=1, replica_groups=mesh['dp'=16,'expert'=64] {'expert'}, dimensions={0} | all-to-all | bytes 1048576 | tf_op jit(solution)/shard_map/cond/branch_1_fun/all_to_all | solution.py:274
  193.0 1.4 spread_kernel.1
  194.4 1.9 collective-permute-start.2
  196.4 11.5 %collective-permute-start.3 = (bf16[64,1536]{1,0:T(8,128)(2,1)S(1)}, bf16[64,1536]{1,0:T(8,128)(2,1)S(1)}, u32[]{:S(2)}, u32[]{:S(2)}) collective-permute-start(bf16[64,1536]{1,0:T(8,128)(2,1)S(1)} %get-tuple-element.46), channel_id=1, source_target_pairs={{0,512},{64,576},{128,640},{192,704},{256,768},{320,832},{384,896}... | collective-permute-start | bytes 589832 | tf_op jit(solution)/shard_map/ppermute | solution.py:258
  207.9 1.9 collective-permute-start.4
  209.8 0.4 mask_kernel.1
  210.3 1.9 combine_kernel.1
  212.2 26.6 %collective-permute-done.3.refs_2_ = bf16[64,1536]{1,0:T(8,128)(2,1)S(1)} collective-permute-done((bf16[64,1536]{1,0:T(8,128)(2,1)S(1)}, bf16[64,1536]{1,0:T(8,128)(2,1)S(1)}, u32[]{:S(2)}, u32[]{:S(2)}) %collective-permute-start.3) | collective-permute-done | bytes 196640 | tf_op jit(solution)/shard_map/ppermute | solution.py:258
  238.8 0.7 last_add_kernel.1
  (25 shorter events, 0.3 us)
Async XLA Ops:
  3.4 87.5 %copy-start.7 = (bf16[1,1024,512]{2,1,0:T(8,128)(2,1)S(1)}, bf16[1,1024,512]{2,1,0:T(8,128)(2,1)}, u32[]{:S(2)}) copy-start(bf16[1,1024,512]{2,1,0:T(8,128)(2,1)} %param.13) | copy-start | bytes 3145732
  3.5 87.4 %all-to-all-start.1 = ((bf16[64,8,512]{2,1,0:T(8,128)(2,1)}), bf16[64,8,512]{2,1,0:T(8,128)(2,1)S(1)}, u32[]{:S(2)}, u32[]{:S(2)}) async-start(bf16[64,8,512]{2,1,0:T(8,128)(2,1)} %bitcast.25), calls=%async_computation.1 | async-start | bytes 1048576 | tf_op jit(solution)/shard_map/all_to_all | solution.py:274
  95.5 1.2 copy-start.1
  96.7 5.5 %collective-permute-start = (bf16[8,64,1536]{2,1,0:T(8,128)(2,1)}, bf16[8,64,1536]{2,1,0:T(8,128)(2,1)S(1)}, u32[]{:S(2)}, u32[]{:S(2)}) collective-permute-start(bf16[8,64,1536]{2,1,0:T(8,128)(2,1)} %get-tuple-element.33), channel_id=1, source_target_pairs={{0,64},{64,0},{128,192},{192,128},{256,320},{320,256},{384,448},{4... | collective-permute-start | bytes 4718600 | tf_op jit(solution)/shard_map/ppermute | solution.py:237
  102.2 1.1 copy-start.4
  103.4 1.4 copy-start.2
  104.8 1.4 copy-start.5
  106.2 16.0 %copy-start = (bf16[1,1024,1024]{2,1,0:T(8,128)(2,1)S(1)}, bf16[1,1024,1024]{2,1,0:T(8,128)(2,1)}, u32[]{:S(2)}) copy-start(bf16[1,1024,1024]{2,1,0:T(8,128)(2,1)} %param.12) | copy-start | bytes 6291460
  107.2 85.8 %collective-permute-start.1 = (bf16[4,64,1536]{2,1,0:T(8,128)(2,1)}, bf16[4,64,1536]{2,1,0:T(8,128)(2,1)}, u32[]{:S(2)}, u32[]{:S(2)}) collective-permute-start(bf16[4,64,1536]{2,1,0:T(8,128)(2,1)} %add_kernel.2), channel_id=1, source_target_pairs={{0,128},{64,192},{128,0},{192,64},{256,384},{320,448},{384,256},{4... | collective-permute-start | bytes 2359304 | tf_op jit(solution)/shard_map/ppermute | solution.py:245
  122.2 2.3 copy-start.3
  122.2 2.3 copy-start.6
  124.7 85.1 %copy-start.9 = (s32[128,8]{0,1:T(8,128)S(1)}, s32[128,8]{0,1:T(8,128)}, u32[]{:S(2)}) copy-start(s32[128,8]{0,1:T(8,128)} %param.9) | copy-start | bytes 12292
  124.7 85.1 %copy-start.10 = (f32[128,8]{0,1:T(8,128)S(1)}, f32[128,8]{0,1:T(8,128)}, u32[]{:S(2)}) copy-start(f32[128,8]{0,1:T(8,128)} %param.10) | copy-start | bytes 12292
  124.7 85.6 %copy-start.8 = (bf16[128,1024]{1,0:T(8,128)(2,1)S(1)}, bf16[128,1024]{1,0:T(8,128)(2,1)}, u32[]{:S(2)}) copy-start(bf16[128,1024]{1,0:T(8,128)(2,1)} %cot_ref.1) | copy-start | bytes 786436
  193.0 17.3 %copy-start.11 = (bf16[512,512]{1,0:T(8,128)(2,1)S(1)}, bf16[512,512]{1,0:T(8,128)(2,1)}, u32[]{:S(2)}) copy-start(bf16[512,512]{1,0:T(8,128)(2,1)} %get-tuple-element.50.home_ref) | copy-start | bytes 1572868
  194.4 17.8 %collective-permute-start.2 = (bf16[64,1536]{1,0:T(8,128)(2,1)S(1)}, bf16[64,1536]{1,0:T(8,128)(2,1)S(1)}, u32[]{:S(2)}, u32[]{:S(2)}) collective-permute-start(bf16[64,1536]{1,0:T(8,128)(2,1)S(1)} %get-tuple-element.45), channel_id=1, source_target_pairs={{0,256},{64,320},{128,384},{192,448},{256,0},{320,64},{384,128},{4... | collective-permute-start | bytes 589832 | tf_op jit(solution)/shard_map/ppermute | solution.py:258
  196.4 42.4 %collective-permute-start.3 = (bf16[64,1536]{1,0:T(8,128)(2,1)S(1)}, bf16[64,1536]{1,0:T(8,128)(2,1)S(1)}, u32[]{:S(2)}, u32[]{:S(2)}) collective-permute-start(bf16[64,1536]{1,0:T(8,128)(2,1)S(1)} %get-tuple-element.46), channel_id=1, source_target_pairs={{0,512},{64,576},{128,640},{192,704},{256,768},{320,832},{384,896}... | collective-permute-start | bytes 589832 | tf_op jit(solution)/shard_map/ppermute | solution.py:258
  207.9 30.9 %collective-permute-start.4 = (bf16[64,1536]{1,0:T(8,128)(2,1)S(1)}, bf16[64,1536]{1,0:T(8,128)(2,1)S(1)}, u32[]{:S(2)}, u32[]{:S(2)}) collective-permute-start(bf16[64,1536]{1,0:T(8,128)(2,1)S(1)} %get-tuple-element.47), channel_id=1, source_target_pairs={{0,768},{64,832},{128,896},{192,960},{256,512},{320,576},{384,640}... | collective-permute-start | bytes 589832 | tf_op jit(solution)/shard_map/ppermute | solution.py:258

commit v9 on v5

--- a/solution.py
+++ b/solution.py
@@ -259,14 +259,15 @@
         expert_kernel,
         [half_terms, half_terms, ((slots, ffw), BF16), ((slots, 2 * ffw), BF16)],
         scratch=[pltpu.VMEM((lat, width), BF16)],
+        vmem=ALL_VMEM_BYTES,
         specs=[smem] + [vmem] * 3,
     )(core, there, w_gate_up[0], w_down[0])
 
     swapped = lax.ppermute(other, "dp", [(i, i ^ 1) for i in range(replicas)])
-    back = call(return_kernel, leave, specs=[smem] + [vmem] * 4)(
+    back = call(return_kernel, leave, specs=[smem] + [vmem] * 4, vmem=ALL_VMEM_BYTES)(
         plane, act, grad_hidden, w_gate_up[0], w_down[0]
     )
-    (pair,) = call(add_kernel, [half_terms], specs=[vmem] * 2)(mine, swapped)
+    (pair,) = call(add_kernel, [half_terms], specs=[vmem] * 2, vmem=ALL_VMEM_BYTES)(mine, swapped)
     pair, *back = lax.optimization_barrier((pair, *back))
     summed = lax.psum_scatter(
         pair.reshape(lat // 2, width), "dp", scatter_dimension=0, tiled=True,

time: 231 us -> 229 us (level)
  Pallas kernels: 17 us -> 19.5 us
  transfers between devices with their start and end apart: 7 -> 7, of which waited for: 4 -> 3; matrix products, arithmetic and copies ran while one was open for 0% -> 0% of each run, Pallas kernels for 2% -> 3%
where the time goes in v9:
time: 229 us; the launch traced here: 228 us
  waiting for transfers between devices  112 us (49%)
  starting transfers between devices  64.5 us (28%)
  Pallas kernels  19.5 us (9%)
  blocking collectives  16.8 us (7%)
  between operations  14.1 us (6%)
    all_to_all x1, waiting for transfers between devices, local(): lax.all_to_all(sent.reshape(columns, GROUP, wide), 'expert', split_axis=0...  63.9 us
    ppermute x1, waiting for transfers between devices, exchange(): one_left = lax.ppermute(left, 'expert', down)  34.4 us
    all_to_all x1, starting transfers between devices, local(): lax.all_to_all(sent.reshape(columns, GROUP, wide), 'expert', split_axis=0...  31.8 us
    all_to_all x1, blocking collectives, exchange(): lax.all_to_all(merged, 'expert', split_axis=0, concat_axis=0, tiled=True,...  16.8 us
    ppermute x1, waiting for transfers between devices, exchange(): two_right = lax.ppermute(one_right[part:], 'expert', up)  13.3 us
    ppermute x1, starting transfers between devices, exchange(): one_right = lax.ppermute(right, 'expert', up)  12.6 us
    ppermute x1, starting transfers between devices, exchange(): two_left = lax.ppermute(one_left[:half], 'expert', down)  10.6 us
    pallas_call x1, Pallas kernels, local(): call(expert_kernel, [half_terms, half_terms, ((slots, ffw), BF16), ((slot...  5.6 us
  transfers between devices with their start and end apart: 7, of which 3 were waited for; matrix products, arithmetic and copies ran while one was open for 0% of the time, Pallas kernels for 3%

profile of v9, /device:TPU:96, one launch (start us, length us, event | category | flops | bytes accessed | tf_op | source)
XLA Modules:
  0.0 228.3 jit_solution(1192368299156872425)
XLA Ops:
  7.2 2.8 %pack_kernel.1 = bf16[512,512]{1,0:T(8,128)(2,1)} custom-call(s32[8,128]{1,0:T(8,128)} %bitcast.20, f32[8,128]{1,0:T(8,128)} %bitcast.23, bf16[128,1024]{1,0:T(8,128)(2,1)} %latent_hbm.1, bf16[128,1024]{1,0:T(8,128)(2,1)} %cot_ref.1), custom_call_target="tpu_custom_call" | custom-call | tf_op jit(solution)/shard_map/pack_kernel/pallas_call | solution.py:243
  10.0 31.8 %all-to-all-start.1 = ((bf16[64,8,512]{2,1,0:T(8,128)(2,1)}), bf16[64,8,512]{2,1,0:T(8,128)(2,1)S(1)}, u32[]{:S(2)}, u32[]{:S(2)}) async-start(bf16[64,8,512]{2,1,0:T(8,128)(2,1)} %bitcast.30), calls=%async_computation.1 | async-start | bytes 1048576 | tf_op jit(solution)/shard_map/all_to_all | solution.py:251
  41.7 0.0 reduce-scatter.2.cloned.1.call-start
  41.8 63.9 %all-to-all-done.1 = bf16[64,8,512]{2,1,0:T(8,128)(2,1)S(1)} async-done(((bf16[64,8,512]{2,1,0:T(8,128)(2,1)}), bf16[64,8,512]{2,1,0:T(8,128)(2,1)S(1)}, u32[]{:S(2)}, u32[]{:S(2)}) %all-to-all-start.1) | async-done | bytes 524320 | tf_op jit(solution)/shard_map/all_to_all | solution.py:251
  105.7 0.8 copy-done.3
  106.5 5.6 %expert_kernel.1 = (bf16[8,64,1536]{2,1,0:T(8,128)(2,1)}, bf16[8,64,1536]{2,1,0:T(8,128)(2,1)}, bf16[128,512]{1,0:T(8,128)(2,1)}, bf16[128,1024]{1,0:T(8,128)(2,1)}) custom-call(s32[1]{0:T(128)} %bitcast.5.core_ref, bf16[512,512]{1,0:T(8,128)(2,1)} %bitcast.32, bf16[1024,1024]{1,0:T(8,128)(2,1)} %bitcast.25, bf16[1024,512]{1,0:T(8,128)(2,1)} %bitcast.28), custom_call_target="tpu_custom_call" | custom-call | tf_op jit(solution)/shard_map/expert_kernel/pallas_call | solution.py:258
  112.1 1.9 collective-permute-start.4
  114.0 3.7 %return_kernel.1 = (bf16[128,512]{1,0:T(8,128)(2,1)S(1)}, bf16[192,512]{1,0:T(8,128)(2,1)S(1)}, bf16[192,512]{1,0:T(8,128)(2,1)S(1)}) custom-call(s32[1]{0:T(128)} %bitcast.12.plane_ref, bf16[128,512]{1,0:T(8,128)(2,1)} %get-tuple-element.50.act_ref, bf16[128,1024]{1,0:T(8,128)(2,1)} %get-tuple-element.51.grad_ref, bf16[1024,1024]{1,0:T(8,128)(2,1)} %bitcast.26, ...), custom_call_target="tpu_custom_call" | custom-call | tf_op jit(solution)/shard_map/return_kernel/pallas_call | solution.py:267
  117.7 3.4 %add_kernel.1 = bf16[8,64,1536]{2,1,0:T(8,128)(2,1)} custom-call(bf16[8,64,1536]{2,1,0:T(8,128)(2,1)} %get-tuple-element.48.a_ref, bf16[8,64,1536]{2,1,0:T(8,128)(2,1)} %collective-permute-done.4.b_ref), custom_call_target="tpu_custom_call" | custom-call | tf_op jit(solution)/shard_map/add_kernel/pallas_call | solution.py:270
  121.1 0.0 reduce-scatter.2.cloned.1.call-update
  121.1 0.7 copy-done.1
  121.8 0.0 copy-done.2
  121.8 0.5 mask_kernel.1
  122.4 0.0 copy-start
  122.4 95.5 %conditional.1 = (bf16[512,512]{1,0:T(8,128)(2,1)S(1)}) conditional(s32[]{:T(128)} %convert_element_type.3, (bf16[128,512]{1,0:T(8,128)(2,1)S(1)}, bf16[192,512]{1,0:T(8,128)(2,1)S(1)}, bf16[192,512]{1,0:T(8,128)(2,1)S(1)}) %return_kernel.1, (bf16[128,512]{1,0:T(8,128)(2,1)S(1)}, bf16[192,512]{1,0:T(8,128)(2,1)S(1)}, ...), branch_computations={%region_1.2_spmd, %region_2.3_spmd} | conditional | flops 2359296 | bytes 5243048 | solution.py:276
  122.4 2.1 collective-permute-start.1
  124.4 12.6 %collective-permute-start = (bf16[192,512]{1,0:T(8,128)(2,1)S(1)}, bf16[192,512]{1,0:T(8,128)(2,1)S(1)}, u32[]{:S(2)}, u32[]{:S(2)}) collective-permute-start(bf16[192,512]{1,0:T(8,128)(2,1)S(1)} %get-tuple-element.19), channel_id=1, source_target_pairs={{0,16},{1,17},{2,18},{3,19},{4,20},{5,21},{6,22},{7,23},{8,24},{9,... | collective-permute-start | bytes 589832 | tf_op jit(solution)/shard_map/cond/branch_1_fun/ppermute | solution.py:310
  137.1 34.4 %collective-permute-done.1 = bf16[192,512]{1,0:T(8,128)(2,1)S(1)} collective-permute-done((bf16[192,512]{1,0:T(8,128)(2,1)S(1)}, bf16[192,512]{1,0:T(8,128)(2,1)S(1)}, u32[]{:S(2)}, u32[]{:S(2)}) %collective-permute-start.1) | collective-permute-done | bytes 196640 | tf_op jit(solution)/shard_map/cond/branch_1_fun/ppermute | solution.py:311
  171.5 10.6 %collective-permute-start.3 = (bf16[64,512]{1,0:T(8,128)(2,1)S(1)}, bf16[64,512]{1,0:T(8,128)(2,1)S(1)}, u32[]{:S(2)}, u32[]{:S(2)}) collective-permute-start(bf16[64,512]{1,0:T(8,128)(2,1)S(1)} %slice.15), channel_id=1, source_target_pairs={{0,48},{1,49},{2,50},{3,51},{4,52},{5,53},{6,54},{7,55},{8,56},{9,... | collective-permute-start | bytes 196616 | tf_op jit(solution)/shard_map/cond/branch_1_fun/ppermute | solution.py:313
  182.2 5.5 %collective-permute-start.2 = (bf16[64,512]{1,0:T(8,128)(2,1)S(1)}, bf16[64,512]{1,0:T(8,128)(2,1)S(1)}, u32[]{:S(2)}, u32[]{:S(2)}) collective-permute-start(bf16[64,512]{1,0:T(8,128)(2,1)S(1)} %slice.14), channel_id=1, source_target_pairs={{0,16},{1,17},{2,18},{3,19},{4,20},{5,21},{6,22},{7,23},{8,24},{9,... | collective-permute-start | bytes 196616 | tf_op jit(solution)/shard_map/cond/branch_1_fun/ppermute | solution.py:312
  187.7 13.3 %collective-permute-done.2 = bf16[64,512]{1,0:T(8,128)(2,1)S(1)} collective-permute-done((bf16[64,512]{1,0:T(8,128)(2,1)S(1)}, bf16[64,512]{1,0:T(8,128)(2,1)S(1)}, u32[]{:S(2)}, u32[]{:S(2)}) %collective-permute-start.2) | collective-permute-done | bytes 65568 | tf_op jit(solution)/shard_map/cond/branch_1_fun/ppermute | solution.py:312
  201.1 16.8 %all_to_all.9 = bf16[16,32,512]{2,1,0:T(8,128)(2,1)S(1)} all-to-all(bf16[16,32,512]{2,1,0:T(8,128)(2,1)S(1)} %pad_maximum_fusion.1), channel_id=1, replica_groups={{0,1,2,3,4,5,6,7,8,9,10,11,12,13,14,15},{16,17,18,19,20,21,22,23,24,25,..., dimensions={0} | all-to-all | bytes 1048576 | tf_op jit(solution)/shard_map/cond/branch_1_fun/all_to_all | solution.py:316
  217.9 1.9 combine_kernel.1
  219.9 1.6 split_kernel.1
  (14 shorter events, 0.1 us)
Async XLA Ops:
  10.0 95.7 %all-to-all-start.1 = ((bf16[64,8,512]{2,1,0:T(8,128)(2,1)}), bf16[64,8,512]{2,1,0:T(8,128)(2,1)S(1)}, u32[]{:S(2)}, u32[]{:S(2)}) async-start(bf16[64,8,512]{2,1,0:T(8,128)(2,1)} %bitcast.30), calls=%async_computation.1 | async-start | bytes 1048576 | tf_op jit(solution)/shard_map/all_to_all | solution.py:251
  41.7 178.1 %reduce-scatter.2.cloned.1.call-start = ((), (), s32[]{:S(2)}) async-start(), calls=%async_computation.3 | async-start | bytes 1769472 | tf_op jit(solution)/shard_map/reduce_scatter | solution.py:272
  105.7 0.8 copy-start.3
  112.1 5.6 %collective-permute-start.4 = (bf16[8,64,1536]{2,1,0:T(8,128)(2,1)}, bf16[8,64,1536]{2,1,0:T(8,128)(2,1)}, u32[]{:S(2)}, u32[]{:S(2)}) collective-permute-start(bf16[8,64,1536]{2,1,0:T(8,128)(2,1)} %get-tuple-element.49), channel_id=1, source_target_pairs={{0,64},{64,0},{128,192},{192,128},{256,320},{320,256},{384,448},{4... | collective-permute-start | bytes 4718600 | tf_op jit(solution)/shard_map/ppermute | solution.py:266
  121.1 0.7 copy-start.1
  121.1 0.7 copy-start.2
  122.4 95.6 %copy-start = (bf16[128,1024]{1,0:T(8,128)(2,1)S(1)}, bf16[128,1024]{1,0:T(8,128)(2,1)}, u32[]{:S(2)}) copy-start(bf16[128,1024]{1,0:T(8,128)(2,1)} %cot_ref.1) | copy-start | bytes 786436
  122.4 49.1 %collective-permute-start.1 = (bf16[192,512]{1,0:T(8,128)(2,1)S(1)}, bf16[192,512]{1,0:T(8,128)(2,1)S(1)}, u32[]{:S(2)}, u32[]{:S(2)}) collective-permute-start(bf16[192,512]{1,0:T(8,128)(2,1)S(1)} %get-tuple-element.20), channel_id=1, source_target_pairs={{0,48},{1,49},{2,50},{3,51},{4,52},{5,53},{6,54},{7,55},{8,56},{9,... | collective-permute-start | bytes 589832 | tf_op jit(solution)/shard_map/cond/branch_1_fun/ppermute | solution.py:311
  124.4 57.7 %collective-permute-start = (bf16[192,512]{1,0:T(8,128)(2,1)S(1)}, bf16[192,512]{1,0:T(8,128)(2,1)S(1)}, u32[]{:S(2)}, u32[]{:S(2)}) collective-permute-start(bf16[192,512]{1,0:T(8,128)(2,1)S(1)} %get-tuple-element.19), channel_id=1, source_target_pairs={{0,16},{1,17},{2,18},{3,19},{4,20},{5,21},{6,22},{7,23},{8,24},{9,... | collective-permute-start | bytes 589832 | tf_op jit(solution)/shard_map/cond/branch_1_fun/ppermute | solution.py:310
  171.5 16.2 %collective-permute-start.3 = (bf16[64,512]{1,0:T(8,128)(2,1)S(1)}, bf16[64,512]{1,0:T(8,128)(2,1)S(1)}, u32[]{:S(2)}, u32[]{:S(2)}) collective-permute-start(bf16[64,512]{1,0:T(8,128)(2,1)S(1)} %slice.15), channel_id=1, source_target_pairs={{0,48},{1,49},{2,50},{3,51},{4,52},{5,53},{6,54},{7,55},{8,56},{9,... | collective-permute-start | bytes 196616 | tf_op jit(solution)/shard_map/cond/branch_1_fun/ppermute | solution.py:313
  182.2 18.8 %collective-permute-start.2 = (bf16[64,512]{1,0:T(8,128)(2,1)S(1)}, bf16[64,512]{1,0:T(8,128)(2,1)S(1)}, u32[]{:S(2)}, u32[]{:S(2)}) collective-permute-start(bf16[64,512]{1,0:T(8,128)(2,1)S(1)} %slice.14), channel_id=1, source_target_pairs={{0,16},{1,17},{2,18},{3,19},{4,20},{5,21},{6,22},{7,23},{8,24},{9,... | collective-permute-start | bytes 196616 | tf_op jit(solution)/shard_map/cond/branch_1_fun/ppermute | solution.py:312
Sparse Core Ops, SparseCore 0:
  121.3 82.1 reduce-scatter.1

commit v10 on v3

--- a/solution.py
+++ b/solution.py
@@ -79,6 +79,10 @@
     return ((index & 2) + ((index >> 2) & 1)) * slots + group * CAP + (index & 1)
 
 
+def line_ring(chips):
+    return list(range(0, chips, 2)) + list(range(1, chips, 2))[::-1]
+
+
 def expert_kernel(
     core_ref, there_ref, win_ref, wout_ref, mine_ref, other_ref, act_ref, grad_ref, terms_ref
 ):
@@ -108,9 +112,9 @@
         terms_ref[top[h], : 2 * ffw] = mm(vec[h], grad_hidden, 0, 0).astype(BF16)
         terms_ref[top[h], 2 * ffw :] = mm(cot[h], act, 0, 0).astype(BF16)
     even = core_ref[0] == 0
-    for block in range(mine_ref.shape[0]):
-        a = terms_ref[pl.ds(2 * block * share, share), :]
-        b = terms_ref[pl.ds((2 * block + 1) * share, share), :]
+    for block, chip in enumerate(line_ring(mine_ref.shape[0])):
+        a = terms_ref[pl.ds(2 * chip * share, share), :]
+        b = terms_ref[pl.ds((2 * chip + 1) * share, share), :]
         mine_ref[block] = jnp.where(even, a, b)
         other_ref[block] = jnp.where(even, b, a)
 
@@ -232,7 +236,7 @@
     pair, back = lax.optimization_barrier((pair, back))
     summed = lax.psum_scatter(
         pair.reshape(lat // 2, width), "dp", scatter_dimension=0, tiled=True,
-        axis_index_groups=[list(range(c, replicas, 2)) for c in range(2)],
+        axis_index_groups=[[2 * chip + c for chip in line_ring(replicas // 2)] for c in range(2)],
     )
     home = lax.cond(core[0] < 2, lambda b: exchange(b, columns), lambda b: b, back)
     pick, weight = call(

time: 227 us -> 215 us (0.947)
  waiting for transfers between devices: 84.4 us -> 72.1 us
    reduce_scatter x1, waiting for transfers between devices: 29.4 us -> 17.2 us  [local(): lax.psum_scatter(pair.reshape(lat // 2, width), 'dp', scatter_dimension=0...]
where the time goes in v10:
time: 215 us; the launch traced here: 214 us
  blocking collectives  77.5 us (36%)
  waiting for transfers between devices  72.1 us (34%)
  starting transfers between devices  36.3 us (17%)
  between operations  14.1 us (7%)
  Pallas kernels  13.3 us (6%)
    all_to_all x1, blocking collectives, exchange(): lax.all_to_all(message.reshape(columns, rows // columns, wide), 'expert',...  77.5 us
    all_to_all x1, waiting for transfers between devices, exchange(): lax.all_to_all(message.reshape(columns, rows // columns, wide), 'expert',...  53 us
    all_to_all x1, starting transfers between devices, exchange(): lax.all_to_all(message.reshape(columns, rows // columns, wide), 'expert',...  34.4 us
    reduce_scatter x1, waiting for transfers between devices, local(): lax.psum_scatter(pair.reshape(lat // 2, width), 'dp', scatter_dimension=0...  17.2 us
  transfers between devices with their start and end apart: 3, of which 3 were waited for; matrix products, arithmetic and copies ran while one was open for 0% of the time, Pallas kernels for 2%

profile of v10, /device:TPU:24, one launch (start us, length us, event | category | flops | bytes accessed | tf_op | source)
XLA Modules:
  0.0 214.1 jit_solution(11747837366918476314)
XLA Ops:
  7.2 2.8 %pack_kernel.1 = bf16[512,512]{1,0:T(8,128)(2,1)} custom-call(s32[8,128]{1,0:T(8,128)} %bitcast.18, f32[8,128]{1,0:T(8,128)} %bitcast.21, bf16[128,1024]{1,0:T(8,128)(2,1)} %latent_hbm.1, bf16[128,1024]{1,0:T(8,128)(2,1)} %cot_ref.1), custom_call_target="tpu_custom_call" | custom-call | tf_op jit(solution)/shard_map/pack_kernel/pallas_call | solution.py:211
  10.0 0.0 copy-start.1
  10.0 34.4 %all-to-all-start.1 = ((bf16[64,8,512]{2,1,0:T(8,128)(2,1)}), bf16[64,8,512]{2,1,0:T(8,128)(2,1)S(1)}, u32[]{:S(2)}, u32[]{:S(2)}) async-start(bf16[64,8,512]{2,1,0:T(8,128)(2,1)} %bitcast.25), calls=%async_computation.1 | async-start | bytes 1048576 | tf_op jit(solution)/shard_map/all_to_all | solution.py:265
  44.3 0.0 reduce-scatter.2.cloned.1.call-start
  44.4 53.0 %all-to-all-done.1 = bf16[64,8,512]{2,1,0:T(8,128)(2,1)S(1)} async-done(((bf16[64,8,512]{2,1,0:T(8,128)(2,1)}), bf16[64,8,512]{2,1,0:T(8,128)(2,1)S(1)}, u32[]{:S(2)}, u32[]{:S(2)}) %all-to-all-start.1) | async-done | bytes 524320 | tf_op jit(solution)/shard_map/all_to_all | solution.py:265
  97.4 0.0 copy-done.1
  97.4 0.0 copy-start
  97.4 3.6 %expert_kernel.1 = (bf16[8,64,1536]{2,1,0:T(8,128)(2,1)S(1)}, bf16[8,64,1536]{2,1,0:T(8,128)(2,1)S(1)}, bf16[128,512]{1,0:T(8,128)(2,1)S(1)}, bf16[128,1024]{1,0:T(8,128)(2,1)S(1)}) custom-call(s32[1]{0:T(128)} %bitcast.2.core_ref, bf16[512,512]{1,0:T(8,128)(2,1)S(1)} %bitcast.17, bf16[1024,1024]{1,0:T(8,128)(2,1)} %bitcast.13, bf16[1024,512]{1,0:T(8,128)(2,1)S(1)} %bitcast.15), custom_call_target="tpu_custom_call" | custom-call | tf_op jit(solution)/shard_map/expert_kernel/pallas_call | solution.py:224
  101.1 1.9 collective-permute-start
  103.0 0.0 copy-done
  103.0 1.4 return_kernel.1
  104.5 1.9 collective-permute-done.b_ref
  106.4 1.5 add_kernel.1
  107.9 0.0 copy-start.3
  107.9 0.0 reduce-scatter.2.cloned.1.call-update
  107.9 0.7 copy-done.3
  108.6 0.0 copy-done.4
  108.6 0.4 mask_kernel.1
  109.1 77.5 %conditional.1 = (bf16[512,512]{1,0:T(8,128)(2,1)S(1)}) conditional(s32[]{:T(128)} %convert_element_type.3, bf16[512,512]{1,0:T(8,128)(2,1)S(1)} %return_kernel.1, bf16[512,512]{1,0:T(8,128)(2,1)S(1)} %return_kernel.1), branch_computations={%region_1.2_spmd, %region_2.3_spmd} | conditional | bytes 2097160 | solution.py:241
  109.1 77.5 %all_to_all.9 = bf16[64,8,512]{2,1,0:T(8,128)(2,1)S(1)} all-to-all(bf16[64,8,512]{2,1,0:T(8,128)(2,1)S(1)} %copy.13), channel_id=1, replica_groups=mesh['dp'=16,'expert'=64] {'expert'}, dimensions={0} | all-to-all | bytes 1048576 | tf_op jit(solution)/shard_map/cond/branch_1_fun/all_to_all | solution.py:265
  186.6 0.0 copy-done.2
  186.6 1.9 combine_kernel.1
  188.5 17.2 %reduce-scatter.2.cloned.1.call-done.sum_hbm = bf16[64,1536]{1,0:T(8,128)(2,1)} async-done(((bf16[512,1536]{1,0:T(8,128)(2,1)}), bf16[64,1536]{1,0:T(8,128)(2,1)}) %reduce-scatter.2.cloned.1.call-update) | async-done | bytes 196624 | tf_op jit(solution)/shard_map/reduce_scatter | solution.py:237
  205.6 1.6 split_kernel.1
  (3 shorter events, 0.0 us)
Async XLA Ops:
  10.0 87.5 %copy-start.1 = (bf16[1,1024,512]{2,1,0:T(8,128)(2,1)S(1)}, bf16[1,1024,512]{2,1,0:T(8,128)(2,1)}, u32[]{:S(2)}) copy-start(bf16[1,1024,512]{2,1,0:T(8,128)(2,1)} %param.13) | copy-start | bytes 3145732
  10.0 87.4 %all-to-all-start.1 = ((bf16[64,8,512]{2,1,0:T(8,128)(2,1)}), bf16[64,8,512]{2,1,0:T(8,128)(2,1)S(1)}, u32[]{:S(2)}, u32[]{:S(2)}) async-start(bf16[64,8,512]{2,1,0:T(8,128)(2,1)} %bitcast.25), calls=%async_computation.1 | async-start | bytes 1048576 | tf_op jit(solution)/shard_map/all_to_all | solution.py:265
  44.3 161.3 %reduce-scatter.2.cloned.1.call-start = ((), (), s32[]{:S(2)}) async-start(), calls=%async_computation.3 | async-start | bytes 1769472 | tf_op jit(solution)/shard_map/reduce_scatter | solution.py:237
  97.4 5.6 %copy-start = (bf16[1,1024,1024]{2,1,0:T(8,128)(2,1)S(1)}, bf16[1,1024,1024]{2,1,0:T(8,128)(2,1)}, u32[]{:S(2)}) copy-start(bf16[1,1024,1024]{2,1,0:T(8,128)(2,1)} %param.12) | copy-start | bytes 6291460
  101.1 5.3 %collective-permute-start = (bf16[8,64,1536]{2,1,0:T(8,128)(2,1)S(1)}, bf16[8,64,1536]{2,1,0:T(8,128)(2,1)S(1)}, u32[]{:S(2)}, u32[]{:S(2)}) collective-permute-start(bf16[8,64,1536]{2,1,0:T(8,128)(2,1)S(1)} %get-tuple-element.28), channel_id=1, source_target_pairs={{0,64},{64,0},{128,192},{192,128},{256,320},{320,256},{384,448},{4... | collective-permute-start | bytes 4718600 | tf_op jit(solution)/shard_map/ppermute | solution.py:231
  107.9 0.7 copy-start.3
  107.9 0.7 copy-start.4
  107.9 78.7 %copy-start.2 = (bf16[128,1024]{1,0:T(8,128)(2,1)S(1)}, bf16[128,1024]{1,0:T(8,128)(2,1)}, u32[]{:S(2)}) copy-start(bf16[128,1024]{1,0:T(8,128)(2,1)} %cot_ref.1) | copy-start | bytes 786436
Sparse Core Ops, SparseCore 0:
  108.0 97.5 reduce-scatter.1

commit v11 on v9

--- a/solution.py
+++ b/solution.py
@@ -103,6 +103,10 @@
     return ((index & 2) + ((index >> 2) & 1)) * slots + group * CAP + (index & 1)
 
 
+def line_ring(chips):
+    return list(range(0, chips, 2)) + list(range(1, chips, 2))[::-1]
+
+
 def expert_kernel(
     core_ref, there_ref, win_ref, wout_ref, mine_ref, other_ref, act_ref, grad_ref, terms_ref
 ):
@@ -132,9 +136,9 @@
         terms_ref[top[h], : 2 * ffw] = mm(vec[h], grad_hidden, 0, 0).astype(BF16)
         terms_ref[top[h], 2 * ffw :] = mm(cot[h], act, 0, 0).astype(BF16)
     even = core_ref[0] == 0
-    for block in range(mine_ref.shape[0]):
-        a = terms_ref[pl.ds(2 * block * share, share), :]
-        b = terms_ref[pl.ds((2 * block + 1) * share, share), :]
+    for block, chip in enumerate(line_ring(mine_ref.shape[0])):
+        a = terms_ref[pl.ds(2 * chip * share, share), :]
+        b = terms_ref[pl.ds((2 * chip + 1) * share, share), :]
         mine_ref[block] = jnp.where(even, a, b)
         other_ref[block] = jnp.where(even, b, a)
 
@@ -271,7 +275,7 @@
     pair, *back = lax.optimization_barrier((pair, *back))
     summed = lax.psum_scatter(
         pair.reshape(lat // 2, width), "dp", scatter_dimension=0, tiled=True,
-        axis_index_groups=[list(range(c, replicas, 2)) for c in range(2)],
+        axis_index_groups=[[2 * chip + c for chip in line_ring(replicas // 2)] for c in range(2)],
     )
     home = lax.cond(
         core[0] < 2,

time: 229 us -> 231 us (level)
  waiting for transfers between devices: 112 us -> 115 us
    ppermute x1, waiting for transfers between devices: 13.3 us -> 8.63 us  [exchange(): two_right = lax.ppermute(one_right[part:], 'expert', up)]
    ppermute x1, waiting for transfers between devices: 34.4 us -> 38.8 us  [exchange(): one_left = lax.ppermute(left, 'expert', down)]
    ppermute x1, waiting for transfers between devices: 0.01 us -> 3.48 us  [exchange(): two_left = lax.ppermute(one_left[:half], 'expert', down)]
    ppermute x1, starting transfers between devices: 10.6 us -> 8.05 us  [exchange(): two_left = lax.ppermute(one_left[:half], 'expert', down)]
  transfers between devices with their start and end apart: 7 -> 7, of which waited for: 3 -> 4; matrix products, arithmetic and copies ran while one was open for 0% -> 0% of each run, Pallas kernels for 3% -> 3%
where the time goes in v11:
time: 231 us
  waiting for transfers between devices  115 us (50%)
  starting transfers between devices  62.9 us (27%)
  Pallas kernels  19.5 us (8%)
  blocking collectives  17.7 us (8%)
  between operations  14.1 us (6%)
    all_to_all x1, waiting for transfers between devices, local(): lax.all_to_all(sent.reshape(columns, GROUP, wide), 'expert', split_axis=0...  63.9 us
    ppermute x1, waiting for transfers between devices, exchange(): one_left = lax.ppermute(left, 'expert', down)  38.8 us
    all_to_all x1, starting transfers between devices, local(): lax.all_to_all(sent.reshape(columns, GROUP, wide), 'expert', split_axis=0...  31.8 us
    all_to_all x1, blocking collectives, exchange(): lax.all_to_all(merged, 'expert', split_axis=0, concat_axis=0, tiled=True,...  17.7 us
    ppermute x1, starting transfers between devices, exchange(): one_right = lax.ppermute(right, 'expert', up)  12.6 us
    ppermute x1, waiting for transfers between devices, exchange(): two_right = lax.ppermute(one_right[part:], 'expert', up)  8.63 us
    ppermute x1, starting transfers between devices, exchange(): two_left = lax.ppermute(one_left[:half], 'expert', down)  8.05 us
    ppermute x1, starting transfers between devices, exchange(): two_right = lax.ppermute(one_right[part:], 'expert', up)  6.5 us
  transfers between devices with their start and end apart: 7, of which 4 were waited for; matrix products, arithmetic and copies ran while one was open for 0% of the time, Pallas kernels for 3%

profile of v11, /device:TPU:96, one launch (start us, length us, event | category | flops | bytes accessed | tf_op | source)
XLA Modules:
  0.0 230.9 jit_solution(11482722180219598975)
XLA Ops:
  7.2 2.8 %pack_kernel.1 = bf16[512,512]{1,0:T(8,128)(2,1)} custom-call(s32[8,128]{1,0:T(8,128)} %bitcast.20, f32[8,128]{1,0:T(8,128)} %bitcast.23, bf16[128,1024]{1,0:T(8,128)(2,1)} %latent_hbm.1, bf16[128,1024]{1,0:T(8,128)(2,1)} %cot_ref.1), custom_call_target="tpu_custom_call" | custom-call | tf_op jit(solution)/shard_map/pack_kernel/pallas_call | solution.py:247
  10.0 31.8 %all-to-all-start.1 = ((bf16[64,8,512]{2,1,0:T(8,128)(2,1)}), bf16[64,8,512]{2,1,0:T(8,128)(2,1)S(1)}, u32[]{:S(2)}, u32[]{:S(2)}) async-start(bf16[64,8,512]{2,1,0:T(8,128)(2,1)} %bitcast.30), calls=%async_computation.1 | async-start | bytes 1048576 | tf_op jit(solution)/shard_map/all_to_all | solution.py:255
  41.7 0.0 reduce-scatter.2.cloned.1.call-start
  41.8 63.9 %all-to-all-done.1 = bf16[64,8,512]{2,1,0:T(8,128)(2,1)S(1)} async-done(((bf16[64,8,512]{2,1,0:T(8,128)(2,1)}), bf16[64,8,512]{2,1,0:T(8,128)(2,1)S(1)}, u32[]{:S(2)}, u32[]{:S(2)}) %all-to-all-start.1) | async-done | bytes 524320 | tf_op jit(solution)/shard_map/all_to_all | solution.py:255
  105.7 0.8 copy-done.3
  106.5 5.6 %expert_kernel.1 = (bf16[8,64,1536]{2,1,0:T(8,128)(2,1)}, bf16[8,64,1536]{2,1,0:T(8,128)(2,1)}, bf16[128,512]{1,0:T(8,128)(2,1)}, bf16[128,1024]{1,0:T(8,128)(2,1)}) custom-call(s32[1]{0:T(128)} %bitcast.5.core_ref, bf16[512,512]{1,0:T(8,128)(2,1)} %bitcast.32, bf16[1024,1024]{1,0:T(8,128)(2,1)} %bitcast.25, bf16[1024,512]{1,0:T(8,128)(2,1)} %bitcast.28), custom_call_target="tpu_custom_call" | custom-call | tf_op jit(solution)/shard_map/expert_kernel/pallas_call | solution.py:262
  112.1 1.9 collective-permute-start.4
  114.0 3.7 %return_kernel.1 = (bf16[128,512]{1,0:T(8,128)(2,1)S(1)}, bf16[192,512]{1,0:T(8,128)(2,1)S(1)}, bf16[192,512]{1,0:T(8,128)(2,1)S(1)}) custom-call(s32[1]{0:T(128)} %bitcast.12.plane_ref, bf16[128,512]{1,0:T(8,128)(2,1)} %get-tuple-element.50.act_ref, bf16[128,1024]{1,0:T(8,128)(2,1)} %get-tuple-element.51.grad_ref, bf16[1024,1024]{1,0:T(8,128)(2,1)} %bitcast.26, ...), custom_call_target="tpu_custom_call" | custom-call | tf_op jit(solution)/shard_map/return_kernel/pallas_call | solution.py:271
  117.7 3.4 %add_kernel.1 = bf16[8,64,1536]{2,1,0:T(8,128)(2,1)} custom-call(bf16[8,64,1536]{2,1,0:T(8,128)(2,1)} %get-tuple-element.48.a_ref, bf16[8,64,1536]{2,1,0:T(8,128)(2,1)} %collective-permute-done.4.b_ref), custom_call_target="tpu_custom_call" | custom-call | tf_op jit(solution)/shard_map/add_kernel/pallas_call | solution.py:274
  121.1 0.0 reduce-scatter.2.cloned.1.call-update
  121.1 0.7 copy-done.1
  121.8 0.0 copy-done.2
  121.8 0.5 mask_kernel.1
  122.4 98.1 %conditional.1 = (bf16[512,512]{1,0:T(8,128)(2,1)S(1)}) conditional(s32[]{:T(128)} %convert_element_type.3, (bf16[128,512]{1,0:T(8,128)(2,1)S(1)}, bf16[192,512]{1,0:T(8,128)(2,1)S(1)}, bf16[192,512]{1,0:T(8,128)(2,1)S(1)}) %return_kernel.1, (bf16[128,512]{1,0:T(8,128)(2,1)S(1)}, bf16[192,512]{1,0:T(8,128)(2,1)S(1)}, ...), branch_computations={%region_1.2_spmd, %region_2.3_spmd} | conditional | flops 2359296 | bytes 5243048 | solution.py:280
  122.4 2.1 collective-permute-start.1
  124.4 12.6 %collective-permute-start = (bf16[192,512]{1,0:T(8,128)(2,1)S(1)}, bf16[192,512]{1,0:T(8,128)(2,1)S(1)}, u32[]{:S(2)}, u32[]{:S(2)}) collective-permute-start(bf16[192,512]{1,0:T(8,128)(2,1)S(1)} %get-tuple-element.19), channel_id=1, source_target_pairs={{0,16},{1,17},{2,18},{3,19},{4,20},{5,21},{6,22},{7,23},{8,24},{9,... | collective-permute-start | bytes 589832 | tf_op jit(solution)/shard_map/cond/branch_1_fun/ppermute | solution.py:314
  137.1 38.8 %collective-permute-done.1 = bf16[192,512]{1,0:T(8,128)(2,1)S(1)} collective-permute-done((bf16[192,512]{1,0:T(8,128)(2,1)S(1)}, bf16[192,512]{1,0:T(8,128)(2,1)S(1)}, u32[]{:S(2)}, u32[]{:S(2)}) %collective-permute-start.1) | collective-permute-done | bytes 196640 | tf_op jit(solution)/shard_map/cond/branch_1_fun/ppermute | solution.py:315
  175.9 8.0 %collective-permute-start.3 = (bf16[64,512]{1,0:T(8,128)(2,1)S(1)}, bf16[64,512]{1,0:T(8,128)(2,1)S(1)}, u32[]{:S(2)}, u32[]{:S(2)}) collective-permute-start(bf16[64,512]{1,0:T(8,128)(2,1)S(1)} %slice.15), channel_id=1, source_target_pairs={{0,48},{1,49},{2,50},{3,51},{4,52},{5,53},{6,54},{7,55},{8,56},{9,... | collective-permute-start | bytes 196616 | tf_op jit(solution)/shard_map/cond/branch_1_fun/ppermute | solution.py:317
  184.0 6.5 %collective-permute-start.2 = (bf16[64,512]{1,0:T(8,128)(2,1)S(1)}, bf16[64,512]{1,0:T(8,128)(2,1)S(1)}, u32[]{:S(2)}, u32[]{:S(2)}) collective-permute-start(bf16[64,512]{1,0:T(8,128)(2,1)S(1)} %slice.14), channel_id=1, source_target_pairs={{0,16},{1,17},{2,18},{3,19},{4,20},{5,21},{6,22},{7,23},{8,24},{9,... | collective-permute-start | bytes 196616 | tf_op jit(solution)/shard_map/cond/branch_1_fun/ppermute | solution.py:316
  190.5 3.5 %collective-permute-done.3 = bf16[64,512]{1,0:T(8,128)(2,1)S(1)} collective-permute-done((bf16[64,512]{1,0:T(8,128)(2,1)S(1)}, bf16[64,512]{1,0:T(8,128)(2,1)S(1)}, u32[]{:S(2)}, u32[]{:S(2)}) %collective-permute-start.3) | collective-permute-done | bytes 65568 | tf_op jit(solution)/shard_map/cond/branch_1_fun/ppermute | solution.py:317
  194.0 8.6 %collective-permute-done.2 = bf16[64,512]{1,0:T(8,128)(2,1)S(1)} collective-permute-done((bf16[64,512]{1,0:T(8,128)(2,1)S(1)}, bf16[64,512]{1,0:T(8,128)(2,1)S(1)}, u32[]{:S(2)}, u32[]{:S(2)}) %collective-permute-start.2) | collective-permute-done | bytes 65568 | tf_op jit(solution)/shard_map/cond/branch_1_fun/ppermute | solution.py:316
  202.7 17.7 %all_to_all.9 = bf16[16,32,512]{2,1,0:T(8,128)(2,1)S(1)} all-to-all(bf16[16,32,512]{2,1,0:T(8,128)(2,1)S(1)} %pad_maximum_fusion.1), channel_id=1, replica_groups={{0,1,2,3,4,5,6,7,8,9,10,11,12,13,14,15},{16,17,18,19,20,21,22,23,24,25,..., dimensions={0} | all-to-all | bytes 1048576 | tf_op jit(solution)/shard_map/cond/branch_1_fun/all_to_all | solution.py:320
  220.5 1.9 combine_kernel.1
  222.4 1.6 split_kernel.1
  (14 shorter events, 0.1 us)
Async XLA Ops:
  10.0 95.7 %all-to-all-start.1 = ((bf16[64,8,512]{2,1,0:T(8,128)(2,1)}), bf16[64,8,512]{2,1,0:T(8,128)(2,1)S(1)}, u32[]{:S(2)}, u32[]{:S(2)}) async-start(bf16[64,8,512]{2,1,0:T(8,128)(2,1)} %bitcast.30), calls=%async_computation.1 | async-start | bytes 1048576 | tf_op jit(solution)/shard_map/all_to_all | solution.py:255
  41.7 180.7 %reduce-scatter.2.cloned.1.call-start = ((), (), s32[]{:S(2)}) async-start(), calls=%async_computation.3 | async-start | bytes 1769472 | tf_op jit(solution)/shard_map/reduce_scatter | solution.py:276
  105.7 0.8 copy-start.3
  112.1 5.6 %collective-permute-start.4 = (bf16[8,64,1536]{2,1,0:T(8,128)(2,1)}, bf16[8,64,1536]{2,1,0:T(8,128)(2,1)}, u32[]{:S(2)}, u32[]{:S(2)}) collective-permute-start(bf16[8,64,1536]{2,1,0:T(8,128)(2,1)} %get-tuple-element.49), channel_id=1, source_target_pairs={{0,64},{64,0},{128,192},{192,128},{256,320},{320,256},{384,448},{4... | collective-permute-start | bytes 4718600 | tf_op jit(solution)/shard_map/ppermute | solution.py:270
  121.1 0.7 copy-start.1
  121.1 0.7 copy-start.2
  122.4 98.1 %copy-start = (bf16[128,1024]{1,0:T(8,128)(2,1)S(1)}, bf16[128,1024]{1,0:T(8,128)(2,1)}, u32[]{:S(2)}) copy-start(bf16[128,1024]{1,0:T(8,128)(2,1)} %cot_ref.1) | copy-start | bytes 786436
  122.4 53.5 %collective-permute-start.1 = (bf16[192,512]{1,0:T(8,128)(2,1)S(1)}, bf16[192,512]{1,0:T(8,128)(2,1)S(1)}, u32[]{:S(2)}, u32[]{:S(2)}) collective-permute-start(bf16[192,512]{1,0:T(8,128)(2,1)S(1)} %get-tuple-element.20), channel_id=1, source_target_pairs={{0,48},{1,49},{2,50},{3,51},{4,52},{5,53},{6,54},{7,55},{8,56},{9,... | collective-permute-start | bytes 589832 | tf_op jit(solution)/shard_map/cond/branch_1_fun/ppermute | solution.py:315
  124.4 59.5 %collective-permute-start = (bf16[192,512]{1,0:T(8,128)(2,1)S(1)}, bf16[192,512]{1,0:T(8,128)(2,1)S(1)}, u32[]{:S(2)}, u32[]{:S(2)}) collective-permute-start(bf16[192,512]{1,0:T(8,128)(2,1)S(1)} %get-tuple-element.19), channel_id=1, source_target_pairs={{0,16},{1,17},{2,18},{3,19},{4,20},{5,21},{6,22},{7,23},{8,24},{9,... | collective-permute-start | bytes 589832 | tf_op jit(solution)/shard_map/cond/branch_1_fun/ppermute | solution.py:314
  175.9 18.1 %collective-permute-start.3 = (bf16[64,512]{1,0:T(8,128)(2,1)S(1)}, bf16[64,512]{1,0:T(8,128)(2,1)S(1)}, u32[]{:S(2)}, u32[]{:S(2)}) collective-permute-start(bf16[64,512]{1,0:T(8,128)(2,1)S(1)} %slice.15), channel_id=1, source_target_pairs={{0,48},{1,49},{2,50},{3,51},{4,52},{5,53},{6,54},{7,55},{8,56},{9,... | collective-permute-start | bytes 196616 | tf_op jit(solution)/shard_map/cond/branch_1_fun/ppermute | solution.py:317
  184.0 18.7 %collective-permute-start.2 = (bf16[64,512]{1,0:T(8,128)(2,1)S(1)}, bf16[64,512]{1,0:T(8,128)(2,1)S(1)}, u32[]{:S(2)}, u32[]{:S(2)}) collective-permute-start(bf16[64,512]{1,0:T(8,128)(2,1)S(1)} %slice.14), channel_id=1, source_target_pairs={{0,16},{1,17},{2,18},{3,19},{4,20},{5,21},{6,22},{7,23},{8,24},{9,... | collective-permute-start | bytes 196616 | tf_op jit(solution)/shard_map/cond/branch_1_fun/ppermute | solution.py:316
Sparse Core Ops, SparseCore 0:
  121.3 85.9 reduce-scatter.1
